TPU v7x, 32 devices: a whole 2x2x4 slice. The times are simulated.
32 devices in a mesh: head: 4 (over z), blk: 8 (over y, x, core).
Axes of the slice: x: 2, y: 2, z: 4, core: 2. Of those that a mesh axis runs over, the one named last changes fastest.
Arguments:
- inputs: bfloat16 [4096, 1024], P(('head', 'blk')), may hold values from -6 to 6
- attn_gain: bfloat16 [1024], P(('head', 'blk')), may hold values from 0.5 to 1.5
- attn_qkv: bfloat16 [1024, 3072], P(('head', 'blk')), may hold values from -0.1875 to 0.1875
- attn_out: bfloat16 [1024, 1024], P(('head', 'blk')), may hold values from -2 to 2
- memory_gain: bfloat16 [1024], P(('head', 'blk')), may hold values from 0.5 to 1.5
- memory_query: bfloat16 [1024, 4096], P(('head', 'blk')), may hold values from -0.1875 to 0.1875
- sub_keys: bfloat16 [2048, 512], P(('head', 'blk')), may hold values from -0.25 to 0.25
- memory_gate: bfloat16 [1024, 1024], P(('head', 'blk')), may hold values from -0.1875 to 0.1875
- memory_out: bfloat16 [1024, 1024], P(('head', 'blk')), may hold values from -0.375 to 0.375
- memory_values: bfloat16 [65536, 1024], P(('head', 'blk')), may hold values from -6 to 6
- doc_lengths: int32 [3], replicated, may hold values from 512 to 2048, as said below
- token_order: int32 [4096], replicated, may hold values from 0 to 4095, as said below
- memory_picks: int32 [4096, 4, 32, 2], P(('head', 'blk')), may hold values from 0 to 255, as said below
- cotangent: bfloat16 [4096, 1024], P(('head', 'blk')), may hold values from -6 to 6
Outputs:
- output: bfloat16 [4096, 1024], P(('head', 'blk'))
- grad_inputs: float32 [4096, 1024], P(('head', 'blk'))
- grad_attn_gain: float32 [1024], P(('head', 'blk'))
- grad_attn_qkv: float32 [1024, 3072], P(('head', 'blk'))
- grad_attn_out: float32 [1024, 1024], P(('head', 'blk'))
- grad_memory_gain: float32 [1024], P(('head', 'blk'))
- grad_memory_query: float32 [1024, 4096], P(('head', 'blk'))
- grad_sub_keys: float32 [2048, 512], P(('head', 'blk'))
- grad_memory_gate: float32 [1024, 1024], P(('head', 'blk'))
- grad_memory_out: float32 [1024, 1024], P(('head', 'blk'))
- grad_memory_values: float32 [65536, 1024], P(('head', 'blk'))
Inputs may be any that keep to these rules, and one draw needn't show every extreme that they name: `doc_lengths`: the entries sum to 4096; each is 512 or more, and one is exactly 2048. `token_order`: A permutation of the tokens. Dealt slots lie in blocks of 128, one block a device in the order of head, then blk, and tokens lie likewise in blocks of 128 in order. The block of device (g, b) holds, for each device (g, b2) of the same head index in blk order, exactly 128 / 8 of the tokens of b2's block. `memory_picks`: each entry is a pair (first, second) naming value row first * 256 + second. The value rows lie in order in 32 equal slices of 2048, one a device in the order of head, then blk. Of the picks of the dealt slots of one device (aligned blocks of 128 slots) at most 1024 name rows of any one slice, and in every draw some slice receives exactly 1024 from every device.
All inputs are finite; a program needn't handle non-finite values.
Results may differ from a plain program's by a relative error of at most 0.035.
Values may be sent and summed in bfloat16 or wider, within the bound.
No kernel may reach another device: no remote copies, remote signals or barrier semaphores. Data moves between devices by JAX's collectives and lax.ppermute only.
A program may use at most 320 MiB of HBM per device.

v0:
```python
import math

import jax
import jax.numpy as jnp
from jax import lax
from jax.sharding import PartitionSpec as P

NH = 16
HD = 64
MH = 4
QHALF = 512
NSUB = 256
KPICK = 32


epsilon = 1e-06
neg_big = -1e30


def norm_scale(hidden):
    return lax.rsqrt(jnp.mean(hidden * hidden, axis=-1, keepdims=True) + epsilon)


def norm_back(hidden, row_scale, gain_wide, grad_normed):
    weighted = grad_normed * gain_wide
    coupled = jnp.mean(hidden * weighted, axis=-1, keepdims=True)
    grad_hidden = row_scale * weighted - hidden * (row_scale * row_scale * row_scale) * coupled
    grad_gain = jnp.sum(grad_normed * hidden * row_scale, axis=0)
    return (grad_hidden, grad_gain)


def document_ids(positions, doc_ends):
    return jnp.sum((positions[:, None] >= doc_ends[None, :]).astype(jnp.int32), axis=1)


def over_blocks(initial, pieces, rows_here, advance):
    length = pieces[0].shape[1]
    stride = min(length, rows_here)
    turns = length // stride
    stacked = tuple(
        (
            jnp.moveaxis(member.reshape((member.shape[0], turns, stride) + member.shape[2:]), 1, 0)
            for member in pieces
        )
    )
    firsts = stride * jnp.arange(turns, dtype=jnp.int32)

    def visit(carried, member):
        return (advance(carried, member[0], member[1]), None)

    final, unused = lax.scan(visit, initial, (stacked, firsts))
    return final


def fetch_rows(requests, memory_values):
    asked = lax.all_to_all(requests, ("head", "blk"), split_axis=0, concat_axis=0, tiled=True)
    return (
        lax.all_to_all(
            memory_values[asked], ("head", "blk"), split_axis=0, concat_axis=0, tiled=True
        ),
        asked,
    )


def body(
    inputs,
    attn_gain,
    attn_qkv,
    attn_out,
    memory_gain,
    memory_query,
    sub_keys,
    memory_gate,
    memory_out,
    memory_values,
    doc_lengths,
    token_order,
    memory_picks,
    cotangent,
):
    rows_here = inputs.shape[0]
    model_width = inputs.shape[1]
    groups = lax.axis_size("head")
    cycle_size = lax.axis_size("blk")
    devices = lax.axis_size(("head", "blk"))
    share_rows = rows_here // cycle_size
    group_index = lax.axis_index("head")
    cycle_index = lax.axis_index("blk")
    source_index = group_index * cycle_size + cycle_index
    slot_base = group_index * cycle_size * rows_here + cycle_index * share_rows
    send_slots = (
        slot_base
        + (jnp.arange(cycle_size, dtype=jnp.int32) * rows_here)[:, None]
        + jnp.arange(share_rows, dtype=jnp.int32)[None, :]
    )
    own_take = (token_order[send_slots] - source_index * rows_here).reshape(-1)
    dealt_in, dealt_cot = (
        lax.all_to_all(
            inputs[own_take].reshape(cycle_size, share_rows, model_width),
            "blk",
            split_axis=0,
            concat_axis=0,
            tiled=True,
        ),
        lax.all_to_all(
            cotangent[own_take].reshape(cycle_size, share_rows, model_width),
            "blk",
            split_axis=0,
            concat_axis=0,
            tiled=True,
        ),
    )
    dealt_in = dealt_in.reshape(rows_here, model_width)
    dealt_cot = dealt_cot.reshape(rows_here, model_width)
    gathered = (
        lax.all_gather(attn_gain, ("head", "blk"), axis=0, tiled=True),
        lax.all_gather(attn_qkv, ("head", "blk"), axis=0, tiled=True),
        lax.all_gather(attn_out, ("head", "blk"), axis=0, tiled=True),
        lax.all_gather(memory_gain, ("head", "blk"), axis=0, tiled=True),
        lax.all_gather(memory_query, ("head", "blk"), axis=0, tiled=True),
        lax.all_gather(sub_keys, ("head", "blk"), axis=0, tiled=True),
        lax.all_gather(memory_gate, ("head", "blk"), axis=0, tiled=True),
        lax.all_gather(memory_out, ("head", "blk"), axis=0, tiled=True),
    )
    gain_one = gathered[0].astype(jnp.float32)
    weight_qkv = gathered[1]
    weight_attn = gathered[2]
    gain_two = gathered[3].astype(jnp.float32)
    weight_query = gathered[4]
    key_table = gathered[5].reshape(MH, 2, NSUB, QHALF)
    weight_gate = gathered[6]
    weight_mixed = gathered[7]
    heads_here = NH // groups
    local_rows = groups * rows_here
    quarter_span = cycle_size * rows_here
    score_scale = 1.0 / math.sqrt(HD)
    doc_ends = jnp.cumsum(doc_lengths)
    quarter = jnp.arange(groups, dtype=jnp.int32)
    query_slots = (
        quarter[:, None] * quarter_span
        + cycle_index * rows_here
        + jnp.arange(rows_here, dtype=jnp.int32)[None, :]
    ).reshape(-1)
    query_pos = token_order[query_slots]
    query_doc = document_ids(query_pos, doc_ends)

    def block_places(first_row, stride):
        slots = (
            quarter[:, None] * quarter_span
            + first_row
            + jnp.arange(stride, dtype=jnp.int32)[None, :]
        ).reshape(-1)
        places = token_order[slots]
        return (places, document_ids(places, doc_ends))

    inputs_wide = dealt_in.astype(jnp.float32)
    scale_one = norm_scale(inputs_wide)
    normed_one = (inputs_wide * scale_one * gain_one).astype(jnp.bfloat16)
    projected = (
        jnp.dot(normed_one, weight_qkv, preferred_element_type=jnp.float32)
        .astype(jnp.bfloat16)
        .reshape(rows_here, 3, NH * HD)
    )
    regrouped = lax.all_to_all(projected, "head", split_axis=2, concat_axis=0, tiled=True)
    query_heads = regrouped[:, 0].reshape(local_rows, heads_here, HD)
    key_heads = regrouped[:, 1].reshape(local_rows, heads_here, HD)
    value_heads = regrouped[:, 2].reshape(local_rows, heads_here, HD)
    query_travel = regrouped[:, 0].reshape(groups, rows_here, heads_here * HD)
    key_travel = regrouped[:, 1].reshape(groups, rows_here, heads_here * HD)
    value_travel = regrouped[:, 2].reshape(groups, rows_here, heads_here * HD)

    def forward_step(carried, members, first_row):
        run_max, run_sum, run_acc = carried
        stride = members[0].shape[1]
        key_pos, key_doc = block_places(first_row, stride)
        allowed = (key_pos[None, :] <= query_pos[:, None]) & (
            key_doc[None, :] == query_doc[:, None]
        )
        key_flat = members[0].reshape(groups * stride, heads_here, HD)
        value_flat = members[1].reshape(groups * stride, heads_here, HD)
        scores = (
            jnp.einsum("qhd,khd->hqk", query_heads, key_flat, preferred_element_type=jnp.float32)
            * score_scale
        )
        masked = jnp.where(allowed[None], scores, neg_big)
        new_max = jnp.maximum(run_max, jnp.max(masked, axis=2))
        powers = jnp.where(allowed[None], jnp.exp(masked - new_max[:, :, None]), 0.0)
        rescale = jnp.exp(run_max - new_max)
        run_sum = run_sum * rescale + jnp.sum(powers, axis=2)
        run_acc = run_acc * rescale[:, :, None] + jnp.einsum(
            "hqk,khd->hqd",
            powers.astype(jnp.bfloat16),
            value_flat,
            preferred_element_type=jnp.float32,
        )
        return (new_max, run_sum, run_acc)

    start_state = (
        jnp.full((heads_here, local_rows), neg_big, jnp.float32),
        jnp.zeros((heads_here, local_rows), jnp.float32),
        jnp.zeros((heads_here, local_rows, HD), jnp.float32),
    )
    run_max, run_sum, run_acc = over_blocks(
        start_state,
        (
            lax.all_gather(key_travel, "blk", axis=1, tiled=True),
            lax.all_gather(value_travel, "blk", axis=1, tiled=True),
        ),
        rows_here,
        forward_step,
    )
    attended = run_acc / run_sum[:, :, None]
    log_total = run_max + jnp.log(run_sum)
    attended_low = (
        jnp.transpose(attended, (1, 0, 2)).reshape(local_rows, heads_here * HD).astype(jnp.bfloat16)
    )
    attended_rows = lax.all_to_all(attended_low, "head", split_axis=0, concat_axis=1, tiled=True)
    hidden_one = inputs_wide + jnp.dot(
        attended_rows, weight_attn, preferred_element_type=jnp.float32
    )
    scale_two = norm_scale(hidden_one)
    normed_two = (hidden_one * scale_two * gain_two).astype(jnp.bfloat16)
    query_mem = (
        jnp.dot(normed_two, weight_query, preferred_element_type=jnp.float32)
        .astype(jnp.bfloat16)
        .reshape(rows_here, MH, 2, QHALF)
    )
    sub_scores = jnp.einsum(
        "thcd,hcnd->thcn", query_mem, key_table, preferred_element_type=jnp.float32
    )
    sub_range = jnp.arange(NSUB, dtype=jnp.int32)
    first_hit = (memory_picks[:, :, :, 0, None] == sub_range).astype(jnp.float32)
    second_hit = (memory_picks[:, :, :, 1, None] == sub_range).astype(jnp.float32)
    picked = jnp.sum(first_hit * sub_scores[:, :, 0, None, :], axis=3) + jnp.sum(
        second_hit * sub_scores[:, :, 1, None, :], axis=3
    )
    picked_exp = jnp.exp(picked - jnp.max(picked, axis=2, keepdims=True))
    pick_weights = picked_exp / jnp.sum(picked_exp, axis=2, keepdims=True)
    weights_low = pick_weights.astype(jnp.bfloat16).reshape(rows_here, MH * KPICK)
    own_rows = memory_values.shape[0]
    capacity = 2 * rows_here * MH * KPICK // devices
    total_picks = rows_here * MH * KPICK
    value_index = (memory_picks[:, :, :, 0] * NSUB + memory_picks[:, :, :, 1]).reshape(-1)
    owner = value_index // own_rows
    local_index = value_index % own_rows
    counts = jnp.sum(
        (owner[:, None] == jnp.arange(devices, dtype=jnp.int32)[None, :]).astype(jnp.int32), axis=0
    )
    starts = jnp.cumsum(counts) - counts
    ordering = jnp.argsort(owner, stable=True)
    ranked = jnp.arange(total_picks, dtype=jnp.int32) - starts[owner[ordering]]
    slot_rank = jnp.zeros((total_picks,), jnp.int32).at[ordering].set(ranked)
    target = owner * capacity + slot_rank
    requests = (
        jnp.zeros((devices * capacity,), jnp.int32)
        .at[target]
        .set(local_index)
        .reshape(devices, capacity)
    )
    fetched, asked_rows = fetch_rows(requests, memory_values)
    picked_rows = fetched.reshape(devices * capacity, model_width)[target].reshape(
        rows_here, MH * KPICK, model_width
    )
    memory = jnp.einsum("tk,tkd->td", weights_low, picked_rows, preferred_element_type=jnp.float32)
    gate_pre = jnp.dot(normed_two, weight_gate, preferred_element_type=jnp.float32)
    gate_sig = jax.nn.sigmoid(gate_pre)
    mixed_low = (memory * gate_pre * gate_sig).astype(jnp.bfloat16)
    output = (
        hidden_one + jnp.dot(mixed_low, weight_mixed, preferred_element_type=jnp.float32)
    ).astype(jnp.bfloat16)
    grad_weight_mixed = jnp.dot(mixed_low.T, dealt_cot, preferred_element_type=jnp.float32)
    grad_mixed = jnp.dot(dealt_cot, weight_mixed.T, preferred_element_type=jnp.float32)
    grad_memory = (grad_mixed * gate_pre * gate_sig).astype(jnp.bfloat16)
    grad_gate = (grad_mixed * memory * gate_sig * (1.0 + gate_pre * (1.0 - gate_sig))).astype(
        jnp.bfloat16
    )
    refetched, unused_rows = fetch_rows(requests, memory_values)
    kept_rows = refetched.reshape(devices * capacity, model_width)[target].reshape(
        rows_here, MH * KPICK, model_width
    )
    grad_pick = jnp.einsum(
        "td,tkd->tk", grad_memory, kept_rows, preferred_element_type=jnp.float32
    ).reshape(rows_here, MH, KPICK)
    grad_picked = pick_weights * (
        grad_pick - jnp.sum(pick_weights * grad_pick, axis=2, keepdims=True)
    )
    grad_first = jnp.sum(grad_picked[:, :, :, None] * first_hit, axis=2)
    grad_second = jnp.sum(grad_picked[:, :, :, None] * second_hit, axis=2)
    grad_sub = jnp.stack([grad_first, grad_second], axis=2).astype(jnp.bfloat16)
    grad_query = (
        jnp.einsum("thcn,hcnd->thcd", grad_sub, key_table, preferred_element_type=jnp.float32)
        .astype(jnp.bfloat16)
        .reshape(rows_here, MH * 2 * QHALF)
    )
    grad_table = jnp.einsum(
        "thcn,thcd->hcnd", grad_sub, query_mem, preferred_element_type=jnp.float32
    ).reshape(MH * 2 * NSUB, QHALF)
    grad_weight_query = jnp.dot(normed_two.T, grad_query, preferred_element_type=jnp.float32)
    grad_weight_gate = jnp.dot(normed_two.T, grad_gate, preferred_element_type=jnp.float32)
    grad_normed_two = jnp.dot(
        grad_gate, weight_gate.T, preferred_element_type=jnp.float32
    ) + jnp.dot(grad_query, weight_query.T, preferred_element_type=jnp.float32)
    grad_hidden_two, grad_gain_two = norm_back(hidden_one, scale_two, gain_two, grad_normed_two)
    grad_hidden = dealt_cot.astype(jnp.float32) + grad_hidden_two
    row_grads = (
        weights_low[:, :, None].astype(jnp.float32) * grad_memory[:, None, :].astype(jnp.float32)
    ).astype(jnp.bfloat16)
    outgoing = (
        jnp.zeros((devices * capacity, model_width), jnp.bfloat16)
        .at[target]
        .set(row_grads.reshape(-1, model_width))
        .reshape(devices, capacity, model_width)
    )
    arrived = lax.all_to_all(outgoing, ("head", "blk"), split_axis=0, concat_axis=0, tiled=True)
    sources = math.gcd(devices, 16)

    def accumulate(step_index, running):
        block_rows = (
            lax.dynamic_slice_in_dim(arrived, step_index * sources, sources, 0)
            .astype(jnp.float32)
            .reshape(-1, model_width)
        )
        row_ids = lax.dynamic_slice_in_dim(asked_rows, step_index * sources, sources, 0).reshape(-1)
        return running + jax.ops.segment_sum(block_rows, row_ids, num_segments=own_rows)

    grad_values = lax.fori_loop(
        0, devices // sources, accumulate, jnp.zeros((own_rows, model_width), jnp.float32)
    )
    grad_branch = grad_hidden.astype(jnp.bfloat16)
    grad_weight_attn = jnp.dot(attended_rows.T, grad_branch, preferred_element_type=jnp.float32)
    grad_attended = jnp.dot(grad_branch, weight_attn.T, preferred_element_type=jnp.float32).astype(
        jnp.bfloat16
    )
    grad_local = lax.all_to_all(grad_attended, "head", split_axis=1, concat_axis=0, tiled=True)
    grad_heads = grad_local.reshape(local_rows, heads_here, HD)
    row_delta = jnp.sum(jnp.transpose(grad_heads, (1, 0, 2)).astype(jnp.float32) * attended, axis=2)

    def query_step(running, members, first_row):
        stride = members[0].shape[1]
        key_pos, key_doc = block_places(first_row, stride)
        allowed = (key_pos[None, :] <= query_pos[:, None]) & (
            key_doc[None, :] == query_doc[:, None]
        )
        key_flat = members[0].reshape(groups * stride, heads_here, HD)
        value_flat = members[1].reshape(groups * stride, heads_here, HD)
        scores = (
            jnp.einsum("qhd,khd->hqk", query_heads, key_flat, preferred_element_type=jnp.float32)
            * score_scale
        )
        attn_probs = jnp.where(allowed[None], jnp.exp(scores - log_total[:, :, None]), 0.0)
        grad_probs = jnp.einsum(
            "qhd,khd->hqk", grad_heads, value_flat, preferred_element_type=jnp.float32
        )
        grad_scores = (attn_probs * (grad_probs - row_delta[:, :, None])).astype(jnp.bfloat16)
        return (
            running
            + jnp.einsum("hqk,khd->hqd", grad_scores, key_flat, preferred_element_type=jnp.float32)
            * score_scale
        )

    grad_query_acc = over_blocks(
        jnp.zeros((heads_here, local_rows, HD), jnp.float32),
        (
            lax.all_gather(key_travel, "blk", axis=1, tiled=True),
            lax.all_gather(value_travel, "blk", axis=1, tiled=True),
        ),
        rows_here,
        query_step,
    )
    grad_travel = grad_local.reshape(groups, rows_here, heads_here * HD)
    total_travel = jnp.transpose(log_total).reshape(groups, rows_here, heads_here)
    delta_travel = jnp.transpose(row_delta).reshape(groups, rows_here, heads_here)

    def key_step(running, members, first_row):
        grad_key, grad_value = running
        stride = members[0].shape[1]
        remote_pos, remote_doc = block_places(first_row, stride)
        allowed = (query_pos[None, :] <= remote_pos[:, None]) & (
            query_doc[None, :] == remote_doc[:, None]
        )
        remote_query = members[0].reshape(groups * stride, heads_here, HD)
        remote_grad = members[1].reshape(groups * stride, heads_here, HD)
        remote_total = jnp.transpose(members[2].reshape(groups * stride, heads_here))
        remote_delta = jnp.transpose(members[3].reshape(groups * stride, heads_here))
        scores = (
            jnp.einsum("qhd,khd->hqk", remote_query, key_heads, preferred_element_type=jnp.float32)
            * score_scale
        )
        attn_probs = jnp.where(allowed[None], jnp.exp(scores - remote_total[:, :, None]), 0.0)
        grad_probs = jnp.einsum(
            "qhd,khd->hqk", remote_grad, value_heads, preferred_element_type=jnp.float32
        )
        grad_scores = (attn_probs * (grad_probs - remote_delta[:, :, None])).astype(jnp.bfloat16)
        grad_key = (
            grad_key
            + jnp.einsum(
                "hqk,qhd->hkd", grad_scores, remote_query, preferred_element_type=jnp.float32
            )
            * score_scale
        )
        grad_value = grad_value + jnp.einsum(
            "hqk,qhd->hkd",
            attn_probs.astype(jnp.bfloat16),
            remote_grad,
            preferred_element_type=jnp.float32,
        )
        return (grad_key, grad_value)

    empty_grads = (
        jnp.zeros((heads_here, local_rows, HD), jnp.float32),
        jnp.zeros((heads_here, local_rows, HD), jnp.float32),
    )
    grad_key_acc, grad_value_acc = over_blocks(
        empty_grads,
        (
            lax.all_gather(query_travel, "blk", axis=1, tiled=True),
            lax.all_gather(grad_travel, "blk", axis=1, tiled=True),
            lax.all_gather(total_travel.astype(jnp.bfloat16), "blk", axis=1, tiled=True).astype(
                jnp.float32
            ),
            lax.all_gather(delta_travel.astype(jnp.bfloat16), "blk", axis=1, tiled=True).astype(
                jnp.float32
            ),
        ),
        rows_here,
        key_step,
    )
    grad_stack = jnp.stack(
        [
            jnp.transpose(grad_query_acc, (1, 0, 2)).reshape(local_rows, heads_here * HD),
            jnp.transpose(grad_key_acc, (1, 0, 2)).reshape(local_rows, heads_here * HD),
            jnp.transpose(grad_value_acc, (1, 0, 2)).reshape(local_rows, heads_here * HD),
        ],
        axis=1,
    ).astype(jnp.bfloat16)
    grad_projected = lax.all_to_all(
        grad_stack, "head", split_axis=0, concat_axis=2, tiled=True
    ).reshape(rows_here, 3 * NH * HD)
    grad_weight_qkv = jnp.dot(normed_one.T, grad_projected, preferred_element_type=jnp.float32)
    grad_normed_one = jnp.dot(grad_projected, weight_qkv.T, preferred_element_type=jnp.float32)
    grad_input_part, grad_gain_one = norm_back(inputs_wide, scale_one, gain_one, grad_normed_one)
    grad_dealt = grad_hidden + grad_input_part
    summed = (
        lax.psum_scatter(grad_gain_one, ("head", "blk"), scatter_dimension=0, tiled=True),
        lax.psum_scatter(grad_weight_qkv, ("head", "blk"), scatter_dimension=0, tiled=True),
        lax.psum_scatter(grad_weight_attn, ("head", "blk"), scatter_dimension=0, tiled=True),
        lax.psum_scatter(grad_gain_two, ("head", "blk"), scatter_dimension=0, tiled=True),
        lax.psum_scatter(grad_weight_query, ("head", "blk"), scatter_dimension=0, tiled=True),
        lax.psum_scatter(grad_table, ("head", "blk"), scatter_dimension=0, tiled=True),
        lax.psum_scatter(grad_weight_gate, ("head", "blk"), scatter_dimension=0, tiled=True),
        lax.psum_scatter(grad_weight_mixed, ("head", "blk"), scatter_dimension=0, tiled=True),
    )
    back_out, back_grad = (
        lax.all_to_all(
            output.astype(jnp.float32)
            .reshape(cycle_size, share_rows, model_width)
            .astype(jnp.bfloat16),
            "blk",
            split_axis=0,
            concat_axis=0,
            tiled=True,
        ).astype(jnp.float32),
        lax.all_to_all(
            grad_dealt.reshape(cycle_size, share_rows, model_width).astype(jnp.bfloat16),
            "blk",
            split_axis=0,
            concat_axis=0,
            tiled=True,
        ).astype(jnp.float32),
    )
    output_home = (
        jnp.zeros((rows_here, model_width), jnp.float32)
        .at[own_take]
        .set(back_out.reshape(rows_here, model_width))
        .astype(jnp.bfloat16)
    )
    grad_home = (
        jnp.zeros((rows_here, model_width), jnp.float32)
        .at[own_take]
        .set(back_grad.reshape(rows_here, model_width))
    )
    return (
        output_home,
        grad_home,
        summed[0],
        summed[1],
        summed[2],
        summed[3],
        summed[4],
        summed[5],
        summed[6],
        summed[7],
        grad_values,
    )


def solution(mesh):
    in_specs = (
        P(("head", "blk"), None),
        P(("head", "blk")),
        P(("head", "blk"), None),
        P(("head", "blk"), None),
        P(("head", "blk")),
        P(("head", "blk"), None),
        P(("head", "blk"), None),
        P(("head", "blk"), None),
        P(("head", "blk"), None),
        P(("head", "blk"), None),
        P(),
        P(),
        P(("head", "blk"), None, None, None),
        P(("head", "blk"), None),
    )
    out_specs = (
        P(("head", "blk"), None),
        P(("head", "blk"), None),
        P(("head", "blk")),
        P(("head", "blk"), None),
        P(("head", "blk"), None),
        P(("head", "blk")),
        P(("head", "blk"), None),
        P(("head", "blk"), None),
        P(("head", "blk"), None),
        P(("head", "blk"), None),
        P(("head", "blk"), None),
    )
    return jax.shard_map(body, mesh=mesh, in_specs=in_specs, out_specs=out_specs, check_vma=False)
```

profile of v0, /device:TPU:0, one launch (start us, length us, event | category | flops | bytes accessed | tf_op | source)
XLA Modules:
  0.0 5340.1 jit_solution(9489242389049750076)
XLA Ops:
  17.7 41.3 all-reduce.5
  59.8 23.4 all-gather.11.cloned.1.call-done
  88.1 29.1 all_to_all.112
  128.0 90.7 %gather_fusion.6 = s32[16384]{0:T(1024)S(1)} fusion(s32[16384]{0:T(1024)S(1)} %add_select_fusion.1, s32[16384]{0:T(1024)S(1)} %get-tuple-element.813), kind=kCustom, calls=%fused_computation.6 | custom fusion | bytes 196608 | tf_op jit(solution)/shard_map/gather | solution.py:251
  246.2 60.3 %scatter_custom_fusion.1 = s32[16384]{0:T(1024)S(1)} fusion(s32[16384]{0:T(1024)S(1)} %get-tuple-element.814, s32[16384]{0:T(1024)S(1)} %select_subtract_fusion, s32[]{:T(128)} %constant.173.clone.1), kind=kCustom, calls=%fused_computation.232 | custom fusion | bytes 65540 | tf_op jit(solution)/shard_map/scatter | solution.py:252
  307.2 60.9 %scatter_custom_fusion.2 = s32[32768]{0:T(1024)} fusion(s32[16384]{0:T(1024)S(1)} %get-tuple-element.787, s32[16384]{0:T(1024)S(1)} %get-tuple-element.812, s32[]{:T(128)} %constant.173.clone.1), kind=kCustom, calls=%fused_computation.225 | custom fusion | bytes 131076 | tf_op jit(solution)/shard_map/scatter | solution.py:257
  388.2 127.9 %while.53 = (s32[]{:T(128)}, f32[4,512]{1,0:T(4,128)S(1)}, f32[4,512]{1,0:T(4,128)S(1)}, f32[4,512,64]{1,2,0:T(8,128)S(1)}, s32[8]{0:T(128)S(1)}, /*index=5*/s32...) while((s32[]{:T(128)}, f32[4,512]{1,0:T(4,128)S(1)}, ...), condition=%wide.region_7.8_spmd.clone, body=%wide.region_3.7_spmd.clone.sunk | while | flops 283264000 | bytes 17725656 | solution.py:51
  521.7 161.9 %gather_fusion.7 = bf16[32768,1024]{1,0:T(8,128)(2,1)} fusion(bf16[2048,1024]{1,0:T(8,128)(2,1)} %param.31, s32[32768]{0:T(1024)S(1)} %broadcast_clamp_fusion), kind=kCustom, calls=%fused_computation.7 | custom fusion | bytes 134348800 | tf_op jit(solution)/shard_map/gather | solution.py:59
  694.3 557.5 %all-gather.17.cloned.1.call-done = bf16[1024,1024]{1,0:T(8,128)(2,1)} async-done(((bf16[32,1024]{1,0:T(8,128)(2,1)}), bf16[1024,1024]{1,0:T(8,128)(2,1)}) %all-gather.17.cloned.1.call-update) | async-done | bytes 2097168 | tf_op jit(solution)/shard_map/all_gather | solution.py:118
  1254.2 328.2 %all-gather.19.cloned.1.call-done = bf16[1024,4096]{1,0:T(8,128)(2,1)} async-done(((bf16[32,4096]{1,0:T(8,128)(2,1)}), bf16[1024,4096]{1,0:T(8,128)(2,1)}) %all-gather.19.cloned.1.call-update) | async-done | bytes 8388624 | tf_op jit(solution)/shard_map/all_gather | solution.py:120
  1587.9 298.5 %all-gather.21.cloned.1.call-done = bf16[2048,512]{1,0:T(8,128)(2,1)} async-done(((bf16[64,512]{1,0:T(8,128)(2,1)}), bf16[2048,512]{1,0:T(8,128)(2,1)}) %all-gather.21.cloned.1.call-update) | async-done | bytes 2097168 | tf_op jit(solution)/shard_map/all_gather | solution.py:121
  1901.2 50.1 all-gather.23.cloned.1.call-done
  1953.3 315.1 %all-to-all-done.4 = bf16[32,1024,1024]{2,1,0:T(8,128)(2,1)} async-done(((bf16[32,1024,1024]{2,1,0:T(8,128)(2,1)}), bf16[32,1024,1024]{2,1,0:T(8,128)(2,1)}, u32[]{:S(2)}, u32[]{:S(2)}) %all-to-all-start.4) | async-done | bytes 67108896 | tf_op jit(solution)/shard_map/all_to_all | solution.py:58
  2272.2 300.2 %gather_fusion.8 = bf16[16384,1024]{1,0:T(8,128)(2,1)} fusion(bf16[32768,1024]{1,0:T(8,128)(2,1)} %bitcast.70, s32[16384]{0:T(1024)S(1)} %copy-done.48), kind=kCustom, calls=%fused_computation.8 | custom fusion | bytes 67174400 | tf_op jit(solution)/shard_map/gather | solution.py:261
  2648.1 112.2 %while.54 = (s32[]{:T(128)}, f32[4,512,64]{1,2,0:T(8,128)}, s32[8]{0:T(128)S(1)}, s32[4096]{0:T(1024)S(1)}, s32[512]{0:T(512)S(1)}, /*index=5*/s32[3]{0:T(128)S(...) while((s32[]{:T(128)}, f32[4,512,64]{1,2,0:T(8,128)}, ...), condition=%wide.region_26.27_spmd.clone, body=%wide.region_24.26_spmd.clone.sunk | while | flops 410131456 | bytes 13416671 | solution.py:51
  2770.2 149.0 %while.55 = (s32[]{:T(128)}, f32[4,512,64]{1,2,0:T(8,128)}, f32[4,512,64]{1,2,0:T(8,128)}, s32[512]{0:T(512)S(1)}, s32[8]{0:T(128)S(1)}, /*index=5*/s32[4096]{0:...) while((s32[]{:T(128)}, f32[4,512,64]{1,2,0:T(8,128)}, ...), condition=%wide.region_29.30_spmd.clone, body=%wide.region_27.29_spmd.clone.sunk | while | flops 548805632 | bytes 20273388 | solution.py:51
  2981.9 256.0 %scatter_custom_fusion.5 = bf16[32768,1024]{1,0:T(8,128)(2,1)} fusion(s32[16384]{0:T(1024)} %get-tuple-element.657, bf16[16384,1024]{1,0:T(8,128)(2,1)} %fusion.46, s32[16384]{0:T(1024)S(1)} %broadcast_clamp_fusion.2, bf16[]{:T(256)} %constant.190.clone.1), kind=kCustom, calls=%fused_computation.93 | custom fusion | bytes 67109376 | tf_op jit(solution)/shard_map/scatter | solution.py:311
  3276.3 1569.7 %all-reduce.4 = (f32[1024]{0:T(1024)S(1)}, f32[1024]{0:T(1024)S(1)}) all-reduce(f32[1024]{0:T(1024)S(1)} %get-tuple-element.661, f32[1024]{0:T(1024)S(1)} %copy-done.60), channel_id=2, replica_groups=mesh['head'=4,'blk'=8] {'head','blk'}, use_global_device_ids=true, to_apply=%region_33.34.clone | all-reduce | flops 2048 | bytes 16384
  4853.5 332.7 %while.52 = (s32[]{:T(128)}, f32[2048,1024]{1,0:T(8,128)}, s32[32,1024]{1,0:T(8,128)S(1)}, bf16[32,1024,1024]{2,1,0:T(8,128)(2,1)}, s32[]{:T(128)}, /*index=5*/s32[]{:T(128)}, s32[]{:T(128)}, s32[]{:T(128)}) while((s32[]{:T(128)}, f32[2048,1024]{1,0:T(8,128)}, s32[32,1024]{1,0:T(8,128)S(1)}, bf16[32,1024,1024]{2,1,0:T(8,128)(2,1)}, ...), condition=%wide.region_45.46_spmd, body=%wide.region_43.45_spmd.sunk | while | flops 33554436 | bytes 109314192 | solution.py:326
  4853.6 23.0 constant_dynamic-slice_fusion.14
  4876.6 142.4 %scatter_custom_fusion.15 = f32[2048,1024]{1,0:T(8,128)} fusion(f32[2048,1024]{1,0:T(8,128)} %get-tuple-element.1287, s32[16384]{0:T(1024)S(1)} %bitcast.413, bf16[16384,1024]{1,0:T(8,128)(2,1)} %bitcast.382), kind=kCustom, calls=%fused_computation.20.clone.1 | custom fusion | flops 33554432 | bytes 41943040 | tf_op jit(solution)/shard_map/while/body/eval_jaxpr/scatter-add | solution.py:324
  5019.0 24.7 constant_dynamic-slice_fusion.14
  5043.8 142.4 %scatter_custom_fusion.15 = f32[2048,1024]{1,0:T(8,128)} fusion(f32[2048,1024]{1,0:T(8,128)} %get-tuple-element.1287, s32[16384]{0:T(1024)S(1)} %bitcast.413, bf16[16384,1024]{1,0:T(8,128)(2,1)} %bitcast.382), kind=kCustom, calls=%fused_computation.20.clone.1 | custom fusion | flops 33554432 | bytes 41943040 | tf_op jit(solution)/shard_map/while/body/eval_jaxpr/scatter-add | solution.py:324
  5186.3 147.1 %reduce-scatter.11.cloned.1.call-done = f32[32,4096]{1,0:T(8,128)} async-done(((f32[1024,4096]{1,0:T(8,128)}), f32[32,4096]{1,0:T(8,128)}) %reduce-scatter.11.cloned.1.call-update) | async-done | bytes 524304 | tf_op jit(solution)/shard_map/reduce_scatter | solution.py:448
  (725 shorter events, 700.2 us)
Async XLA Ops:
  7.2 76.0 %all-gather.11.cloned.1.call-start = ((), (), s32[]{:S(2)}) async-start(), calls=%async_computation.17 | async-start | bytes 6488064 | tf_op jit(solution)/shard_map/all_gather | solution.py:117
  11.9 47.1 all-to-all-start
  17.1 362.6 %all-gather.13.cloned.1.call-start = ((), (), s32[]{:S(2)}) async-start(), calls=%async_computation.18 | async-start | bytes 2359296 | tf_op jit(solution)/shard_map/all_gather | solution.py:206
  118.4 265.6 %all-gather.15.cloned.1.call-start = ((), (), s32[]{:S(2)}) async-start(), calls=%async_computation.19 | async-start | bytes 2359296 | tf_op jit(solution)/shard_map/all_gather | solution.py:207
  517.6 166.0 %all-to-all-start.2 = ((bf16[4,128,256]{1,2,0:T(8,128)(2,1)}), bf16[4,128,256]{1,2,0:T(8,128)(2,1)}, u32[]{:S(2)}, u32[]{:S(2)}) async-start(bf16[4,128,256]{1,2,0:T(8,128)(2,1)} %copy.190), calls=%async_computation.2 | async-start | bytes 524288 | tf_op jit(solution)/shard_map/all_to_all | solution.py:217
  683.7 1584.7 %all-to-all-start.4 = ((bf16[32,1024,1024]{2,1,0:T(8,128)(2,1)}), bf16[32,1024,1024]{2,1,0:T(8,128)(2,1)}, u32[]{:S(2)}, u32[]{:S(2)}) async-start(bf16[32,1024,1024]{2,1,0:T(8,128)(2,1)} %bitcast.69), calls=%async_computation.4 | async-start | bytes 134217728 | tf_op jit(solution)/shard_map/all_to_all | solution.py:58
  688.9 562.9 %all-gather.17.cloned.1.call-start = ((), (), s32[]{:S(2)}) async-start(), calls=%async_computation.20 | async-start | bytes 2162688 | tf_op jit(solution)/shard_map/all_gather | solution.py:118
  689.5 892.9 %all-gather.19.cloned.1.call-start = ((), (), s32[]{:S(2)}) async-start(), calls=%async_computation.21 | async-start | bytes 8650752 | tf_op jit(solution)/shard_map/all_gather | solution.py:120
  690.1 1196.3 %all-gather.21.cloned.1.call-start = ((), (), s32[]{:S(2)}) async-start(), calls=%async_computation.22 | async-start | bytes 2162688 | tf_op jit(solution)/shard_map/all_gather | solution.py:121
  690.7 1260.6 %all-gather.23.cloned.1.call-start = ((), (), s32[]{:S(2)}) async-start(), calls=%async_computation.23 | async-start | bytes 2162688 | tf_op jit(solution)/shard_map/all_gather | solution.py:122
  691.4 1893.9 %all-gather.25.cloned.1.call-start = ((), (), s32[]{:S(2)}) async-start(), calls=%async_computation.24 | async-start | bytes 2162688 | tf_op jit(solution)/shard_map/all_gather | solution.py:123
  692.2 2077.9 %all-gather.27.cloned.1.call-start = ((), (), s32[]{:S(2)}) async-start(), calls=%async_computation.25 | async-start | bytes 2359296 | tf_op jit(solution)/shard_map/all_gather | solution.py:416
  2268.4 316.9 %all-to-all-start.6 = ((bf16[8,16,1024]{2,1,0:T(8,128)(2,1)}), bf16[8,16,1024]{2,1,0:T(8,128)(2,1)S(1)}, u32[]{:S(2)}, u32[]{:S(2)}) async-start(bf16[8,16,1024]{2,1,0:T(8,128)(2,1)} %bitcast.416), calls=%async_computation.6 | async-start | bytes 524288 | tf_op jit(solution)/shard_map/all_to_all | solution.py:105
  2631.8 14.2 all-to-all-start.7
  2635.3 134.9 %all-gather.29.cloned.1.call-start = ((), (), s32[]{:S(2)}) async-start(), calls=%async_computation.26 | async-start | bytes 2359296 | tf_op jit(solution)/shard_map/all_gather | solution.py:417
  2922.9 31.6 all-to-all-start.8
  2966.5 271.4 %all-to-all-start.9 = ((bf16[8,16,1024]{2,1,0:T(8,128)(2,1)}), bf16[8,16,1024]{2,1,0:T(8,128)(2,1)S(1)}, u32[]{:S(2)}, u32[]{:S(2)}) async-start(bf16[8,16,1024]{2,1,0:T(8,128)(2,1)} %bitcast.111), calls=%async_computation.9 | async-start | bytes 524288 | tf_op jit(solution)/shard_map/all_to_all | solution.py:463
  3238.6 1610.5 %all-to-all-start.10 = ((bf16[32,1024,1024]{2,1,0:T(8,128)(2,1)}), bf16[32,1024,1024]{2,1,0:T(8,128)(2,1)}, u32[]{:S(2)}, u32[]{:S(2)}) async-start(bf16[32,1024,1024]{2,1,0:T(8,128)(2,1)} %bitcast.117), calls=%async_computation.16 | async-start | bytes 134217728 | tf_op jit(solution)/shard_map/all_to_all | solution.py:314
  3243.7 1942.5 %reduce-scatter.9.cloned.1.call-start = ((), (), s32[]{:S(2)}) async-start(), calls=%async_computation.28 | async-start | bytes 4325376 | tf_op jit(solution)/shard_map/reduce_scatter | solution.py:446
  3247.5 1938.7 %reduce-scatter.13.cloned.1.call-start = ((), (), s32[]{:S(2)}) async-start(), calls=%async_computation.30 | async-start | bytes 4325376 | tf_op jit(solution)/shard_map/reduce_scatter | solution.py:449
  3250.6 1935.6 %reduce-scatter.15.cloned.1.call-start = ((), (), s32[]{:S(2)}) async-start(), calls=%async_computation.31 | async-start | bytes 4325376 | tf_op jit(solution)/shard_map/reduce_scatter | solution.py:450
  3254.6 1931.7 %reduce-scatter.17.cloned.1.call-start = ((), (), s32[]{:S(2)}) async-start(), calls=%async_computation.32 | async-start | bytes 4325376 | tf_op jit(solution)/shard_map/reduce_scatter | solution.py:451
  3257.3 1929.0 %reduce-scatter.7.cloned.1.call-start = ((), (), s32[]{:S(2)}) async-start(), calls=%async_computation.27 | async-start | bytes 12976128 | tf_op jit(solution)/shard_map/reduce_scatter | solution.py:445
  3263.9 2069.5 %reduce-scatter.11.cloned.1.call-start = ((), (), s32[]{:S(2)}) async-start(), calls=%async_computation.29 | async-start | bytes 17301504 | tf_op jit(solution)/shard_map/reduce_scatter | solution.py:448
  (73 other events, 7302.4 us)
Sparse Core Ops, SparseCore 0:
  10.9 72.2 all-gather.10
  118.6 26.2 all-gather.12
  219.6 26.1 all-gather.14
  692.3 559.4 all-gather.16
  1254.5 327.8 all-gather.18
  1585.1 301.2 all-gather.20
  1889.3 61.9 all-gather.22
  1954.1 136.1 all-gather.24
  2092.2 102.8 all-gather.26
  2646.9 28.2 all-gather.28
  3247.6 630.1 reduce-scatter.8
  3880.4 767.0 reduce-scatter.12
  4650.4 188.6 reduce-scatter.14
  4841.8 149.0 reduce-scatter.16
  4997.3 151.2 reduce-scatter.6
  5151.5 181.8 reduce-scatter.10
where the time goes:
time: 5360 us; the launch traced here: 5340 us
  waiting for transfers between devices  1740 us (32%)
  blocking collectives  1660 us (31%)
  local copies, waits for them, and re-layouts  1150 us (21%)
  other arithmetic  428 us (8%)
  matrix products  301 us (6%)
    unnamed x2, blocking collectives  1610 us
    all_gather x1, waiting for transfers between devices, body(): lax.all_gather(attn_out, ('head', 'blk'), axis=0, tiled=True)  558 us
    all_gather x1, waiting for transfers between devices, body(): lax.all_gather(memory_query, ('head', 'blk'), axis=0, tiled=True)  328 us
    all_to_all x1, waiting for transfers between devices, fetch_rows(): lax.all_to_all(memory_values[asked], ('head', 'blk'), split_axis=0, conca...  315 us
    gather x1, local copies, waits for them, and re-layouts, body(): fetched.reshape(devices * capacity, model_width)[target]  300 us
    all_gather x1, waiting for transfers between devices, body(): lax.all_gather(sub_keys, ('head', 'blk'), axis=0, tiled=True)  299 us
    scatter-add x2, other arithmetic, accumulate(): jax.ops.segment_sum(block_rows, row_ids, num_segments=own_rows)  285 us
    scatter x2, local copies, waits for them, and re-layouts, body(): outgoing = jnp.zeros((devices * capacity, model_width), jnp.bfloat16).at[...  256 us
  transfers between devices with their start and end apart: 26, of which 9 were waited for; matrix products, arithmetic and copies ran while one was open for 30% of the time, Pallas kernels for 0%

commit v1 on v0

v1 whole, which is shorter than its diff:
```python
import math

import jax
import jax.numpy as jnp
from jax import lax
from jax.experimental import pallas as pl
from jax.experimental.pallas import tpu as pltpu
from jax.sharding import Mesh
from jax.sharding import PartitionSpec as P

NH = 16
HD = 64
MH = 4
QHALF = 512
NSUB = 256
KPICK = 32
TP = 2 * MH

GROUP = ("head", "outer")
BLK = ("outer", "tp")
ALL = ("head", "outer", "tp")

epsilon = 1e-06
neg_big = -1e30
LANES = 128
bf16 = jnp.bfloat16
f32 = jnp.float32
NT = (((1,), (1,)), ((), ()))
TN = (((0,), (0,)), ((), ()))


def mm(left, right, dims=(((1,), (0,)), ((), ()))):
    return lax.dot_general(left, right, dims, preferred_element_type=f32)


def params(mib):
    return pltpu.CompilerParams(vmem_limit_bytes=mib * 1024 * 1024)


def head_rows(pair):
    lane = lax.broadcasted_iota(jnp.int32, pair.shape, 1)
    zero = jnp.zeros_like(pair)
    return (jnp.where(lane < HD, pair, zero), jnp.where(lane < HD, zero, pair))


def key_range(base, block_q, block_k, low_first_ref):
    step = pl.program_id(0)
    first = low_first_ref[step] // block_k
    last = (base + (step + 1) * block_q - 1) // block_k
    return step, first, last + 1


def attn_fwd_kernel(base, block_k, low_first_ref, q_ref, kv_ref, low_ref, att_ref, lse_ref):
    block_q = q_ref.shape[0]
    step, first, stop = key_range(base, block_q, block_k, low_first_ref)
    queries = head_rows(q_ref[...])
    low = low_ref[...]
    high = base + step * block_q + lax.broadcasted_iota(jnp.int32, (1, block_q), 1)

    def visit(turn, carried):
        start = pl.multiple_of(turn * block_k, block_k)
        keys = kv_ref[pl.ds(start, block_k), :LANES]
        values = kv_ref[pl.ds(start, block_k), LANES:]
        place = start + lax.broadcasted_iota(jnp.int32, (block_k, block_q), 0)
        allowed = (place >= low) & (place <= high)
        out = []
        for head in range(2):
            run_max, run_sum, run_acc = carried[head]
            scores = jnp.where(allowed, mm(keys, queries[head], NT), neg_big)
            new_max = jnp.maximum(run_max, jnp.max(scores, axis=0, keepdims=True))
            powers = jnp.exp(scores - new_max)
            rescale = jnp.exp(run_max - new_max)
            run_sum = run_sum * rescale + jnp.sum(powers, axis=0, keepdims=True)
            run_acc = run_acc * rescale + mm(values, powers.astype(bf16), TN)
            out.append((new_max, run_sum, run_acc))
        return tuple(out)

    fresh = (
        jnp.full((1, block_q), neg_big, f32),
        jnp.zeros((1, block_q), f32),
        jnp.zeros((LANES, block_q), f32),
    )
    done = lax.fori_loop(first, stop, visit, (fresh, fresh))
    att_ref[:HD, :] = done[0][2][:HD] / done[0][1]
    att_ref[HD:, :] = done[1][2][HD:] / done[1][1]
    lse_ref[0:1, :] = done[0][0] + jnp.log(done[0][1])
    lse_ref[1:2, :] = done[1][0] + jnp.log(done[1][1])


def attn_fwd(base, low_first, low, queries, keys_values):
    rows = queries.shape[0]
    block_q, block_k = 256, 512
    return pl.pallas_call(
        lambda *refs: attn_fwd_kernel(base, block_k, *refs),
        grid_spec=pltpu.PrefetchScalarGridSpec(
            num_scalar_prefetch=1,
            grid=(rows // block_q,),
            in_specs=[
                pl.BlockSpec((block_q, LANES), lambda i, s: (i, 0)),
                pl.BlockSpec(keys_values.shape, lambda i, s: (0, 0)),
                pl.BlockSpec((1, block_q), lambda i, s: (0, i)),
            ],
            out_specs=[
                pl.BlockSpec((LANES, block_q), lambda i, s: (0, i)),
                pl.BlockSpec((2, block_q), lambda i, s: (0, i)),
            ],
        ),
        out_shape=[
            jax.ShapeDtypeStruct((LANES, rows), f32),
            jax.ShapeDtypeStruct((2, rows), f32),
        ],
        compiler_params=params(32),
        name="attn_fwd",
    )(low_first[::block_q], queries, keys_values, low[None, :])


def attn_bwd_kernel(
    base,
    block_k,
    low_first_ref,
    q_ref,
    kv_ref,
    low_ref,
    lse_ref,
    att_ref,
    grad_ref,
    dq_ref,
    dk_ref,
    dv_ref,
):
    block_q = q_ref.shape[0]
    step, first, stop = key_range(base, block_q, block_k, low_first_ref)

    @pl.when(step == 0)
    def clear():
        dk_ref[...] = jnp.zeros_like(dk_ref)
        dv_ref[...] = jnp.zeros_like(dv_ref)

    queries = head_rows(q_ref[...])
    grads = head_rows(grad_ref[...])
    grad_turned = jnp.transpose(grad_ref[...].astype(f32)) * att_ref[...]
    deltas = (
        jnp.sum(grad_turned[:HD], axis=0, keepdims=True),
        jnp.sum(grad_turned[HD:], axis=0, keepdims=True),
    )
    low = low_ref[...]
    high = base + step * block_q + lax.broadcasted_iota(jnp.int32, (1, block_q), 1)

    def visit(turn, carried):
        start = pl.multiple_of(turn * block_k, block_k)
        keys = kv_ref[pl.ds(start, block_k), :LANES]
        values = kv_ref[pl.ds(start, block_k), LANES:]
        place = start + lax.broadcasted_iota(jnp.int32, (block_k, block_q), 0)
        allowed = (place >= low) & (place <= high)
        out = []
        grad_key = dk_ref[pl.ds(start, block_k), :]
        grad_value = dv_ref[pl.ds(start, block_k), :]
        for head in range(2):
            scores = mm(keys, queries[head], NT)
            probs = jnp.where(allowed, jnp.exp(scores - lse_ref[head : head + 1, :]), 0.0)
            grad_probs = mm(values, grads[head], NT)
            grad_scores = (probs * (grad_probs - deltas[head])).astype(bf16)
            grad_key = grad_key + mm(grad_scores, queries[head])
            grad_value = grad_value + mm(probs.astype(bf16), grads[head])
            out.append(carried[head] + mm(keys, grad_scores, TN))
        dk_ref[pl.ds(start, block_k), :] = grad_key
        dv_ref[pl.ds(start, block_k), :] = grad_value
        return tuple(out)

    fresh = jnp.zeros((LANES, block_q), f32)
    done = lax.fori_loop(first, stop, visit, (fresh, fresh))
    dq_ref[:HD, :] = done[0][:HD]
    dq_ref[HD:, :] = done[1][HD:]


def attn_bwd(base, low_first, low, queries, keys_values, lse, att, grads):
    rows = queries.shape[0]
    block_q, block_k = 256, 512
    span = keys_values.shape[0]
    return pl.pallas_call(
        lambda *refs: attn_bwd_kernel(base, block_k, *refs),
        grid_spec=pltpu.PrefetchScalarGridSpec(
            num_scalar_prefetch=1,
            grid=(rows // block_q,),
            in_specs=[
                pl.BlockSpec((block_q, LANES), lambda i, s: (i, 0)),
                pl.BlockSpec(keys_values.shape, lambda i, s: (0, 0)),
                pl.BlockSpec((1, block_q), lambda i, s: (0, i)),
                pl.BlockSpec((2, block_q), lambda i, s: (0, i)),
                pl.BlockSpec((LANES, block_q), lambda i, s: (0, i)),
                pl.BlockSpec((block_q, LANES), lambda i, s: (i, 0)),
            ],
            out_specs=[
                pl.BlockSpec((LANES, block_q), lambda i, s: (0, i)),
                pl.BlockSpec((span, LANES), lambda i, s: (0, 0)),
                pl.BlockSpec((span, LANES), lambda i, s: (0, 0)),
            ],
        ),
        out_shape=[
            jax.ShapeDtypeStruct((LANES, rows), f32),
            jax.ShapeDtypeStruct((span, LANES), f32),
            jax.ShapeDtypeStruct((span, LANES), f32),
        ],
        compiler_params=params(48),
        name="attn_bwd",
    )(low_first[::block_q], queries, keys_values, low[None, :], lse, att, grads)


def hits(count, row):
    return lax.broadcasted_iota(jnp.int32, (count, row.shape[1]), 0) == row


def one_hot(count, row):
    return jnp.where(hits(count, row), 1.0, 0.0).astype(bf16)


def bucket_kernel(high_ref, low_ref, load_ref, out_ref):
    loads = load_ref.shape[0]
    chunks = high_ref.shape[0]
    total = jnp.zeros(out_ref.shape, f32)
    for chunk in range(chunks):
        high = one_hot(out_ref.shape[0], high_ref[chunk : chunk + 1, :])
        mask = hits(LANES, low_ref[chunk : chunk + 1, :])
        parts = [
            jnp.where(mask, load_ref[load, chunk : chunk + 1, :], 0.0).astype(bf16)
            for load in range(loads)
        ]
        total = total + mm(high, jnp.concatenate(parts, axis=0), NT)
    out_ref[...] = total


def to_buckets(high, low, loads, places):
    return pl.pallas_call(
        bucket_kernel,
        out_shape=jax.ShapeDtypeStruct((places // LANES, loads.shape[0] * LANES), f32),
        compiler_params=params(32),
        name="to_buckets",
    )(high, low, loads)


def unbucket_kernel(high_ref, low_ref, main_ref, rest_ref, out_ref):
    count = main_ref.shape[1]
    for chunk in range(high_ref.shape[0]):
        high = one_hot(count, high_ref[chunk : chunk + 1, :])
        found = mm(main_ref[...], high) + mm(rest_ref[...], high)
        mask = hits(LANES, low_ref[chunk : chunk + 1, :])
        out_ref[chunk : chunk + 1, :] = jnp.sum(
            jnp.where(mask, found, 0.0), axis=0, keepdims=True
        )


def from_buckets(high, low, table):
    turned = jnp.transpose(table)
    main = turned.astype(bf16)
    rest = (turned - main.astype(f32)).astype(bf16)
    return pl.pallas_call(
        unbucket_kernel,
        out_shape=jax.ShapeDtypeStruct(high.shape, f32),
        compiler_params=params(32),
        name="from_buckets",
    )(high, low, main, rest)


def place_rows(rows, subs, token_row, first_row):
    tokens = one_hot(rows, token_row)
    return jnp.concatenate(
        [tokens * jnp.where(first_row == first, 1.0, 0.0).astype(bf16) for first in range(subs)],
        axis=0,
    )


def spread_kernel(rows, subs, token_ref, first_ref, second_ref, weight_ref, out_ref):
    left = place_rows(rows, subs, token_ref[0], first_ref[0])
    right = jnp.where(hits(NSUB, second_ref[0]), weight_ref[0], 0.0).astype(bf16)
    table = mm(left, right, NT).astype(bf16)
    for first in range(subs):
        out_ref[:, first * NSUB : (first + 1) * NSUB] = table[first * rows : (first + 1) * rows]


def spread_weights(rows, subs, token, first, second, weight):
    devices, unused, capacity = token.shape
    row = pl.BlockSpec((1, 1, capacity), lambda i: (i, 0, 0))
    return pl.pallas_call(
        lambda *refs: spread_kernel(rows, subs, *refs),
        grid=(devices,),
        in_specs=[row, row, row, row],
        out_specs=pl.BlockSpec((rows, subs * NSUB), lambda i: (i, 0)),
        out_shape=jax.ShapeDtypeStruct((devices * rows, subs * NSUB), bf16),
        compiler_params=params(48),
        name="spread_weights",
    )(token, first, second, weight)


def dots_kernel(rows, subs, token_ref, first_ref, second_ref, grad_ref, value_ref, out_ref):
    pair = token_ref.shape[0]
    found = []
    for first in range(subs):
        found.append(
            mm(value_ref[first * NSUB : (first + 1) * NSUB, :], grad_ref[...], NT).astype(bf16)
        )
    for block in range(pair):
        left = place_rows(rows, subs, token_ref[block], first_ref[block])
        table = jnp.concatenate(
            [part[:, block * rows : (block + 1) * rows] for part in found], axis=1
        )
        spread = mm(table, left)
        out_ref[block] = jnp.sum(
            jnp.where(hits(NSUB, second_ref[block]), spread, 0.0), axis=0, keepdims=True
        )


def row_dots(rows, subs, token, first, second, grads, values):
    devices, unused, capacity = token.shape
    pair = 2
    row = pl.BlockSpec((pair, 1, capacity), lambda i: (i, 0, 0))
    return pl.pallas_call(
        lambda *refs: dots_kernel(rows, subs, *refs),
        grid=(devices // pair,),
        in_specs=[
            row,
            row,
            row,
            pl.BlockSpec((pair * rows, grads.shape[1]), lambda i: (i, 0)),
            pl.BlockSpec(values.shape, lambda i: (0, 0)),
        ],
        out_specs=row,
        out_shape=jax.ShapeDtypeStruct(token.shape, f32),
        compiler_params=params(48),
        name="row_dots",
    )(token, first, second, grads, values)


def swap(array, axes):
    return lax.all_to_all(array, axes, split_axis=0, concat_axis=0, tiled=True)


def gather(array, axes):
    return lax.all_gather(array, axes, axis=0, tiled=True)


def sum_back(partial, rows):
    pieces = swap(partial.astype(bf16).reshape(TP, rows, -1), "tp")
    return jnp.sum(pieces.astype(f32), axis=0)


def norm_scale(hidden):
    return lax.rsqrt(jnp.mean(hidden * hidden, axis=-1, keepdims=True) + epsilon)


def norm_back(hidden, scale, weighted):
    coupled = jnp.mean(hidden * weighted, axis=-1, keepdims=True)
    return scale * weighted - hidden * (scale * scale * scale) * coupled


def body(
    inputs,
    attn_gain,
    attn_qkv,
    attn_out,
    memory_gain,
    memory_query,
    sub_keys,
    memory_gate,
    memory_out,
    memory_values,
    doc_lengths,
    token_order,
    memory_picks,
    cotangent,
):
    rows, width = inputs.shape
    outer = lax.axis_size("outer")
    heads = lax.axis_size("head")
    groups = heads * outer
    blocks = outer * TP
    devices = groups * TP
    share = rows // blocks
    span = TP * rows
    tokens = token_order.shape[0]
    head_index = lax.axis_index("head")
    outer_index = lax.axis_index("outer")
    group_index = head_index * outer + outer_index
    rows_w = attn_qkv.shape[0]
    own_rows = memory_values.shape[0]
    subs = own_rows // NSUB
    picks = MH * KPICK
    capacity = 2 * rows * picks // devices
    back = min(groups - 1, -(-(tokens // 2 - 1) // span))
    base = back * span

    gain_one = attn_gain.astype(f32)[:, None]
    gain_two = memory_gain.astype(f32)[:, None]
    scaled_qkv = (attn_qkv.astype(f32) * gain_one).astype(bf16)
    scaled_query = (memory_query.astype(f32) * gain_two).astype(bf16)
    scaled_gate = (memory_gate.astype(f32) * gain_two).astype(bf16)

    def columns(piece):
        return jnp.moveaxis(piece, 1, 0).reshape(TP, rows_w, -1)

    qkv_cut = jnp.transpose(scaled_qkv.reshape(rows_w, 3, TP, LANES), (2, 0, 1, 3))
    weight_qkv = gather(swap(qkv_cut.reshape(TP, rows_w, 3 * LANES), "tp").reshape(TP * rows_w, -1), GROUP)
    rest_cut = jnp.concatenate(
        [columns(scaled_query.reshape(rows_w, TP, -1)), columns(scaled_gate.reshape(rows_w, TP, -1))],
        axis=2,
    )
    weight_rest = gather(swap(rest_cut, "tp").reshape(TP * rows_w, -1), GROUP)
    to_turned = [
        (groups * part + group, group * TP + part) for group in range(groups) for part in range(TP)
    ]
    from_turned = [(there, here) for here, there in to_turned]
    row_cut = jnp.stack([attn_out, memory_out, sub_keys.reshape(rows_w, width)])
    row_all = lax.all_gather(lax.ppermute(row_cut, ALL, to_turned), GROUP, axis=1, tiled=True)
    weight_attn = row_all[0]
    weight_mixed = row_all[1]
    key_table = row_all[2].reshape(NSUB, QHALF)

    by_half = jnp.transpose(
        memory_picks.reshape(outer, TP * share, MH, KPICK, 2), (0, 2, 4, 1, 3)
    ).reshape(blocks, TP * share, KPICK)
    half_index = swap(by_half, BLK).reshape(span, KPICK)
    first_pick = memory_picks[:, :, :, 0].reshape(rows, picks)
    second_pick = memory_picks[:, :, :, 1].reshape(rows, picks)
    owner = first_pick // subs
    device_range = jnp.arange(devices, dtype=jnp.int32)
    owned = (owner[None] == device_range[:, None, None]).astype(bf16)
    before = (
        jnp.arange(picks, dtype=jnp.int32)[:, None] < jnp.arange(picks, dtype=jnp.int32)[None, :]
    ).astype(bf16)
    before_rows = (
        jnp.arange(rows, dtype=jnp.int32)[:, None] < jnp.arange(rows, dtype=jnp.int32)[None, :]
    ).astype(bf16)
    in_row = jnp.einsum("dtk,kj->dtj", owned, before, preferred_element_type=f32)
    row_counts = jnp.sum(owned.astype(f32), axis=2)
    of_rows = jnp.dot(row_counts.astype(bf16), before_rows, preferred_element_type=f32)
    rank = jnp.sum(owned.astype(f32) * (in_row + of_rows[:, :, None]), axis=0).astype(jnp.int32)
    target = owner * capacity + rank
    chunked = (-1, 1024)
    target_high = (target // LANES).reshape(chunked)
    target_low = (target % LANES).reshape(chunked)
    places = devices * capacity
    entry_loads = jnp.stack(
        [
            jnp.broadcast_to(jnp.arange(rows, dtype=jnp.int32)[:, None], (rows, picks)),
            first_pick % subs,
            second_pick,
        ]
    ).astype(f32).reshape(3, -1, 1024)
    entries = to_buckets(target_high, target_low, entry_loads, places)
    entries = jnp.transpose(entries.reshape(devices, capacity // LANES, 3, LANES), (0, 2, 1, 3))
    entries = swap(entries.reshape(devices, 3, capacity).astype(jnp.int32), ALL)
    entry_token = entries[:, 0:1]
    entry_first = entries[:, 1:2]
    entry_second = entries[:, 2:3]

    laid = token_order.reshape(heads, blocks, outer, TP * share)
    mine = lax.dynamic_index_in_dim(laid, head_index, 0, keepdims=False)
    mine = lax.dynamic_index_in_dim(mine, outer_index, 1, keepdims=False)
    local = mine.reshape(span) - group_index * span
    deal = (local[:, None] == jnp.arange(span, dtype=jnp.int32)[None, :]).astype(bf16)

    def dealt(array):
        return mm(deal, array).astype(bf16)

    def undealt(array):
        return mm(deal, array, TN).astype(bf16)

    group_inputs = gather(inputs, "tp")
    group_wide = group_inputs.astype(f32)
    normed_one = (group_wide * norm_scale(group_wide)).astype(bf16)
    projected = mm(normed_one, weight_qkv).astype(bf16)
    queries = projected[:, :LANES] * jnp.asarray(1.0 / math.sqrt(HD), bf16)
    own_kv = projected[:, LANES:]
    keys_values = jnp.concatenate(
        [
            lax.ppermute(own_kv, GROUP, [(at, at + away) for at in range(groups - away)])
            for away in range(back, 0, -1)
        ]
        + [own_kv],
        axis=0,
    )
    positions = group_index * span + jnp.arange(span, dtype=jnp.int32)
    doc_ends = jnp.cumsum(doc_lengths)
    doc_start = jnp.max(
        jnp.where(positions[:, None] >= doc_ends[None, :], doc_ends[None, :], 0), axis=1
    )
    low = doc_start - (group_index - back) * span
    attended, lse = attn_fwd(base, low, low, queries, keys_values)
    attended_low = attended.astype(bf16)
    inputs_wide = inputs.astype(f32)
    hidden_one = inputs_wide + sum_back(mm(attended_low, weight_attn, TN), rows)
    scale_two = norm_scale(hidden_one)
    normed_two = dealt(gather((hidden_one * scale_two).astype(bf16), "tp"))
    dealt_cot = dealt(gather(cotangent, "tp"))

    pre = mm(normed_two, weight_rest)
    query_mem = pre[:, :QHALF].astype(bf16)
    gate_pre = pre[:, QHALF:]
    gate_sig = jax.nn.sigmoid(gate_pre)
    grad_mixed = mm(dealt_cot, weight_mixed, NT)
    grad_memory = (grad_mixed * gate_pre * gate_sig).astype(bf16)
    every_grad = gather(grad_memory, ALL).reshape(
        heads, outer, TP, blocks, TP * share, LANES
    )
    every_grad = jnp.transpose(every_grad, (0, 3, 1, 4, 2, 5)).reshape(devices * rows, width)

    sub_scores = mm(query_mem, key_table, NT)
    sub_range = jnp.arange(NSUB, dtype=jnp.int32)
    half_hit = half_index[:, :, None] == sub_range
    picked_half = jnp.sum(jnp.where(half_hit, sub_scores[:, None, :], 0.0), axis=2)
    picked = swap(picked_half.reshape(blocks, TP * share, KPICK), BLK)
    picked = jnp.transpose(
        picked.reshape(outer, MH, 2, TP * share, KPICK), (0, 3, 1, 2, 4)
    ).reshape(rows, MH, 2, KPICK)
    picked = picked[:, :, 0] + picked[:, :, 1]
    picked_exp = jnp.exp(picked - jnp.max(picked, axis=2, keepdims=True))
    pick_weights = picked_exp / jnp.sum(picked_exp, axis=2, keepdims=True)
    weight_loads = pick_weights.reshape(1, -1, 1024)
    sent_weights = to_buckets(target_high, target_low, weight_loads, places)
    entry_weight = swap(sent_weights.astype(bf16).reshape(devices, 1, capacity), ALL).astype(f32)

    spread = spread_weights(rows, subs, entry_token, entry_first, entry_second, entry_weight)
    partial = mm(spread, memory_values).astype(bf16)
    partial = jnp.transpose(
        partial.reshape(heads, blocks, outer, TP * share, TP, LANES), (0, 2, 4, 1, 3, 5)
    ).reshape(devices * span, LANES)
    memory = lax.psum_scatter(partial, ALL, scatter_dimension=0, tiled=True).astype(f32)
    mixed_low = (memory * gate_pre * gate_sig).astype(bf16)
    grad_gate = (grad_mixed * memory * gate_sig * (1.0 + gate_pre * (1.0 - gate_sig))).astype(bf16)
    output = (hidden_one + sum_back(mm(undealt(mixed_low), weight_mixed), rows)).astype(bf16)
    grad_mixed_rows = mm(mixed_low, dealt_cot, TN)

    entry_dots = row_dots(
        rows, subs, entry_token, entry_first, entry_second, every_grad, memory_values
    )
    returned = swap(entry_dots, ALL).reshape(places // LANES, LANES)
    grad_pick = from_buckets(target_high, target_low, returned).reshape(rows, MH, KPICK)
    grad_picked = pick_weights * (
        grad_pick - jnp.sum(pick_weights * grad_pick, axis=2, keepdims=True)
    )
    to_half = jnp.transpose(grad_picked.reshape(outer, TP * share, MH, KPICK), (0, 2, 1, 3))
    to_half = jnp.broadcast_to(
        to_half[:, :, None], (outer, MH, 2, TP * share, KPICK)
    ).reshape(blocks, TP * share, KPICK)
    grad_half = swap(to_half, BLK).reshape(span, KPICK)
    grad_sub = jnp.sum(jnp.where(half_hit, grad_half[:, :, None], 0.0), axis=1).astype(bf16)
    grad_query = mm(grad_sub, key_table).astype(bf16)
    grad_table = mm(grad_sub, query_mem, TN).reshape(LANES, width)
    grad_values = mm(spread, every_grad, TN)
    grad_pre = jnp.concatenate([grad_query, grad_gate], axis=1)
    grad_rest_cut = mm(normed_two, grad_pre, TN)
    weighted_two = sum_back(mm(undealt(grad_pre), weight_rest, NT), rows)
    grad_hidden = cotangent.astype(f32) + norm_back(hidden_one, scale_two, weighted_two)

    grad_branch = gather(grad_hidden.astype(bf16), "tp")
    grad_attn_rows = mm(attended_low, grad_branch)
    grad_attended = mm(grad_branch, weight_attn, NT).astype(bf16)
    grad_q, grad_k, grad_v = attn_bwd(
        base, low, low, queries, keys_values, lse, attended, grad_attended
    )
    grad_kv = jnp.concatenate([grad_k, grad_v], axis=1)
    own_grad_kv = grad_kv[base:]
    for away in range(1, back + 1):
        piece = grad_kv[base - away * span : base - (away - 1) * span].astype(bf16)
        own_grad_kv = own_grad_kv + lax.ppermute(
            piece, GROUP, [(at + away, at) for at in range(groups - away)]
        ).astype(f32)
    grad_projected = jnp.concatenate(
        [jnp.transpose(grad_q) * (1.0 / math.sqrt(HD)), own_grad_kv], axis=1
    ).astype(bf16)
    grad_qkv_cut = mm(normed_one, grad_projected, TN)
    weighted_one = sum_back(mm(grad_projected, weight_qkv, NT), rows)
    grad_inputs = grad_hidden + norm_back(inputs_wide, norm_scale(inputs_wide), weighted_one)

    def columns_home(cut):
        summed = lax.psum_scatter(cut, GROUP, scatter_dimension=0, tiled=True)
        return jnp.moveaxis(swap(summed.reshape(TP, rows_w, -1), "tp"), 0, 1)

    row_grads = jnp.stack([grad_attn_rows, grad_mixed_rows, grad_table], axis=1)
    row_home = lax.ppermute(
        lax.psum_scatter(row_grads, GROUP, scatter_dimension=0, tiled=True), ALL, from_turned
    )
    rest_home = columns_home(grad_rest_cut)
    query_home = rest_home[:, :, :QHALF].reshape(rows_w, -1)
    gate_home = rest_home[:, :, QHALF:].reshape(rows_w, -1)
    qkv_home = jnp.transpose(
        columns_home(grad_qkv_cut).reshape(rows_w, TP, 3, LANES), (0, 2, 1, 3)
    ).reshape(rows_w, -1)
    grad_attn_gain = jnp.sum(qkv_home * attn_qkv.astype(f32), axis=1)
    grad_memory_gain = jnp.sum(query_home * memory_query.astype(f32), axis=1) + jnp.sum(
        gate_home * memory_gate.astype(f32), axis=1
    )
    return (
        output,
        grad_inputs,
        grad_attn_gain,
        qkv_home * gain_one,
        row_home[:, 0],
        grad_memory_gain,
        query_home * gain_two,
        row_home[:, 2].reshape(sub_keys.shape),
        gate_home * gain_two,
        row_home[:, 1],
        grad_values,
    )


def solution(mesh):
    heads, blocks = mesh.devices.shape
    cut_mesh = Mesh(mesh.devices.reshape(heads, blocks // TP, TP), ALL)
    matrix = P(ALL, None)
    in_specs = (
        matrix,
        P(ALL),
        matrix,
        matrix,
        P(ALL),
        matrix,
        matrix,
        matrix,
        matrix,
        matrix,
        P(),
        P(),
        P(ALL, None, None, None),
        matrix,
    )
    out_specs = (
        matrix,
        matrix,
        P(ALL),
        matrix,
        matrix,
        P(ALL),
        matrix,
        matrix,
        matrix,
        matrix,
        matrix,
    )
    return jax.shard_map(
        body, mesh=cut_mesh, in_specs=in_specs, out_specs=out_specs, check_vma=False
    )
```

time: 5360 us -> 993 us (0.19)
  blocking collectives: 1660 us -> 112 us
  waiting for transfers between devices: 1740 us -> 443 us
  local copies, waits for them, and re-layouts: 1150 us -> 113 us
  other arithmetic: 428 us -> 47 us
  matrix products: 301 us -> 101 us
  Pallas kernels: 0 us -> 92.6 us
    unnamed x2 -> x0, blocking collectives: 1610 us -> none
    all_gather x10 -> x6, waiting for transfers between devices: 1260 us -> 128 us  [gather(): return lax.all_gather(array, axes, axis=0, tiled=True)]
    gather x33 -> x0, local copies, waits for them, and re-layouts: 638 us -> none  [the longest x1 300 us: body(): fetched.reshape(devices * capacity, model_width)[target]]
    scatter x4 -> x0, local copies, waits for them, and re-layouts: 377 us -> none  [the longest x2 256 us: body(): outgoing = jnp.zeros((devices * capacity, model_width), jnp.bfloat16).at[...]
    scatter-add x2 -> x0, other arithmetic: 285 us -> none  [accumulate(): jax.ops.segment_sum(block_rows, row_ids, num_segments=own_rows)]
    all_to_all x10 -> x12, waiting for transfers between devices: 335 us -> 67.2 us  [swap(): return lax.all_to_all(array, axes, split_axis=0, concat_axis=0, tiled=True)]
    dot_general x76 -> x21, matrix products: 301 us -> 101 us  [the longest x19 99.6 us: mm(): return lax.dot_general(left, right, dims, preferred_element_type=f32)]
    dynamic_slice x74 -> x0, local copies, waits for them, and re-layouts: 92.8 us -> none  [the longest x2 47.8 us: accumulate(): lax.dynamic_slice_in_dim(arrived, step_index * sources, sources, 0)]
  transfers between devices with their start and end apart: 26 -> 28, of which waited for: 9 -> 17; matrix products, arithmetic and copies ran while one was open for 30% -> 19% of each run, Pallas kernels for 0% -> 4%
where the time goes in v1:
time: 993 us; the launch traced here: 982 us
  waiting for transfers between devices  443 us (45%)
  local copies, waits for them, and re-layouts  113 us (11%)
  blocking collectives  112 us (11%)
  matrix products  101 us (10%)
  Pallas kernels  92.6 us (9%)
  starting transfers between devices  58.5 us (6%)
  other arithmetic  47 us (5%)
  between operations  15.4 us (2%)
    reduce_scatter x1, waiting for transfers between devices, body(): lax.psum_scatter(partial, ALL, scatter_dimension=0, tiled=True).astype(f32)  140 us
    all_gather x6, waiting for transfers between devices, gather(): return lax.all_gather(array, axes, axis=0, tiled=True)  128 us
    reduce_scatter x2, waiting for transfers between devices, columns_home(): summed = lax.psum_scatter(cut, GROUP, scatter_dimension=0, tiled=True)  99.7 us
    dot_general x19, matrix products, mm(): return lax.dot_general(left, right, dims, preferred_element_type=f32)  99.6 us
    all_to_all x12, waiting for transfers between devices, swap(): return lax.all_to_all(array, axes, split_axis=0, concat_axis=0, tiled=True)  67.2 us
    all_gather x1, blocking collectives, body(): lax.all_gather(lax.ppermute(row_cut, ALL, to_turned), GROUP, axis=1, tile...  47.1 us
    all_to_all x12, starting transfers between devices, swap(): return lax.all_to_all(array, axes, split_axis=0, concat_axis=0, tiled=True)  44.5 us
    all_to_all x2, blocking collectives, swap(): return lax.all_to_all(array, axes, split_axis=0, concat_axis=0, tiled=True)  41.8 us
  transfers between devices with their start and end apart: 28, of which 17 were waited for; matrix products, arithmetic and copies ran while one was open for 19% of the time, Pallas kernels for 4%

profile of v1, /device:TPU:0, one launch (start us, length us, event | category | flops | bytes accessed | tf_op | source)
XLA Modules:
  0.0 981.7 jit_solution(11521274730362339627)
XLA Ops:
  22.2 22.8 %all_gather.25 = bf16[1024,384]{1,0:T(8,128)(2,1)S(1)} all-gather(bf16[256,384]{1,0:T(8,128)(2,1)S(1)} %bitcast.206), channel_id=1, replica_groups=mesh['head'=4,'blk'=8] {'head'}, dimensions={0}, use_global_device_ids=true | all-gather | bytes 983040 | tf_op jit(solution)/shard_map/all_gather | solution.py:338
  56.4 47.1 %all_gather.26 = bf16[3,128,1024]{2,1,0:T(8,128)(2,1)S(1)} all-gather(bf16[3,32,1024]{2,1,0:T(8,128)(2,1)S(1)} %collective-permute-done.2), channel_id=1, replica_groups=mesh['head'=4,'blk'=8] {'head'}, dimensions={1}, use_global_device_ids=true | all-gather | bytes 983040 | tf_op jit(solution)/shard_map/all_gather | solution.py:412
  111.3 29.7 %all_to_all.70 = bf16[8,128,1024]{2,1,0:T(8,128)(2,1)S(1)} all-to-all(bf16[8,128,1024]{2,1,0:T(8,128)(2,1)S(1)} %bitcast.189), channel_id=1, replica_groups=mesh['head'=4,'blk'=8] {'blk'}, dimensions={0} | all-to-all | bytes 4194304 | tf_op jit(solution)/shard_map/all_to_all | solution.py:334
  166.7 9.7 all-gather.9.cloned.1.call-done
  181.7 29.6 %all-gather.11.cloned.1.call-done = bf16[1024,640]{1,0:T(8,128)(2,1)} async-done(((bf16[256,640]{1,0:T(8,128)(2,1)}), bf16[1024,640]{1,0:T(8,128)(2,1)}) %all-gather.11.cloned.1.call-update) | async-done | bytes 1310736 | tf_op jit(solution)/shard_map/all_gather | solution.py:338
  216.9 11.1 %select_reduce_fusion.1 = f32[1024,32]{1,0:T(8,128)} fusion(f32[1024,256]{1,0:T(8,128)S(1)} %fusion.47, s32[1024,32]{1,0:T(8,128)S(1)} %bitcast.190), kind=kLoop, calls=%fused_computation.1 | loop fusion | flops 25133056 | bytes 1310720 | tf_op jit(solution)/shard_map/reduce_sum | solution.py:509
  267.8 25.6 %spread_weights.1 = bf16[4096,2048]{1,0:T(8,128)(2,1)} custom-call(s32[32,1,1024]{2,1,0:T(1,128)S(1)} %get-tuple-element.38.refs_0_, s32[32,1,1024]{2,1,0:T(1,128)S(1)} %get-tuple-element.37.refs_1_, s32[32,1,1024]{2,1,0:T(1,128)S(1)} %get-tuple-element.36.refs_2_, f32[32,1,1024]{2,1,0:T(1,128)S(1)} %convert_element_type.201.refs_3_), custom_call_target="tpu_custom_call" | custom-call | tf_op jit(solution)/shard_map/spread_weights/pallas_call | solution.py:283
  293.4 22.2 %convert_bitcast_fusion = bf16[512,8,8,128]{3,1,2,0:T(8,128)(2,1)} fusion(bf16[4096,2048]{1,0:T(8,128)(2,1)} %spread_weights.1, bf16[2048,1024]{1,0:T(8,128)(2,1)S(1)} %copy-done.1), kind=kOutput, calls=%fused_computation.4 | convolution fusion | flops 17184063488 | bytes 29360128 | tf_op jit(solution)/shard_map/dot_general | solution.py:33
  315.6 8.8 copy.195
  324.4 26.8 %copy.171 = bf16[4,8,1,128,8,128]{3,1,4,0,5,2:T(8,128)(2,1)} copy(bf16[4,8,1,128,8,128]{5,4,3,1,0,2:T(8,128)(2,1)} %bitcast.185) | data formatting | bytes 16777216 | tf_op jit(solution)/shard_map/reshape | solution.py:524
  351.2 13.3 %reshape.426 = bf16[32768,128]{0,1:T(8,128)(2,1)} reshape(bf16[4,1,8,8,128,128]{4,3,2,0,5,1:T(8,128)(2,1)} %bitcast.186) | data formatting | bytes 16777216 | tf_op jit(solution)/shard_map/reshape | solution.py:525
  370.1 140.0 %reduce-scatter.5.cloned.1.call-done = bf16[1024,128]{0,1:T(8,128)(2,1)} async-done(((bf16[32768,128]{0,1:T(8,128)(2,1)}), bf16[1024,128]{0,1:T(8,128)(2,1)}) %reduce-scatter.5.cloned.1.call-update) | async-done | bytes 262160 | tf_op jit(solution)/shard_map/reduce_scatter | solution.py:526
  513.6 73.7 %all-gather.15.cloned.1.call-done = bf16[32768,128]{0,1:T(8,128)(2,1)} async-done(((bf16[1024,128]{0,1:T(8,128)(2,1)}), bf16[32768,128]{0,1:T(8,128)(2,1)}) %all-gather.15.cloned.1.call-update) | async-done | bytes 8388624 | tf_op jit(solution)/shard_map/all_gather | solution.py:338
  587.3 9.3 copy.196
  596.6 24.6 %copy.172 = bf16[4,1,8,8,128,128]{5,2,4,3,0,1:T(8,128)(2,1)} copy(bf16[4,1,8,8,128,128]{4,3,2,0,5,1:T(8,128)(2,1)} %bitcast.187) | data formatting | bytes 16777216 | tf_op jit(solution)/shard_map/reshape | solution.py:501
  621.1 9.1 copy.207
  630.3 40.2 %row_dots.1 = f32[32,1,1024]{2,1,0:T(1,128)S(1)} custom-call(s32[32,1,1024]{2,1,0:T(1,128)S(1)} %get-tuple-element.38.refs_0_, s32[32,1,1024]{2,1,0:T(1,128)S(1)} %get-tuple-element.37.refs_1_, s32[32,1,1024]{2,1,0:T(1,128)S(1)} %get-tuple-element.36.refs_2_, bf16[4096,1024]{1,0:T(8,128)(2,1)} %bitcast.184, bf16[2048,1024]{1,0:T(8,128)(2,1)S(1)} %copy-done.2), custom_call_target="tpu_custom_call" | custom-call | tf_op jit(solution)/shard_map/row_dots/pallas_call | solution.py:316
  670.5 12.1 %all_to_all.71 = f32[32,1,1024]{2,1,0:T(1,128)S(1)} all-to-all(f32[32,1,1024]{2,1,0:T(1,128)S(1)} %row_dots.1), channel_id=1, replica_groups=mesh['head'=4,'blk'=8] {'head','blk'}, dimensions={0} | all-to-all | bytes 262144 | tf_op jit(solution)/shard_map/all_to_all | solution.py:334
  702.0 11.4 %select_reduce_fusion = bf16[1024,256]{1,0:T(8,128)(2,1)S(1)} fusion(f32[1024,32]{1,0:T(8,128)S(1)} %bitcast.194, s32[1024,32]{1,0:T(8,128)S(1)} %bitcast.191), kind=kLoop, calls=%fused_computation | loop fusion | flops 24903680 | bytes 786432 | tf_op jit(solution)/shard_map/reduce_sum | solution.py:545
  735.3 24.2 %all-to-all-done.10 = bf16[8,128,1024]{2,1,0:T(8,128)(2,1)} async-done(((bf16[8,128,1024]{2,1,0:T(8,128)(2,1)}), bf16[8,128,1024]{2,1,0:T(8,128)(2,1)}, u32[]{:S(2)}, u32[]{:S(2)}) %all-to-all-start.10) | async-done | bytes 2097184 | tf_op jit(solution)/shard_map/all_to_all | solution.py:334
  773.1 15.0 %all-gather.17.cloned.1.call-done = bf16[1024,1024]{1,0:T(8,128)(2,1)} async-done(((bf16[128,1024]{1,0:T(8,128)(2,1)}), bf16[1024,1024]{1,0:T(8,128)(2,1)}) %all-gather.17.cloned.1.call-update) | async-done | bytes 2097168 | tf_op jit(solution)/shard_map/all_gather | solution.py:338
  809.0 55.7 %reduce-scatter.11.cloned.1.call-done = f32[256,640]{1,0:T(8,128)} async-done(((f32[1024,640]{1,0:T(8,128)}), f32[256,640]{1,0:T(8,128)}) %reduce-scatter.11.cloned.1.call-update) | async-done | bytes 655376 | tf_op jit(solution)/shard_map/reduce_scatter | solution.py:575
  887.6 24.1 %fusion.88 = f32[2048,1024]{1,0:T(8,128)} fusion(bf16[4096,2048]{1,0:T(8,128)(2,1)} %spread_weights.1, bf16[512,8,8,128]{3,2,1,0:T(8,128)(2,1)} %bitcast.183), kind=kOutput, calls=%fused_computation.176 | convolution fusion | flops 17179869184 | bytes 33554432 | tf_op jit(solution)/shard_map/dot_general | solution.py:33
  917.2 43.9 %reduce-scatter.7.cloned.1.call-done = f32[256,384]{1,0:T(8,128)} async-done(((f32[1024,384]{1,0:T(8,128)}), f32[256,384]{1,0:T(8,128)}) %reduce-scatter.7.cloned.1.call-update) | async-done | bytes 393232 | tf_op jit(solution)/shard_map/reduce_scatter | solution.py:575
  (267 shorter events, 236.2 us)
Async XLA Ops:
  7.2 37.8 %all-gather.7.cloned.1.call-start = ((), (), s32[]{:S(2)}) async-start(), calls=%async_computation.18 | async-start | bytes 2359296 | tf_op jit(solution)/shard_map/all_gather | solution.py:338
  10.7 11.5 %all-to-all-start = ((bf16[8,32,384]{2,1,0:T(8,128)(2,1)}), bf16[8,32,384]{2,1,0:T(8,128)(2,1)S(1)}, u32[]{:S(2)}, u32[]{:S(2)}) async-start(bf16[8,32,384]{2,1,0:T(8,128)(2,1)} %reshape.412), calls=%async_computation | async-start | bytes 393216 | tf_op jit(solution)/shard_map/all_to_all | solution.py:334
  15.8 160.6 %all-gather.9.cloned.1.call-start = ((), (), s32[]{:S(2)}) async-start(), calls=%async_computation.19 | async-start | bytes 2359296 | tf_op jit(solution)/shard_map/all_gather | solution.py:338
  16.0 40.4 %collective-permute-start.2 = (bf16[3,32,1024]{2,1,0:T(8,128)(2,1)S(1)}, bf16[3,32,1024]{2,1,0:T(8,128)(2,1)S(1)}, u32[]{:S(2)}, u32[]{:S(2)}) collective-permute-start(bf16[3,32,1024]{2,1,0:T(8,128)(2,1)S(1)} %pad_maximum_fusion.11), channel_id=1, source_target_pairs={{0,0},{4,1},{8,2},{12,3},{16,4},{20,5},{24,6},{28,7},{1,8},{5,9},{... | collective-permute-start | bytes 589832 | tf_op jit(solution)/shard_map/ppermute | solution.py:412
  48.8 54.7 %collective-permute-start.1 = (bf16[1024,256]{1,0:T(8,128)(2,1)S(1)}, bf16[1024,256]{1,0:T(8,128)(2,1)S(1)}, u32[]{:S(2)}, u32[]{:S(2)}) collective-permute-start(bf16[1024,256]{1,0:T(8,128)(2,1)S(1)} %slice.97), channel_id=1, source_target_pairs={{0,8},{8,16},{16,24},{1,9},{9,17},{17,25},{2,10},{10,18},{18,26},{... | collective-permute-start | bytes 1572872 | tf_op jit(solution)/shard_map/ppermute | solution.py:475
  51.9 51.7 %collective-permute-start = (bf16[1024,256]{1,0:T(8,128)(2,1)S(1)}, bf16[1024,256]{1,0:T(8,128)(2,1)S(1)}, u32[]{:S(2)}, u32[]{:S(2)}) collective-permute-start(bf16[1024,256]{1,0:T(8,128)(2,1)S(1)} %slice.97), channel_id=1, source_target_pairs={{0,16},{8,24},{1,17},{9,25},{2,18},{10,26},{3,19},{11,27},{4,20},{... | collective-permute-start | bytes 1572872 | tf_op jit(solution)/shard_map/ppermute | solution.py:475
  155.2 11.2 %all-to-all-start.3 = ((s32[8,128,32]{1,2,0:T(8,128)}), s32[8,128,32]{1,2,0:T(8,128)S(1)}, u32[]{:S(2)}, u32[]{:S(2)}) async-start(s32[8,128,32]{1,2,0:T(8,128)} %bitcast.17), calls=%async_computation.3 | async-start | bytes 262144 | tf_op jit(solution)/shard_map/all_to_all | solution.py:334
  158.5 52.7 %all-gather.11.cloned.1.call-start = ((), (), s32[]{:S(2)}) async-start(), calls=%async_computation.20 | async-start | bytes 1638400 | tf_op jit(solution)/shard_map/all_gather | solution.py:338
  239.0 18.2 %all-to-all-start.2 = ((s32[32,3,1024]{2,1,0:T(4,128)}), s32[32,3,1024]{2,1,0:T(4,128)S(1)}, u32[]{:S(2)}, u32[]{:S(2)}) async-start(s32[32,3,1024]{2,1,0:T(4,128)} %copy.160), calls=%async_computation.2 | async-start | bytes 1048576 | tf_op jit(solution)/shard_map/all_to_all | solution.py:334
  241.6 123.1 %all-gather.13.cloned.1.call-start = ((), (), s32[]{:S(2)}) async-start(), calls=%async_computation.22 | async-start | bytes 2359296 | tf_op jit(solution)/shard_map/all_gather | solution.py:338
  260.2 249.9 %reduce-scatter.5.cloned.1.call-start = ((), (), s32[]{:S(2)}) async-start(), calls=%async_computation.21 | async-start | bytes 8650752 | tf_op jit(solution)/shard_map/reduce_scatter | solution.py:526
  364.5 222.7 %all-gather.15.cloned.1.call-start = ((), (), s32[]{:S(2)}) async-start(), calls=%async_computation.23 | async-start | bytes 8650752 | tf_op jit(solution)/shard_map/all_gather | solution.py:338
  697.3 31.1 %all-to-all-start.7 = ((bf16[8,128,1024]{2,1,0:T(8,128)(2,1)}), bf16[8,128,1024]{2,1,0:T(8,128)(2,1)}, u32[]{:S(2)}, u32[]{:S(2)}) async-start(bf16[8,128,1024]{2,1,0:T(8,128)(2,1)} %bitcast.196), calls=%async_computation.8 | async-start | bytes 4194304 | tf_op jit(solution)/shard_map/all_to_all | solution.py:334
  728.5 31.0 %all-to-all-start.10 = ((bf16[8,128,1024]{2,1,0:T(8,128)(2,1)}), bf16[8,128,1024]{2,1,0:T(8,128)(2,1)}, u32[]{:S(2)}, u32[]{:S(2)}) async-start(bf16[8,128,1024]{2,1,0:T(8,128)(2,1)} %bitcast.197), calls=%async_computation.11 | async-start | bytes 4194304 | tf_op jit(solution)/shard_map/all_to_all | solution.py:334
  732.8 55.3 %all-gather.17.cloned.1.call-start = ((), (), s32[]{:S(2)}) async-start(), calls=%async_computation.24 | async-start | bytes 2359296 | tf_op jit(solution)/shard_map/all_gather | solution.py:338
  763.0 101.8 %reduce-scatter.11.cloned.1.call-start = ((), (), s32[]{:S(2)}) async-start(), calls=%async_computation.27 | async-start | bytes 3276800 | tf_op jit(solution)/shard_map/reduce_scatter | solution.py:575
  768.3 147.2 %reduce-scatter.9.cloned.1.call-start = ((), (), s32[]{:S(2)}) async-start(), calls=%async_computation.26 | async-start | bytes 1966080 | tf_op jit(solution)/shard_map/reduce_scatter | solution.py:580
  806.4 62.3 %collective-permute-start.3 = (bf16[1024,256]{1,0:T(8,128)(2,1)}, bf16[1024,256]{1,0:T(8,128)(2,1)S(1)}, u32[]{:S(2)}, u32[]{:S(2)}) collective-permute-start(bf16[1024,256]{1,0:T(8,128)(2,1)} %get-tuple-element.31), channel_id=1, source_target_pairs={{8,0},{16,8},{24,16},{9,1},{17,9},{25,17},{10,2},{18,10},{26,18},{... | collective-permute-start | bytes 1572872 | tf_op jit(solution)/shard_map/ppermute | solution.py:564
  807.7 67.5 %collective-permute-start.4 = (bf16[1024,256]{1,0:T(8,128)(2,1)}, bf16[1024,256]{1,0:T(8,128)(2,1)S(1)}, u32[]{:S(2)}, u32[]{:S(2)}) collective-permute-start(bf16[1024,256]{1,0:T(8,128)(2,1)} %get-tuple-element.32), channel_id=1, source_target_pairs={{16,0},{24,8},{17,1},{25,9},{18,2},{26,10},{19,3},{27,11},{20,4},{... | collective-permute-start | bytes 1572872 | tf_op jit(solution)/shard_map/ppermute | solution.py:564
  864.7 19.0 %all-to-all-start.13 = ((f32[8,32,640]{2,1,0:T(8,128)}), f32[8,32,640]{2,1,0:T(8,128)S(1)}, u32[]{:S(2)}, u32[]{:S(2)}) async-start(f32[8,32,640]{2,1,0:T(8,128)} %bitcast.207), calls=%async_computation.17 | async-start | bytes 1310720 | tf_op jit(solution)/shard_map/all_to_all | solution.py:334
  868.4 92.7 %reduce-scatter.7.cloned.1.call-start = ((), (), s32[]{:S(2)}) async-start(), calls=%async_computation.25 | async-start | bytes 1966080 | tf_op jit(solution)/shard_map/reduce_scatter | solution.py:575
  883.8 31.2 %all-to-all-start.11 = ((bf16[8,128,1024]{2,1,0:T(8,128)(2,1)}), bf16[8,128,1024]{2,1,0:T(8,128)(2,1)S(1)}, u32[]{:S(2)}, u32[]{:S(2)}) async-start(bf16[8,128,1024]{2,1,0:T(8,128)(2,1)} %bitcast.195), calls=%async_computation.12 | async-start | bytes 4194304 | tf_op jit(solution)/shard_map/all_to_all | solution.py:334
  915.5 51.2 %collective-permute-start.5 = (f32[32,3,1024]{2,0,1:T(8,128)}, f32[32,3,1024]{2,0,1:T(8,128)S(1)}, u32[]{:S(2)}, u32[]{:S(2)}) collective-permute-start(f32[32,3,1024]{2,0,1:T(8,128)} %reduce-scatter.9.cloned.1.call-done), channel_id=1, source_target_pairs={{0,0},{1,4},{2,8},{3,12},{4,16},{5,20},{6,24},{7,28},{8,1},{9,5},{... | collective-permute-start | bytes 1179656 | tf_op jit(solution)/shard_map/ppermute | solution.py:579
  961.1 11.9 %all-to-all-start.12 = ((f32[8,32,384]{2,1,0:T(8,128)}), f32[8,32,384]{2,1,0:T(8,128)S(1)}, u32[]{:S(2)}, u32[]{:S(2)}) async-start(f32[8,32,384]{2,1,0:T(8,128)} %bitcast.211), calls=%async_computation.14 | async-start | bytes 786432 | tf_op jit(solution)/shard_map/all_to_all | solution.py:334
  (42 other events, 454.5 us)
Sparse Core Ops, SparseCore 0:
  9.9 34.2 all-gather.6
  143.1 33.2 all-gather.8
  178.5 32.6 all-gather.10
  244.1 29.3 all-gather.12
  364.7 145.4 reduce-scatter.4
  513.7 73.5 all-gather.14
  763.1 24.9 all-gather.16
  790.4 74.2 reduce-scatter.10
  867.0 34.9 reduce-scatter.8
  904.2 56.8 reduce-scatter.6

commit v2 on v1

v2 whole, which is shorter than its diff:
```python
import math

import jax
import jax.numpy as jnp
from jax import lax
from jax.experimental import pallas as pl
from jax.experimental.pallas import tpu as pltpu
from jax.sharding import Mesh
from jax.sharding import PartitionSpec as P

NH = 16
HD = 64
MH = 4
QHALF = 512
NSUB = 256
KPICK = 32
TP = 2 * MH

GROUP = ("head", "outer")
BLK = ("outer", "tp")
ALL = ("head", "outer", "tp")

epsilon = 1e-06
neg_big = -1e30
LANES = 128
bf16 = jnp.bfloat16
f32 = jnp.float32
NN = (((1,), (0,)), ((), ()))
NT = (((1,), (1,)), ((), ()))
TN = (((0,), (0,)), ((), ()))


def mm(left, right, dims=NN):
    return lax.dot_general(left, right, dims, preferred_element_type=f32)


def params(mib):
    return pltpu.CompilerParams(vmem_limit_bytes=mib * 1024 * 1024)


def lasting(microseconds):
    return pl.CostEstimate(
        flops=0, bytes_accessed=int(microseconds * 3.5e6), transcendentals=0
    )


def head_rows(pair):
    lane = lax.broadcasted_iota(jnp.int32, pair.shape, 1)
    zero = jnp.zeros_like(pair)
    return (jnp.where(lane < HD, pair, zero), jnp.where(lane < HD, zero, pair))


def turned_block(step, here, block, rows):
    return jnp.bitwise_xor(step, here * rows // block)


def turned_iota(shape, axis, here, rows):
    place = lax.broadcasted_iota(jnp.int32, shape, axis)
    return jnp.bitwise_xor(place, lax.rem(here * rows, shape[axis]))


def key_blocks(step, base, block_q, block_k, low_first_ref):
    return (
        low_first_ref[step] // block_k,
        (base + (step + 1) * block_q - 1) // block_k + 1,
    )


def key_start(turn, span, here, block_k, rows):
    per_group = span // block_k
    group = turn // per_group
    within = turned_block(lax.rem(turn, per_group), here, block_k, rows)
    return pl.multiple_of(group * span + within * block_k, block_k)


def attn_fwd_kernel(
    base, span, rows, block_k, low_first_ref, here_ref, q_ref, kv_ref, low_ref, att_ref, lse_ref, out_ref
):
    block_q = q_ref.shape[0]
    step = pl.program_id(0)
    here = here_ref[0]
    first, stop = key_blocks(step, base, block_q, block_k, low_first_ref)
    queries = head_rows(q_ref[...])
    low = low_ref[...]
    high = base + step * block_q + turned_iota((1, block_q), 1, here, rows)
    inner = turned_iota((block_k, block_q), 0, here, rows)

    def visit(turn, carried):
        start = key_start(turn, span, here, block_k, rows)
        keys = kv_ref[pl.ds(start, block_k), :LANES]
        values = kv_ref[pl.ds(start, block_k), LANES:]
        place = turn * block_k + inner
        allowed = (place >= low) & (place <= high)
        out = []
        for head in range(2):
            run_max, run_sum, run_acc = carried[head]
            scores = jnp.where(allowed, mm(keys, queries[head], NT), neg_big)
            new_max = jnp.maximum(run_max, jnp.max(scores, axis=0, keepdims=True))
            powers = jnp.exp(scores - new_max)
            rescale = jnp.exp(run_max - new_max)
            run_sum = run_sum * rescale + jnp.sum(powers, axis=0, keepdims=True)
            run_acc = run_acc * rescale + mm(values, powers.astype(bf16), TN)
            out.append((new_max, run_sum, run_acc))
        return tuple(out)

    fresh = (
        jnp.full((1, block_q), neg_big, f32),
        jnp.zeros((1, block_q), f32),
        jnp.zeros((LANES, block_q), f32),
    )
    done = lax.fori_loop(first, stop, visit, (fresh, fresh))
    att_ref[:HD, :] = done[0][2][:HD] / done[0][1]
    att_ref[HD:, :] = done[1][2][HD:] / done[1][1]
    out_ref[...] = jnp.transpose(att_ref[...]).astype(bf16)
    lse_ref[0:1, :] = done[0][0] + jnp.log(done[0][1])
    lse_ref[1:2, :] = done[1][0] + jnp.log(done[1][1])


def attn_specs(block_q, rows, span):
    def turn(i, here):
        return turned_block(i, here[0], block_q, rows)

    return (
        pl.BlockSpec((block_q, LANES), lambda i, s, here: (turn(i, here), 0)),
        pl.BlockSpec((1, block_q), lambda i, s, here: (0, turn(i, here))),
        pl.BlockSpec((2, block_q), lambda i, s, here: (0, turn(i, here))),
        pl.BlockSpec((LANES, block_q), lambda i, s, here: (0, turn(i, here))),
    )


def attn_fwd(base, rows, low_first, here, low, queries, keys_values):
    span = queries.shape[0]
    block_q, block_k = 256, 512
    by_row, one_lane, two_lane, by_lane = attn_specs(block_q, rows, span)
    return pl.pallas_call(
        lambda *refs: attn_fwd_kernel(base, span, rows, block_k, *refs),
        grid_spec=pltpu.PrefetchScalarGridSpec(
            num_scalar_prefetch=2,
            grid=(span // block_q,),
            in_specs=[
                by_row,
                pl.BlockSpec(keys_values.shape, lambda i, s, here: (0, 0)),
                one_lane,
            ],
            out_specs=[by_lane, two_lane, by_row],
        ),
        out_shape=[
            jax.ShapeDtypeStruct((LANES, span), f32),
            jax.ShapeDtypeStruct((2, span), f32),
            jax.ShapeDtypeStruct((span, LANES), bf16),
        ],
        compiler_params=params(32),
        cost_estimate=lasting(keys_values.shape[0] / 250),
        name="attn_fwd",
    )(low_first[::block_q], here, queries, keys_values, low[None, :])


def attn_bwd_kernel(
    base,
    span,
    rows,
    block_k,
    low_first_ref,
    here_ref,
    q_ref,
    kv_ref,
    low_ref,
    lse_ref,
    att_ref,
    grad_ref,
    dq_ref,
    *refs,
):
    dk_ref, dv_ref = refs[-2:]
    block_q = q_ref.shape[0]
    step = pl.program_id(0)
    here = here_ref[0]
    first, stop = key_blocks(step, base, block_q, block_k, low_first_ref)

    @pl.when(step == 0)
    def clear():
        dk_ref[...] = jnp.zeros_like(dk_ref)
        dv_ref[...] = jnp.zeros_like(dv_ref)

    queries = head_rows(q_ref[...])
    grads = head_rows(grad_ref[...])
    grad_turned = jnp.transpose(grad_ref[...].astype(f32)) * att_ref[...]
    deltas = (
        jnp.sum(grad_turned[:HD], axis=0, keepdims=True),
        jnp.sum(grad_turned[HD:], axis=0, keepdims=True),
    )
    low = low_ref[...]
    high = base + step * block_q + turned_iota((1, block_q), 1, here, rows)
    inner = turned_iota((block_k, block_q), 0, here, rows)

    def visit(turn, carried):
        start = key_start(turn, span, here, block_k, rows)
        keys = kv_ref[pl.ds(start, block_k), :LANES]
        values = kv_ref[pl.ds(start, block_k), LANES:]
        place = turn * block_k + inner
        allowed = (place >= low) & (place <= high)
        out = []
        grad_key = dk_ref[pl.ds(start, block_k), :]
        grad_value = dv_ref[pl.ds(start, block_k), :]
        for head in range(2):
            scores = mm(keys, queries[head], NT)
            probs = jnp.where(allowed, jnp.exp(scores - lse_ref[head : head + 1, :]), 0.0)
            grad_probs = mm(values, grads[head], NT)
            grad_scores = (probs * (grad_probs - deltas[head])).astype(bf16)
            grad_key = grad_key + mm(grad_scores, queries[head])
            grad_value = grad_value + mm(probs.astype(bf16), grads[head])
            out.append(carried[head] + mm(keys, grad_scores, TN))
        dk_ref[pl.ds(start, block_k), :] = grad_key
        dv_ref[pl.ds(start, block_k), :] = grad_value
        return tuple(out)

    fresh = jnp.zeros((LANES, block_q), f32)
    done = lax.fori_loop(first, stop, visit, (fresh, fresh))
    turned = jnp.concatenate([done[0][:HD], done[1][HD:]], axis=0) * (1.0 / math.sqrt(HD))
    dq_ref[...] = jnp.transpose(turned).astype(bf16)

    @pl.when(step == span // block_q - 1)
    def leave():
        for turn, out_ref in enumerate(refs[:-2]):
            out_ref[:, :LANES] = dk_ref[turn * span : (turn + 1) * span, :].astype(bf16)
            out_ref[:, LANES:] = dv_ref[turn * span : (turn + 1) * span, :].astype(bf16)


def attn_bwd(base, rows, low_first, here, low, queries, keys_values, lse, att, grads):
    span = queries.shape[0]
    block_q, block_k = 256, 512
    reach = keys_values.shape[0]
    by_row, one_lane, two_lane, by_lane = attn_specs(block_q, rows, span)
    return pl.pallas_call(
        lambda *refs: attn_bwd_kernel(base, span, rows, block_k, *refs),
        grid_spec=pltpu.PrefetchScalarGridSpec(
            num_scalar_prefetch=2,
            grid=(span // block_q,),
            in_specs=[
                by_row,
                pl.BlockSpec(keys_values.shape, lambda i, s, here: (0, 0)),
                one_lane,
                two_lane,
                by_lane,
                by_row,
            ],
            out_specs=[by_row]
            + [pl.BlockSpec((span, 2 * LANES), lambda i, s, here: (0, 0))] * (reach // span),
            scratch_shapes=[pltpu.VMEM((reach, LANES), f32), pltpu.VMEM((reach, LANES), f32)],
        ),
        out_shape=[jax.ShapeDtypeStruct((span, LANES), bf16)]
        + [jax.ShapeDtypeStruct((span, 2 * LANES), bf16)] * (reach // span),
        compiler_params=params(48),
        cost_estimate=lasting(keys_values.shape[0] / 200),
        name="attn_bwd",
    )(low_first[::block_q], here, queries, keys_values, low[None, :], lse, att, grads)


def hits(count, row):
    return lax.broadcasted_iota(jnp.int32, (count, row.shape[1]), 0) == row


def one_hot(count, row):
    return jnp.where(hits(count, row), 1.0, 0.0).astype(bf16)


def wide_hits(count, ref, top, rows):
    return [hits(count, ref[row : row + 1, :]) for row in range(top, top + rows)]


def bucket_rows(high_ref, low_ref, load_refs, places):
    batch = 8
    total = jnp.zeros((places, len(load_refs) * LANES), f32)
    for top in range(0, high_ref.shape[0], batch):
        high = [
            jnp.where(hit, 1.0, 0.0).astype(bf16) for hit in wide_hits(places, high_ref, top, batch)
        ]
        low = wide_hits(LANES, low_ref, top, batch)
        parts = [
            jnp.concatenate(
                [
                    jnp.where(low[row], load_ref[top + row : top + row + 1, :], 0.0).astype(bf16)
                    for row in range(batch)
                ],
                axis=1,
            )
            for load_ref in load_refs
        ]
        total = total + mm(jnp.concatenate(high, axis=1), jnp.concatenate(parts, axis=0), NT)
    return total


def entries_kernel(high_ref, low_ref, first_ref, second_ref, out_ref, token_ref):
    token_ref[...] = lax.broadcasted_iota(jnp.int32, token_ref.shape, 0).astype(f32)
    loads = (token_ref, first_ref, second_ref)
    out_ref[...] = bucket_rows(high_ref, low_ref, loads, out_ref.shape[0]).astype(bf16)


def make_entries(high, low, first, second, places):
    return pl.pallas_call(
        entries_kernel,
        out_shape=jax.ShapeDtypeStruct((places // LANES, 3 * LANES), bf16),
        scratch_shapes=[pltpu.VMEM(high.shape, f32)],
        compiler_params=params(32),
        cost_estimate=lasting(5),
        name="make_entries",
    )(high, low, first.astype(f32), second.astype(f32))


def weights_kernel(picked_ref, high_ref, low_ref, weight_ref, out_ref):
    parts = []
    for head in range(MH):
        picked = picked_ref[2 * head] + picked_ref[2 * head + 1]
        powers = jnp.exp(picked - jnp.max(picked, axis=0, keepdims=True))
        parts.append(powers / jnp.sum(powers, axis=0, keepdims=True))
    weight_ref[...] = jnp.transpose(jnp.concatenate(parts, axis=0))
    out_ref[...] = bucket_rows(high_ref, low_ref, (weight_ref,), out_ref.shape[0]).astype(bf16)


def make_weights(picked, high, low, places):
    return pl.pallas_call(
        weights_kernel,
        out_shape=[
            jax.ShapeDtypeStruct(high.shape, f32),
            jax.ShapeDtypeStruct((places // LANES, LANES), bf16),
        ],
        compiler_params=params(32),
        cost_estimate=lasting(3),
        name="make_weights",
    )(picked, high, low)


def grads_kernel(high_ref, low_ref, weight_ref, table_ref, out_ref, found_ref):
    turned = jnp.transpose(table_ref[...])
    main = turned.astype(bf16)
    rest = (turned - main.astype(f32)).astype(bf16)
    batch = 8
    for top in range(0, high_ref.shape[0], batch):
        high = jnp.concatenate(
            [
                jnp.where(hit, 1.0, 0.0).astype(bf16)
                for hit in wide_hits(table_ref.shape[0], high_ref, top, batch)
            ],
            axis=1,
        )
        found = mm(main, high) + mm(rest, high)
        low = jnp.concatenate(wide_hits(LANES, low_ref, top, batch), axis=1)
        line = jnp.sum(jnp.where(low, found, 0.0), axis=0, keepdims=True)
        for row in range(batch):
            found_ref[top + row : top + row + 1, :] = line[:, row * LANES : (row + 1) * LANES]
    grads = jnp.transpose(found_ref[...])
    weights = jnp.transpose(weight_ref[...])
    for head in range(MH):
        rows = slice(head * KPICK, (head + 1) * KPICK)
        coupled = jnp.sum(weights[rows] * grads[rows], axis=0, keepdims=True)
        out_ref[rows, :] = weights[rows] * (grads[rows] - coupled)


def pick_grads(high, low, weights, table):
    return pl.pallas_call(
        grads_kernel,
        out_shape=jax.ShapeDtypeStruct((high.shape[1], high.shape[0]), f32),
        scratch_shapes=[pltpu.VMEM(high.shape, f32)],
        compiler_params=params(32),
        cost_estimate=lasting(5),
        name="pick_grads",
    )(high, low, weights, table)


def place_rows(rows, subs, token_row, first_row):
    tokens = one_hot(rows, token_row)
    return jnp.concatenate(
        [tokens * jnp.where(first_row == first, 1.0, 0.0).astype(bf16) for first in range(subs)],
        axis=0,
    )


def spread_kernel(
    rows, subs, outer, here_ref, token_ref, first_ref, second_ref, weight_ref, value_ref, *refs
):
    table_ref, keep_ref, send_ref = refs[-3:]
    count = token_ref.shape[1]
    fold = rows // outer
    for block in range(count):
        left = place_rows(rows, subs, token_ref[0, block], first_ref[0, block])
        right = jnp.where(hits(NSUB, second_ref[0, block]), weight_ref[0, block], 0.0).astype(bf16)
        table = mm(left, right, NT).astype(bf16)
        for first in range(subs):
            table_ref[0, block * rows : (block + 1) * rows, first * NSUB : (first + 1) * NSUB] = (
                table[first * rows : (first + 1) * rows]
            )
    partial = mm(table_ref[0], value_ref[...]).astype(bf16)
    here = here_ref[0]
    chip = here // 2

    def store(core):
        for there in range(TP):
            target_ref = keep_ref if there % 2 == core else send_ref
            place = jnp.bitwise_xor(chip, there // 2)
            for block in range(count):
                for part in range(outer):
                    top = block * rows + part * fold
                    target_ref[place, 0, part, block] = partial[
                        top : top + fold, there * LANES : (there + 1) * LANES
                    ]

    pl.when(here % 2 == 0)(lambda: store(0))
    pl.when(here % 2 == 1)(lambda: store(1))


def spread_weights(
    rows, subs, heads, outer, turn, turns, here, token, first, second, weight, values, table
):
    blocks, capacity = token.shape[1], token.shape[3]
    width = values.shape[1]
    count = 2
    steps = blocks // turns // count
    fold = rows // outer
    row = pl.BlockSpec((1, count, 1, capacity), lambda h, i, s: (h, turn * steps + i, 0, 0))
    piece = pl.BlockSpec(
        (TP // 2, 1, outer, count, fold, LANES), lambda h, i, s: (0, h, 0, i, 0, 0)
    )
    piece_shape = jax.ShapeDtypeStruct(
        (TP // 2, heads, outer, blocks // turns, fold, LANES), bf16
    )
    operands = [here, token, first, second, weight, values]
    in_specs = [row, row, row, row, pl.BlockSpec(values.shape, lambda h, i, s: (0, 0))]
    aliases = {}
    if table is not None:
        operands.append(table)
        in_specs.append(pl.BlockSpec(memory_space=pl.ANY))
        aliases = {6: 0}
    return pl.pallas_call(
        lambda *refs: spread_kernel(rows, subs, outer, *refs),
        grid_spec=pltpu.PrefetchScalarGridSpec(
            num_scalar_prefetch=1,
            grid=(heads, steps),
            in_specs=in_specs,
            out_specs=[
                pl.BlockSpec(
                    (1, count * rows, subs * NSUB), lambda h, i, s: (h, turn * steps + i, 0)
                ),
                piece,
                piece,
            ],
        ),
        out_shape=[
            jax.ShapeDtypeStruct((heads, blocks * rows, subs * NSUB), bf16),
            piece_shape,
            piece_shape,
        ],
        input_output_aliases=aliases,
        compiler_params=params(48),
        cost_estimate=lasting(heads * blocks // turns * rows / 90),
        name="spread_weights",
    )(*operands)


def dots_kernel(
    rows, subs, outer, token_ref, first_ref, second_ref, grad_ref, value_ref, *refs
):
    out_ref, dense_ref = refs[-2:]
    count = token_ref.shape[1]
    fold = rows // outer
    for block in range(count):
        for part in range(outer):
            top = block * rows + part * fold
            for there in range(TP):
                dense_ref[0, top : top + fold, there * LANES : (there + 1) * LANES] = grad_ref[
                    0, part, there, block
                ]
    dense = dense_ref[0]
    found = [
        mm(value_ref[first * NSUB : (first + 1) * NSUB, :], dense, NT).astype(bf16)
        for first in range(subs)
    ]
    for block in range(count):
        left = place_rows(rows, subs, token_ref[0, block], first_ref[0, block])
        table = jnp.concatenate(
            [
                found[first][:, block * rows : (block + 1) * rows] for first in range(subs)
            ],
            axis=1,
        )
        spread = mm(table, left)
        out_ref[0, block] = jnp.sum(
            jnp.where(hits(NSUB, second_ref[0, block]), spread, 0.0), axis=0, keepdims=True
        )


def row_dots(rows, subs, head, outer, token, first, second, grads, values, dense):
    heads, blocks, capacity = token.shape[0], token.shape[1], token.shape[3]
    width = values.shape[1]
    count = 2
    fold = rows // outer
    row = pl.BlockSpec((1, count, 1, capacity), lambda i: (head, i, 0, 0))
    operands = [token, first, second, grads, values]
    in_specs = [
        row,
        row,
        row,
        pl.BlockSpec((1, outer, TP, count, fold, LANES), lambda i: (head, 0, 0, i, 0, 0)),
        pl.BlockSpec(values.shape, lambda i: (0, 0)),
    ]
    aliases = {}
    if dense is not None:
        operands.append(dense)
        in_specs.append(pl.BlockSpec(memory_space=pl.ANY))
        aliases = {5: 1}
    return pl.pallas_call(
        lambda *refs: dots_kernel(rows, subs, outer, *refs),
        grid=(blocks // count,),
        in_specs=in_specs,
        out_specs=[
            pl.BlockSpec((1, count, 1, capacity), lambda i: (0, i, 0, 0)),
            pl.BlockSpec((1, count * rows, width), lambda i: (head, i, 0)),
        ],
        out_shape=[
            jax.ShapeDtypeStruct((1, blocks, 1, capacity), f32),
            jax.ShapeDtypeStruct((heads, blocks * rows, width), bf16),
        ],
        input_output_aliases=aliases,
        compiler_params=params(48),
        cost_estimate=lasting(blocks * rows / 90),
        name="row_dots",
    )(*operands)


def value_grads_kernel(table_ref, dense_ref, *refs):
    out_ref = refs[-1]
    out_ref[...] = mm(table_ref[...], dense_ref[...], TN)


def value_grads(turn, turns, table, dense, sums):
    tokens, own_rows = table.shape
    width = dense.shape[1]
    block = min(512, own_rows // turns)
    steps = own_rows // turns // block
    operands = [table, dense]
    in_specs = [
        pl.BlockSpec((tokens, block), lambda i: (0, turn * steps + i)),
        pl.BlockSpec(dense.shape, lambda i: (0, 0)),
    ]
    aliases = {}
    if sums is not None:
        operands.append(sums)
        in_specs.append(pl.BlockSpec(memory_space=pl.ANY))
        aliases = {2: 0}
    return pl.pallas_call(
        value_grads_kernel,
        grid=(steps,),
        in_specs=in_specs,
        out_specs=pl.BlockSpec((block, width), lambda i: (turn * steps + i, 0)),
        out_shape=jax.ShapeDtypeStruct((own_rows, width), f32),
        input_output_aliases=aliases,
        compiler_params=params(56),
        cost_estimate=lasting(15 * 2 / turns),
        name="value_grads",
    )(*operands)


def pick_kernel(query_ref, table_ref, index_ref, out_ref):
    scores = mm(query_ref[...], table_ref[...], NT)
    index = index_ref[...]
    place = jnp.bitwise_and(index, LANES - 1)
    low = jnp.take_along_axis(scores[:, :LANES], place, axis=1)
    high = jnp.take_along_axis(scores[:, LANES:], place, axis=1)
    out_ref[...] = jnp.transpose(jnp.where(index < LANES, low, high))[:KPICK]


def pick_scores(query, table, index):
    rows = query.shape[0]
    block = 256
    return pl.pallas_call(
        pick_kernel,
        grid=(rows // block,),
        in_specs=[
            pl.BlockSpec((block, QHALF), lambda i: (i, 0)),
            pl.BlockSpec((NSUB, QHALF), lambda i: (0, 0)),
            pl.BlockSpec((block, LANES), lambda i: (i, 0)),
        ],
        out_specs=pl.BlockSpec((KPICK, block), lambda i: (0, i)),
        out_shape=jax.ShapeDtypeStruct((KPICK, rows), f32),
        compiler_params=params(32),
        cost_estimate=lasting(rows / 600),
        name="pick_scores",
    )(query, table, index)


def unpick_kernel(grad_ref, index_ref, table_ref, sub_ref, query_ref):
    count = grad_ref.shape[1]
    place = lax.broadcasted_iota(jnp.int32, (NSUB, count), 0)
    total = jnp.zeros((NSUB, count), f32)
    for pick in range(KPICK):
        hit = place == index_ref[pick : pick + 1, :]
        total = total + jnp.where(hit, grad_ref[pick : pick + 1, :], 0.0)
    low = total.astype(bf16)
    sub_ref[...] = low
    query_ref[...] = mm(low, table_ref[...], TN).astype(bf16)


def unpick_scores(grads, index, table):
    rows = grads.shape[1]
    block = 256
    return pl.pallas_call(
        unpick_kernel,
        grid=(rows // block,),
        in_specs=[
            pl.BlockSpec((KPICK, block), lambda i: (0, i)),
            pl.BlockSpec((KPICK, block), lambda i: (0, i)),
            pl.BlockSpec((NSUB, QHALF), lambda i: (0, 0)),
        ],
        out_specs=[
            pl.BlockSpec((NSUB, block), lambda i: (0, i)),
            pl.BlockSpec((block, QHALF), lambda i: (i, 0)),
        ],
        out_shape=[
            jax.ShapeDtypeStruct((NSUB, rows), bf16),
            jax.ShapeDtypeStruct((rows, QHALF), bf16),
        ],
        compiler_params=params(32),
        cost_estimate=lasting(rows / 180),
        name="unpick_scores",
    )(grads, index, table)


def swap(array, axes):
    return lax.all_to_all(array, axes, split_axis=0, concat_axis=0, tiled=True)


def gather(array, axes):
    return lax.all_gather(array, axes, axis=0, tiled=True)


def across(array, distance):
    return lax.ppermute(array, "tp", [(at, at ^ distance) for at in range(TP)])


def onward(array, count, step):
    pairs = [(at, at + step) for at in range(count) if 0 <= at + step < count]
    return lax.ppermute(array, GROUP, pairs)


def gather_tp(own):
    half = own.shape[0] // 2
    near = across(own, 2)
    next_one = across(own, 4)
    far = jnp.concatenate([across(near[:half], 4), across(next_one[half:], 2)])
    quad = jnp.stack([own, near, next_one, far])
    both = jnp.stack([quad, across(quad, 1)], axis=1)
    return both.reshape((TP * own.shape[0],) + own.shape[1:])


def halves(array):
    blocks = array.reshape((TP // 2, 2, -1) + array.shape[1:])
    return tuple(blocks[:, core].reshape((-1,) + array.shape[1:]) for core in range(2))


def sum_back_start(left, right, dims, rows):
    keep_left, send_left = halves(left)
    met = across(mm(send_left, right, dims).astype(bf16), 1)
    return mm(keep_left, right, dims).reshape(4, rows, -1), met.reshape(4, rows, -1)


def first_hop(keep, met):
    half = keep.shape[1] // 2
    sums = keep + met.astype(f32)
    stay = (sums[0::2, :half], sums[:2, half:])
    got = (across(sums[1::2, :half].astype(bf16), 2), across(sums[2:, half:].astype(bf16), 4))
    return stay, got


def second_hop(stay, got):
    sums = (stay[0] + got[0].astype(f32), stay[1] + got[1].astype(f32))
    got = (across(sums[0][1].astype(bf16), 4), across(sums[1][1].astype(bf16), 2))
    return (sums[0][0], sums[1][0]), got


def last_hop(stay, got):
    return jnp.concatenate(
        [stay[0] + got[0].astype(f32), stay[1] + got[1].astype(f32)], axis=0
    )


def sum_back(left, right, dims, rows):
    return last_hop(*second_hop(*first_hop(*sum_back_start(left, right, dims, rows))))


def chip_sums(keep_ref, met_ref, chip, half):
    size = keep_ref.shape[2] // 2
    rows = slice(half * size, (half + 1) * size)
    return keep_ref[chip, 0, rows].astype(f32) + met_ref[chip, 0, rows].astype(f32)


def leave_kernel(keep_ref, met_ref, along_ref, aside_ref):
    for turn in range(2):
        along_ref[turn, 0] = chip_sums(keep_ref, met_ref, 2 * turn + 1, 0).astype(bf16)
        aside_ref[turn, 0] = chip_sums(keep_ref, met_ref, 2 + turn, 1).astype(bf16)


def pass_kernel(keep_ref, met_ref, along_ref, aside_ref, out_along_ref, out_aside_ref):
    along = chip_sums(keep_ref, met_ref, 2, 0) + along_ref[1, 0].astype(f32)
    aside = chip_sums(keep_ref, met_ref, 1, 1) + aside_ref[1, 0].astype(f32)
    out_along_ref[0] = along.astype(bf16)
    out_aside_ref[0] = aside.astype(bf16)


def total_kernel(keep_ref, met_ref, along_ref, aside_ref, far_ref, side_ref, out_ref):
    size = keep_ref.shape[2] // 2
    along = chip_sums(keep_ref, met_ref, 0, 0) + along_ref[0, 0].astype(f32)
    aside = chip_sums(keep_ref, met_ref, 0, 1) + aside_ref[0, 0].astype(f32)
    out_ref[0, :size] = (along + far_ref[0].astype(f32)).astype(bf16)
    out_ref[0, size:] = (aside + side_ref[0].astype(f32)).astype(bf16)


def hop_call(kernel, name, keep, outs, *operands):
    groups, rows = keep.shape[1:3]
    four = pl.BlockSpec((4, 1, rows, LANES), lambda i: (0, i, 0, 0))
    two = pl.BlockSpec((2, 1, rows // 2, LANES), lambda i: (0, i, 0, 0))
    one = pl.BlockSpec((1, rows // 2, LANES), lambda i: (i, 0, 0))
    whole = pl.BlockSpec((1, rows, LANES), lambda i: (i, 0, 0))
    specs = {"two": two, "one": one, "whole": whole}
    shapes = {
        "two": (2, groups, rows // 2, LANES),
        "one": (groups, rows // 2, LANES),
        "whole": (groups, rows, LANES),
    }
    return pl.pallas_call(
        kernel,
        grid=(groups,),
        in_specs=[four, four, two, two, one, one][: len(operands) + 1],
        out_specs=[specs[out] for out in outs],
        out_shape=[jax.ShapeDtypeStruct(shapes[out], bf16) for out in outs],
        compiler_params=params(32),
        cost_estimate=lasting(keep.size / 5e5),
        name=name,
    )(keep, *operands)


def sum_groups_start(total, groups, group_index):
    parts = [lax.dynamic_index_in_dim(total, group_index, 0, keepdims=False)]
    low = total.astype(bf16)
    for away in range(1, groups):
        piece = lax.dynamic_index_in_dim(
            low, lax.rem(group_index + away, groups), 0, keepdims=False
        )
        pairs = [(at, (at + away) % groups) for at in range(groups)]
        parts.append(lax.ppermute(piece, GROUP, pairs))
    return parts


def sum_groups(total, groups, group_index):
    return sum(part.astype(f32) for part in sum_groups_start(total, groups, group_index))


def shift(own, groups, away):
    return lax.ppermute(own, GROUP, [(at, (at + away) % groups) for at in range(groups)])


def by_group(own, shifts, groups, group_index):
    result = jnp.zeros((groups,) + own.shape, own.dtype)
    result = lax.dynamic_update_index_in_dim(result, own, group_index, 0)
    for away, piece in shifts.items():
        source = lax.rem(group_index + groups - away, groups)
        result = lax.dynamic_update_index_in_dim(result, piece, source, 0)
    return result


def tie(*arrays):
    return lax.optimization_barrier(arrays)


def norm_scale(hidden):
    return lax.rsqrt(jnp.mean(hidden * hidden, axis=-1, keepdims=True) + epsilon)


def norm_back(hidden, scale, weighted):
    coupled = jnp.mean(hidden * weighted, axis=-1, keepdims=True)
    return scale * weighted - hidden * (scale * scale * scale) * coupled


def body(
    inputs,
    attn_gain,
    attn_qkv,
    attn_out,
    memory_gain,
    memory_query,
    sub_keys,
    memory_gate,
    memory_out,
    memory_values,
    doc_lengths,
    token_order,
    memory_picks,
    cotangent,
):
    rows, width = inputs.shape
    outer = lax.axis_size("outer")
    heads = lax.axis_size("head")
    groups = heads * outer
    blocks = outer * TP
    devices = groups * TP
    share = rows // blocks
    fold = TP * share
    span = TP * rows
    tokens = token_order.shape[0]
    head_index = lax.axis_index("head")
    outer_index = lax.axis_index("outer")
    here = lax.axis_index("tp")
    here_word = here.astype(jnp.int32)[None]
    group_index = head_index * outer + outer_index
    rows_w = attn_qkv.shape[0]
    subs = memory_values.shape[0] // NSUB
    picks = MH * KPICK
    capacity = 2 * rows * picks // devices
    back = min(groups - 1, -(-(tokens // 2 - 1) // span))
    base = back * span

    group_inputs = gather_tp(inputs)
    gain_one = attn_gain.astype(f32)[:, None]
    gain_two = memory_gain.astype(f32)[:, None]
    scaled_qkv = (attn_qkv.astype(f32) * gain_one).astype(bf16)
    scaled_query = (memory_query.astype(f32) * gain_two).astype(bf16)
    scaled_gate = (memory_gate.astype(f32) * gain_two).astype(bf16)
    qkv_cut = jnp.transpose(scaled_qkv.reshape(rows_w, 3, TP, LANES), (2, 0, 1, 3))
    qkv_cut = jnp.broadcast_to(
        qkv_cut.reshape(1, TP, rows_w, 3 * LANES), (groups, TP, rows_w, 3 * LANES)
    ).reshape(devices, rows_w, 3 * LANES)
    weight_qkv = swap(qkv_cut, ALL).reshape(width, 3 * LANES)
    to_turned = [
        (groups * part + group, group * TP + part) for group in range(groups) for part in range(TP)
    ]
    from_turned = [(there, at) for at, there in to_turned]

    def columns(piece):
        return jnp.moveaxis(piece.reshape(rows_w, TP, -1), 1, 0)

    by_half = jnp.transpose(memory_picks.reshape(outer, fold, MH, KPICK, 2), (0, 2, 4, 3, 1))
    by_half = by_half.reshape(blocks, KPICK, fold).astype(bf16)
    rest_cut = jnp.concatenate([columns(scaled_query), columns(scaled_gate)], axis=2)
    rest_width = rest_cut.shape[2]
    row_cut = jnp.stack([attn_out, memory_out, sub_keys.reshape(rows_w, width)])

    laid = token_order.reshape(heads, blocks, outer, fold)
    mine = lax.dynamic_index_in_dim(laid, head_index, 0, keepdims=False)
    mine = lax.dynamic_index_in_dim(mine, outer_index, 1, keepdims=False)
    local = jnp.bitwise_xor(mine.reshape(span) - group_index * span, here * rows)
    span_range = jnp.arange(span, dtype=jnp.int32)
    deal = (local[:, None] == span_range[None, :]).astype(bf16)
    undeal = (span_range[:, None] == local[None, :]).astype(bf16)

    group_wide = group_inputs.astype(f32)
    normed_one = (group_wide * norm_scale(group_wide)).astype(bf16)
    projected = mm(normed_one, weight_qkv).astype(bf16)
    queries = projected[:, :LANES] * jnp.asarray(1.0 / math.sqrt(HD), bf16)
    kv_pieces = [projected[:, LANES:]]
    own_cot, own_picks, rest_cut, by_half, row_cut, unused = tie(
        cotangent, memory_picks, rest_cut, by_half, row_cut, kv_pieces[0]
    )
    if back > 0:
        kv_pieces.insert(0, onward(kv_pieces[0], groups, 1))
    group_cot = gather_tp(own_cot)
    row_cut = lax.ppermute(row_cut, ALL, to_turned)
    attn_shifts = {away: shift(row_cut[0], groups, away) for away in range(1, groups)}
    weight_attn = by_group(row_cut[0], attn_shifts, groups, group_index).reshape(LANES, width)
    if by_half.shape[:2] == rest_cut.shape[:2]:
        both = swap(jnp.concatenate([rest_cut, by_half], axis=2), "tp")
        rest_rows, by_half = both[:, :, :rest_width], both[:, :, rest_width:]
    else:
        rest_rows, by_half = swap(rest_cut, "tp"), swap(by_half, BLK)
    rest_rows = rest_rows.reshape(TP * rows_w, rest_width)
    kv_pieces[0], rest_rows = tie(kv_pieces[0], rest_rows)
    for away in range(1, back):
        kv_pieces.insert(0, onward(kv_pieces[0], groups, 1))

    first_pick = own_picks[:, :, :, 0].reshape(rows, picks)
    second_pick = own_picks[:, :, :, 1].reshape(rows, picks)
    owner = first_pick // subs
    device_range = jnp.arange(devices, dtype=jnp.int32)
    owned = (owner[None] == device_range[:, None, None]).astype(bf16)
    before = (
        jnp.arange(picks, dtype=jnp.int32)[:, None] < jnp.arange(picks, dtype=jnp.int32)[None, :]
    ).astype(bf16)
    before_rows = (
        jnp.arange(rows, dtype=jnp.int32)[:, None] < jnp.arange(rows, dtype=jnp.int32)[None, :]
    ).astype(bf16)
    in_row = jnp.einsum("dtk,kj->dtj", owned, before, preferred_element_type=f32)
    row_counts = jnp.sum(owned.astype(f32), axis=2)
    of_rows = jnp.dot(row_counts.astype(bf16), before_rows, preferred_element_type=f32)
    rank = jnp.sum(owned.astype(f32) * (in_row + of_rows[:, :, None]), axis=0).astype(jnp.int32)
    target = owner * capacity + rank
    target_high = target // LANES
    target_low = target % LANES
    places = devices * capacity
    entries = make_entries(target_high, target_low, first_pick % subs, second_pick, places)

    turned_one, unused = tie(jnp.transpose(normed_one), kv_pieces[0])
    keys_values, rest_rows, by_half, entries, turned_one, group_cot, row_cut = tie(
        jnp.concatenate(kv_pieces, axis=0),
        rest_rows,
        by_half,
        entries,
        turned_one,
        group_cot,
        row_cut,
    )
    half_index = jnp.moveaxis(by_half, 1, 0).reshape(KPICK, span).astype(jnp.int32)
    wide_index = jnp.pad(jnp.transpose(half_index), ((0, 0), (0, LANES - KPICK)))
    rest_shifts = {away: shift(rest_rows, groups, away) for away in range(1, groups, 2)}
    doc_ends = jnp.cumsum(doc_lengths)

    def lowest(inside):
        positions = group_index * span + inside
        starts = jnp.where(positions[:, None] >= doc_ends[None, :], doc_ends[None, :], 0)
        return jnp.max(starts, axis=1) - (group_index - back) * span

    low_first = lowest(span_range)
    low = lowest(jnp.bitwise_xor(span_range, here * rows))
    attended, lse, attended_low = attn_fwd(
        base, rows, low_first, here_word, low, queries, keys_values
    )
    attended_low, rest_rows, *shifted = tie(attended_low, rest_rows, *rest_shifts.values())
    rest_shifts = dict(zip(rest_shifts, shifted))
    even_shifts = {away: shift(rest_rows, groups, away) for away in range(2, groups, 2)}
    inputs_wide = inputs.astype(f32)
    hidden_one = inputs_wide + sum_back(attended_low, weight_attn, NN, rows)
    hidden_one, row_cut, *shifted = tie(hidden_one, row_cut, *even_shifts.values())
    rest_shifts.update(zip(even_shifts, shifted))
    weight_rest = by_group(rest_rows, rest_shifts, groups, group_index).reshape(width, rest_width)
    row_shifts = {away: shift(row_cut[1:], groups, away) for away in range(1, groups)}
    row_all = by_group(row_cut[1:], row_shifts, groups, group_index)
    row_all = jnp.moveaxis(row_all, 0, 1).reshape(2, LANES, width)
    weight_mixed = row_all[0]
    key_table = row_all[1].reshape(NSUB, QHALF)
    scale_two = norm_scale(hidden_one)
    group_cot, unused = tie(group_cot, attended_low)
    dealt_cot = mm(deal, group_cot).astype(bf16)
    grad_mixed = mm(dealt_cot, weight_mixed, NT)
    normed_two = mm(deal, gather_tp((hidden_one * scale_two).astype(bf16))).astype(bf16)

    pre = mm(normed_two, weight_rest)
    query_mem = pre[:, :QHALF].astype(bf16)
    gate_pre = pre[:, QHALF:]
    gate_sig = jax.nn.sigmoid(gate_pre)
    grad_memory = (grad_mixed * gate_pre * gate_sig).astype(bf16)
    query_mem, grad_memory = tie(query_mem, grad_memory)
    every_grad = gather(grad_memory, ALL).reshape(heads, outer, TP, blocks, fold, LANES)
    picked_half = pick_scores(query_mem, key_table, wide_index).reshape(KPICK, blocks, fold)
    picked = swap(jnp.moveaxis(picked_half, 1, 0), BLK)
    turned_two, unused = tie(jnp.transpose(normed_two), picked_half)
    picked, turned_two = tie(picked, turned_two)
    picked = jnp.moveaxis(picked.reshape(outer, TP, KPICK, fold), 0, 2).reshape(TP, KPICK, rows)
    pick_weights, sent_weights = make_weights(picked, target_high, target_low, places)
    sent = jnp.concatenate([entries, sent_weights], axis=1)
    sent = jnp.moveaxis(sent.reshape(devices, capacity // LANES, 4, LANES), 2, 1)
    entries = swap(sent.reshape(devices, 4, capacity), ALL).astype(f32)
    entries = entries.reshape(heads, blocks, 4, 1, capacity)
    entry_token = entries[:, :, 0].astype(jnp.int32)
    entry_first = entries[:, :, 1].astype(jnp.int32)
    entry_second = entries[:, :, 2].astype(jnp.int32)
    entry_weight = entries[:, :, 3]

    turns = 2
    table = None
    leaving = []
    flat = (TP // 2, groups, span // turns, LANES)
    for turn in range(turns):
        table, keep, send = spread_weights(
            rows,
            subs,
            heads,
            outer,
            turn,
            turns,
            here_word,
            entry_token,
            entry_first,
            entry_second,
            entry_weight,
            memory_values,
            table,
        )
        leaving.append((keep.reshape(flat), across(send.reshape(flat), 1)))
    leaves = []
    for keep, met in leaving:
        leaves += hop_call(leave_kernel, "sums_first", keep, ("two", "two"), met)

    parts = [None] * heads

    def dots(head, dense, *moved):
        parts[head], dense = row_dots(
            rows,
            subs,
            head,
            outer,
            entry_token,
            entry_first,
            entry_second,
            every_grad,
            memory_values,
            dense,
        )
        parts[head], dense, *moved = tie(parts[head], dense, *moved)
        return dense, moved

    every_grad, *leaves = tie(every_grad, *leaves)
    first = [across(leaf, (2, 4)[turn % 2]) for turn, leaf in enumerate(leaves)]
    dense, unused = dots(0, None)
    dense, first = dots(1, dense, *first)
    leaves = []
    for turn, (keep, met) in enumerate(leaving):
        leaves += hop_call(
            pass_kernel, "sums_second", keep, ("one", "one"), met, *first[2 * turn : 2 * turn + 2]
        )
    dense, *leaves = tie(dense, *leaves)
    second = [across(leaf, (4, 2)[turn % 2]) for turn, leaf in enumerate(leaves)]
    dense, second = dots(2, dense, *second)
    total = jnp.concatenate(
        [
            hop_call(
                total_kernel,
                "sums_last",
                keep,
                ("whole",),
                met,
                *first[2 * turn : 2 * turn + 2],
                *second[2 * turn : 2 * turn + 2],
            )[0]
            for turn, (keep, met) in enumerate(leaving)
        ],
        axis=1,
    )
    dense, total = tie(dense, total)
    dense, unused = dots(3, dense)
    for head in range(4, heads):
        dense, unused = dots(head, dense)
    memory = sum_groups(total, groups, group_index)

    entry_dots = jnp.concatenate(parts, axis=0).reshape(devices, capacity)
    returned = swap(entry_dots, ALL).reshape(places // LANES, LANES)
    table = table.reshape(tokens, subs * NSUB)
    dense = dense.reshape(tokens, width)
    grad_values = value_grads(0, turns, table, dense, None)
    returned, grad_values = tie(returned, grad_values)
    grad_picked = pick_grads(target_high, target_low, pick_weights, returned)
    to_half = jnp.moveaxis(grad_picked.reshape(MH, KPICK, outer, fold), 2, 0)
    to_half = jnp.broadcast_to(to_half[:, :, None], (outer, MH, 2, KPICK, fold))
    grad_half = swap(to_half.reshape(blocks, KPICK, fold), BLK)
    grad_half = jnp.moveaxis(grad_half, 1, 0).reshape(KPICK, span)
    grad_sub, grad_query = unpick_scores(grad_half, half_index, key_table)

    mixed_low = (memory * gate_pre * gate_sig).astype(bf16)
    grad_gate = (grad_mixed * memory * gate_sig * (1.0 + gate_pre * (1.0 - gate_sig))).astype(bf16)
    grad_pre = jnp.concatenate([grad_query, grad_gate], axis=1)
    home_pre = mm(undeal, grad_pre).astype(bf16)

    keep, met = sum_back_start(home_pre, weight_rest, NT, rows)
    met, grad_pre, mixed_low, grad_sub = tie(met, grad_pre, mixed_low, grad_sub)
    stay, got = first_hop(keep, met)
    rest_grads = mm(turned_two, grad_pre).astype(bf16)
    row_grads = [mm(mixed_low, dealt_cot, TN), mm(grad_sub, query_mem).reshape(LANES, width)]
    row_grads = jnp.stack(row_grads).astype(bf16).reshape(2, groups, rows_w, width)
    row_grads = jnp.moveaxis(row_grads, 0, 1).reshape(groups * TP * rows_w, -1)
    memory_grads = jnp.concatenate([rest_grads, row_grads], axis=1)
    got_0, got_1, memory_grads = tie(*got, memory_grads)
    weighted_two = last_hop(*second_hop(stay, (got_0, got_1)))
    memory_grads = lax.psum_scatter(memory_grads, GROUP, scatter_dimension=0, tiled=True)
    grad_hidden = cotangent.astype(f32) + norm_back(hidden_one, scale_two, weighted_two)

    grad_branch = gather_tp(grad_hidden.astype(bf16))
    grad_attended = mm(grad_branch, weight_attn, NT).astype(bf16)
    grad_q, *grad_kv = attn_bwd(
        base, rows, low_first, here_word, low, queries, keys_values, lse, attended, grad_attended
    )
    mixed_low, table, memory_grads, *grad_kv = tie(mixed_low, table, memory_grads, *grad_kv)
    home_mixed = mm(undeal, mixed_low).astype(bf16)
    output_stay, output_got = first_hop(*sum_back_start(home_mixed, weight_mixed, NN, rows))
    carry = grad_kv[0]
    for away in range(back):
        met = onward(carry, groups, -1)
        if away == 0:
            grad_values = value_grads(1, turns, table, dense, grad_values)
            met, grad_values, memory_grads, *output_got = tie(
                met, grad_values, memory_grads, *output_got
            )
        carry = (grad_kv[away + 1].astype(f32) + met.astype(f32)).astype(bf16)
    if back == 0:
        grad_values = value_grads(1, turns, table, dense, grad_values)
    output_stay, output_got = second_hop(output_stay, output_got)
    output = (hidden_one + last_hop(output_stay, output_got)).astype(bf16)

    def columns_home(cut, *splits):
        home = jnp.moveaxis(swap(cut.reshape(TP, rows_w, -1), "tp"), 0, 1).astype(f32)
        return jnp.split(home, splits, axis=2)

    query_home, gate_home = columns_home(memory_grads[:, :rest_width], QHALF)
    query_home = query_home.reshape(rows_w, -1)
    gate_home = gate_home.reshape(rows_w, -1)
    grad_projected = jnp.concatenate([grad_q, carry], axis=1)
    grad_projected, output, query_home, gate_home = tie(
        grad_projected, output, query_home, gate_home
    )

    stay, got = first_hop(*sum_back_start(grad_projected, weight_qkv, NT, rows))
    late_grads = mm(turned_one, grad_projected).reshape(groups, TP * rows_w, 3 * LANES)
    attn_rows = mm(attended_low, grad_branch, TN).reshape(groups, TP * rows_w, LANES)
    late_grads = jnp.concatenate([late_grads, attn_rows], axis=2)
    late_parts = sum_groups_start(late_grads, groups, group_index)
    got_0, got_1, *late_parts = tie(*got, *late_parts)
    stay, got = second_hop(stay, (got_0, got_1))
    late_grads = sum(part.astype(f32) for part in late_parts).astype(bf16)
    got_0, got_1, late_grads = tie(*got, late_grads)
    weighted_one = last_hop(stay, (got_0, got_1))
    grad_inputs = grad_hidden + norm_back(inputs_wide, norm_scale(inputs_wide), weighted_one)
    qkv_home = columns_home(late_grads[:, : 3 * LANES])[0]
    qkv_home = jnp.moveaxis(qkv_home.reshape(rows_w, TP, 3, LANES), 1, 2).reshape(rows_w, -1)
    row_sums = memory_grads[:, rest_width:].reshape(2, rows_w, width)
    row_home = jnp.concatenate([late_grads[:, 3 * LANES :].reshape(1, rows_w, width), row_sums])
    row_home = lax.ppermute(row_home, ALL, from_turned).astype(f32)
    grad_attn_gain = jnp.sum(qkv_home * attn_qkv.astype(f32), axis=1)
    grad_memory_gain = jnp.sum(query_home * memory_query.astype(f32), axis=1) + jnp.sum(
        gate_home * memory_gate.astype(f32), axis=1
    )
    return (
        output,
        grad_inputs,
        grad_attn_gain,
        qkv_home * gain_one,
        row_home[0],
        grad_memory_gain,
        query_home * gain_two,
        row_home[2].reshape(sub_keys.shape),
        gate_home * gain_two,
        row_home[1],
        grad_values,
    )


def solution(mesh):
    heads, blocks = mesh.devices.shape
    cut_mesh = Mesh(mesh.devices.reshape(heads, blocks // TP, TP), ALL)
    matrix = P(ALL, None)
    in_specs = (
        matrix,
        P(ALL),
        matrix,
        matrix,
        P(ALL),
        matrix,
        matrix,
        matrix,
        matrix,
        matrix,
        P(),
        P(),
        P(ALL, None, None, None),
        matrix,
    )
    out_specs = (
        matrix,
        matrix,
        P(ALL),
        matrix,
        matrix,
        P(ALL),
        matrix,
        matrix,
        matrix,
        matrix,
        matrix,
    )
    return jax.shard_map(
        body, mesh=cut_mesh, in_specs=in_specs, out_specs=out_specs, check_vma=False
    )
```

time: 993 us -> 550 us (0.55)
  the two profiles are of different devices: /device:TPU:0 before, /device:TPU:1 now
where the time goes in v2:
time: 550 us; the launch traced here: 540 us
  Pallas kernels  163 us (30%)
  starting transfers between devices  133 us (24%)
  waiting for transfers between devices  109 us (20%)
  other arithmetic  47.1 us (9%)
  local copies, waits for them, and re-layouts  34.4 us (6%)
  matrix products  23.8 us (4%)
  between operations  16.3 us (3%)
  blocking collectives  13.2 us (2%)
    ppermute x50, starting transfers between devices, across(): return lax.ppermute(array, 'tp', [(at, at ^ distance) for at in range(TP)])  55 us
    ppermute x50, waiting for transfers between devices, across(): return lax.ppermute(array, 'tp', [(at, at ^ distance) for at in range(TP)])  48.5 us
    pallas_call x2, Pallas kernels, spread_weights(): pl.pallas_call(lambda *refs: spread_kernel(rows, subs, outer, *refs), gri...  46.1 us
    pallas_call x4, Pallas kernels, row_dots(): pl.pallas_call(lambda *refs: dots_kernel(rows, subs, outer, *refs), grid=...  44.2 us
    all_to_all x7, starting transfers between devices, swap(): return lax.all_to_all(array, axes, split_axis=0, concat_axis=0, tiled=True)  36.1 us
    pallas_call x2, Pallas kernels, value_grads(): pl.pallas_call(value_grads_kernel, grid=(steps,), in_specs=in_specs, out_...  30.3 us
    dot_general x21, matrix products, mm(): return lax.dot_general(left, right, dims, preferred_element_type=f32)  23 us
    ppermute x6, waiting for transfers between devices, sum_groups_start(): parts.append(lax.ppermute(piece, GROUP, pairs))  17.1 us
  transfers between devices with their start and end apart: 80, of which 36 were waited for; matrix products, arithmetic and copies ran while one was open for 12% of the time, Pallas kernels for 26%

profile of v2, /device:TPU:1, one launch (start us, length us, event | category | flops | bytes accessed | tf_op | source)
XLA Modules:
  0.0 540.0 jit_solution(4157262529188190319)
XLA Ops:
  21.8 6.9 %collective-permute-done.2 = bf16[64,1024]{1,0:T(8,128)(2,1)S(1)} collective-permute-done((bf16[64,1024]{1,0:T(8,128)(2,1)S(1)}, bf16[64,1024]{1,0:T(8,128)(2,1)S(1)}, u32[]{:S(2)}, u32[]{:S(2)}) %collective-permute-start.2) | collective-permute-done | bytes 131104 | tf_op jit(solution)/shard_map/ppermute | solution.py:636
  88.5 6.1 %collective-permute-start.14 = (bf16[256,640]{1,0:T(8,128)(2,1)S(1)}, bf16[256,640]{1,0:T(8,128)(2,1)S(1)}, u32[]{:S(2)}, u32[]{:S(2)}) collective-permute-start(bf16[256,640]{1,0:T(8,128)(2,1)S(1)} %bitcast.416), channel_id=1, source_target_pairs={{0,24},{8,0},{16,8},{24,16},{1,25},{9,1},{17,9},{25,17},{2,26},{10... | collective-permute-start | bytes 983048 | tf_op jit(solution)/shard_map/ppermute | solution.py:757
  94.7 6.5 %attn_fwd.1 = (f32[128,1024]{1,0:T(8,128)S(1)}, f32[2,1024]{1,0:T(2,128)S(1)}, bf16[1024,128]{1,0:T(8,128)(2,1)S(1)}) custom-call(s32[4]{0:T(128)S(1)} %slice.242.refs_0_, s32[1]{0:T(128)} %bitcast.2.refs_1_.refs_0_, bf16[1024,128]{1,0:T(8,128)(2,1)S(1)} %slice_multiply_fusion.refs_2_, bf16[3072,256]{1,0:T(8,128)(2,1)S(1)} %pad_maximum_fusion.5.refs_3_, ...), custom_call_target="tpu_custom_call" | custom-call | bytes 43008000 | tf_op jit(solution)/shard_map/attn_fwd/pallas_call | solution.py:135
  101.3 9.8 %collective-permute-done.13 = bf16[256,640]{1,0:T(8,128)(2,1)S(1)} collective-permute-done((bf16[256,640]{1,0:T(8,128)(2,1)S(1)}, bf16[256,640]{1,0:T(8,128)(2,1)S(1)}, u32[]{:S(2)}, u32[]{:S(2)}) %collective-permute-start.13) | collective-permute-done | bytes 327712 | tf_op jit(solution)/shard_map/ppermute | solution.py:757
  121.1 6.1 %collective-permute-done.19 = bf16[2,64,1024]{2,1,0:T(8,128)(2,1)S(1)} collective-permute-done((bf16[2,64,1024]{2,1,0:T(8,128)(2,1)S(1)}, bf16[2,64,1024]{2,1,0:T(8,128)(2,1)S(1)}, u32[]{:S(2)}, u32[]{:S(2)}) %collective-permute-start.19) | collective-permute-done | bytes 262176 | tf_op jit(solution)/shard_map/ppermute | solution.py:636
  144.8 5.1 collective-permute-start.28
  166.5 5.4 all-to-all-done.2.picked_ref
  175.0 13.2 %all_to_all.44 = bf16[32,4,1024]{2,1,0:T(4,128)(2,1)S(1)} all-to-all(bf16[32,4,1024]{2,1,0:T(4,128)(2,1)S(1)} %reshape.448), channel_id=1, replica_groups=mesh['head'=4,'blk'=8] {'head','blk'}, dimensions={0} | all-to-all | bytes 524288 | tf_op jit(solution)/shard_map/all_to_all | solution.py:628
  188.8 23.0 %spread_weights.2 = (bf16[4,1024,2048]{2,1,0:T(8,128)(2,1)}, bf16[4,4,1,4,128,128]{5,4,3,2,1,0:T(8,128)(2,1)S(1)}, bf16[4,4,1,4,128,128]{5,4,3,2,1,0:T(8,128)(2,1)S(1)}) custom-call(s32[1]{0:T(128)} %bitcast.2.refs_1_.refs_0_, s32[4,8,1,1024]{3,2,1,0:T(1,128)S(1)} %get-tuple-element.296.refs_1_.refs_0_, ...), custom_call_target="tpu_custom_call" | custom-call | bytes 79644448 | tf_op jit(solution)/shard_map/spread_weights/pallas_call | solution.py:433
  212.4 23.0 %spread_weights.3 = (bf16[4,1024,2048]{2,1,0:T(8,128)(2,1)}, bf16[4,4,1,4,128,128]{5,4,3,2,1,0:T(8,128)(2,1)S(1)}, bf16[4,4,1,4,128,128]{5,4,3,2,1,0:T(8,128)(2,1)S(1)}) custom-call(s32[1]{0:T(128)} %bitcast.2.refs_1_.refs_0_, s32[4,8,1,1024]{3,2,1,0:T(1,128)S(1)} %get-tuple-element.296.refs_1_.refs_0_, ...), custom_call_target="tpu_custom_call", output_to_operand_aliasing={{0}: (6, {})} | custom-call | bytes 79644448 | tf_op jit(solution)/shard_map/spread_weights/pallas_call | solution.py:433
  248.4 11.2 %row_dots.4 = (f32[1,8,1,1024]{3,2,1,0:T(1,128)S(1)}, bf16[4,1024,1024]{2,1,0:T(8,128)(2,1)}) custom-call(s32[4,8,1,1024]{3,2,1,0:T(1,128)S(1)} %get-tuple-element.296.refs_1_.refs_0_, s32[4,8,1,1024]{3,2,1,0:T(1,128)S(1)} %get-tuple-element.295.refs_2_.refs_1_, s32[4,8,1,1024]{3,2,1,0:T(1,128)S(1)} %get-tuple-element.294.refs_3_.refs_2_, ...), custom_call_target="tpu_custom_call" | custom-call | bytes 39822224 | tf_op jit(solution)/shard_map/row_dots/pallas_call | solution.py:510
  259.6 11.1 %row_dots.5 = (f32[1,8,1,1024]{3,2,1,0:T(1,128)S(1)}, bf16[4,1024,1024]{2,1,0:T(8,128)(2,1)}) custom-call(s32[4,8,1,1024]{3,2,1,0:T(1,128)S(1)} %get-tuple-element.296.refs_1_.refs_0_, s32[4,8,1,1024]{3,2,1,0:T(1,128)S(1)} %get-tuple-element.295.refs_2_.refs_1_, ...), custom_call_target="tpu_custom_call", output_to_operand_aliasing={{1}: (5, {})} | custom-call | bytes 39822224 | tf_op jit(solution)/shard_map/row_dots/pallas_call | solution.py:510
  277.9 10.9 %row_dots.6 = (f32[1,8,1,1024]{3,2,1,0:T(1,128)S(1)}, bf16[4,1024,1024]{2,1,0:T(8,128)(2,1)}) custom-call(s32[4,8,1,1024]{3,2,1,0:T(1,128)S(1)} %get-tuple-element.296.refs_1_.refs_0_, s32[4,8,1,1024]{3,2,1,0:T(1,128)S(1)} %get-tuple-element.295.refs_2_.refs_1_, ...), custom_call_target="tpu_custom_call", output_to_operand_aliasing={{1}: (5, {})} | custom-call | bytes 39822224 | tf_op jit(solution)/shard_map/row_dots/pallas_call | solution.py:510
  293.7 11.0 %row_dots.7 = (f32[1,8,1,1024]{3,2,1,0:T(1,128)S(1)}, bf16[4,1024,1024]{2,1,0:T(8,128)(2,1)}) custom-call(s32[4,8,1,1024]{3,2,1,0:T(1,128)S(1)} %get-tuple-element.296.refs_1_.refs_0_, s32[4,8,1,1024]{3,2,1,0:T(1,128)S(1)} %get-tuple-element.295.refs_2_.refs_1_, ...), custom_call_target="tpu_custom_call", output_to_operand_aliasing={{1}: (5, {})} | custom-call | bytes 39822224 | tf_op jit(solution)/shard_map/row_dots/pallas_call | solution.py:510
  309.5 7.7 %all-to-all-start.4 = ((f32[32,1,1024]{2,1,0:T(1,128)}), f32[32,1,1024]{2,1,0:T(1,128)S(1)}, u32[]{:S(2)}, u32[]{:S(2)}) async-start(f32[32,1,1024]{2,1,0:T(1,128)} %bitcast.96), calls=%async_computation.4 | async-start | bytes 262144 | tf_op jit(solution)/shard_map/all_to_all | solution.py:628
  317.2 15.1 %value_grads.2.refs_0_ = f32[2048,1024]{1,0:T(8,128)} custom-call(bf16[4096,2048]{1,0:T(8,128)(2,1)} %bitcast.378, bf16[4096,1024]{1,0:T(8,128)(2,1)} %bitcast.376), custom_call_target="tpu_custom_call" | custom-call | bytes 52500000 | tf_op jit(solution)/shard_map/value_grads/pallas_call | solution.py:549
  334.4 5.1 pick_grads.1
  349.2 5.9 %unpick_scores.1 = (bf16[256,1024]{1,0:T(8,128)(2,1)S(1)}, bf16[1024,512]{1,0:T(8,128)(2,1)S(1)}) custom-call(f32[32,1024]{1,0:T(8,128)S(1)} %copy_bitcast_fusion.2.grad_ref, s32[32,1024]{1,0:T(8,128)S(1)} %copy-done.21, bf16[256,512]{1,0:T(8,128)(2,1)S(1)} %copy-done.12), custom_call_target="tpu_custom_call" | custom-call | bytes 19911112 | tf_op jit(solution)/shard_map/unpick_scores/pallas_call | solution.py:605
  405.2 6.7 %attn_bwd.1 = (bf16[1024,128]{1,0:T(8,128)(2,1)S(1)}, bf16[1024,256]{1,0:T(8,128)(2,1)S(1)}, bf16[1024,256]{1,0:T(8,128)(2,1)S(1)}, bf16[1024,256]{1,0:T(8,128)(2,1)S(1)}) custom-call(s32[4]{0:T(128)S(1)} %slice.242.refs_0_, s32[1]{0:T(128)} %bitcast.2.refs_1_.refs_0_, bf16[1024,128]{1,0:T(8,128)(2,1)S(1)} %copy-done.10, bf16[3072,256]{1,0:T(8,128)(2,1)S(1)} %copy-done.8, ...), custom_call_target="tpu_custom_call" | custom-call | bytes 53760000 | tf_op jit(solution)/shard_map/attn_bwd/pallas_call | solution.py:234
  423.2 15.2 %value_grads.3 = f32[2048,1024]{1,0:T(8,128)} custom-call(bf16[4096,2048]{1,0:T(8,128)(2,1)} %bitcast.379, bf16[4096,1024]{1,0:T(8,128)(2,1)} %bitcast.377, f32[2048,1024]{1,0:T(8,128)} %value_grads.2.refs_0_), custom_call_target="tpu_custom_call", output_to_operand_aliasing={{}: (2, {})} | custom-call | bytes 52500000 | tf_op jit(solution)/shard_map/value_grads/pallas_call | solution.py:549
  461.0 8.7 %collective-permute-done.59 = bf16[1024,256]{1,0:T(8,128)(2,1)} collective-permute-done((bf16[1024,256]{1,0:T(8,128)(2,1)}, bf16[1024,256]{1,0:T(8,128)(2,1)}, u32[]{:S(2)}, u32[]{:S(2)}) %collective-permute-start.59) | collective-permute-done | bytes 524320 | tf_op jit(solution)/shard_map/ppermute | solution.py:641
  485.9 17.1 %collective-permute-done.66 = bf16[256,512]{1,0:T(8,128)(2,1)S(1)} collective-permute-done((bf16[256,512]{1,0:T(8,128)(2,1)S(1)}, bf16[256,512]{1,0:T(8,128)(2,1)S(1)}, u32[]{:S(2)}, u32[]{:S(2)}) %collective-permute-start.66) | collective-permute-done | bytes 262176 | tf_op jit(solution)/shard_map/ppermute | solution.py:748
  508.7 5.7 %all-to-all-start.7 = ((bf16[8,32,384]{2,1,0:T(8,128)(2,1)}), bf16[8,32,384]{2,1,0:T(8,128)(2,1)S(1)}, u32[]{:S(2)}, u32[]{:S(2)}) async-start(bf16[8,32,384]{2,1,0:T(8,128)(2,1)} %bitcast.152), calls=%async_computation.8 | async-start | bytes 393216 | tf_op jit(solution)/shard_map/all_to_all | solution.py:628
  521.5 10.0 %collective-permute-done.70 = bf16[3,32,1024]{2,1,0:T(8,128)(2,1)S(1)} collective-permute-done((bf16[3,32,1024]{2,1,0:T(8,128)(2,1)S(1)}, bf16[3,32,1024]{2,1,0:T(8,128)(2,1)S(1)}, u32[]{:S(2)}, u32[]{:S(2)}) %collective-permute-start.70) | collective-permute-done | bytes 196640 | tf_op jit(solution)/shard_map/ppermute | solution.py:1120
  (518 shorter events, 277.1 us)
Async XLA Ops:
  13.6 28.5 %all-to-all-start = ((bf16[32,32,384]{2,1,0:T(8,128)(2,1)}), bf16[32,32,384]{2,1,0:T(8,128)(2,1)S(1)}, u32[]{:S(2)}, u32[]{:S(2)}) async-start(bf16[32,32,384]{2,1,0:T(8,128)(2,1)} %bitcast.12), calls=%async_computation | async-start | bytes 1572864 | tf_op jit(solution)/shard_map/all_to_all | solution.py:628
  45.7 23.5 %collective-permute-start.5 = (bf16[1024,256]{1,0:T(8,128)(2,1)S(1)}, bf16[1024,256]{1,0:T(8,128)(2,1)}, u32[]{:S(2)}, u32[]{:S(2)}) collective-permute-start(bf16[1024,256]{1,0:T(8,128)(2,1)S(1)} %slice.317), channel_id=1, source_target_pairs={{0,8},{8,16},{16,24},{1,9},{9,17},{17,25},{2,10},{10,18},{18,26},{... | collective-permute-start | bytes 1572872 | tf_op jit(solution)/shard_map/ppermute | solution.py:641
  54.5 188.8 %all-gather.2.cloned.1.call-start = ((), (), s32[]{:S(2)}) async-start(), calls=%async_computation.9 | async-start | bytes 8650752 | tf_op jit(solution)/shard_map/all_gather | solution.py:632
  55.2 17.9 %collective-permute-start.12 = (bf16[3,32,1024]{2,1,0:T(8,128)(2,1)}, bf16[3,32,1024]{2,1,0:T(8,128)(2,1)}, u32[]{:S(2)}, u32[]{:S(2)}) collective-permute-start(bf16[3,32,1024]{2,1,0:T(8,128)(2,1)} %pad_maximum_fusion.17), channel_id=1, source_target_pairs={{0,0},{4,1},{8,2},{12,3},{16,4},{20,5},{24,6},{28,7},{1,8},{5,9},{... | collective-permute-start | bytes 589832 | tf_op jit(solution)/shard_map/ppermute | solution.py:864
  67.5 19.0 %collective-permute-start.11 = (bf16[4,128,1024]{2,1,0:T(8,128)(2,1)}, bf16[4,128,1024]{2,1,0:T(8,128)(2,1)}, u32[]{:S(2)}, u32[]{:S(2)}) collective-permute-start(bf16[4,128,1024]{2,1,0:T(8,128)(2,1)} %get-tuple-element.288), channel_id=1, source_target_pairs={{0,1},{1,0},{2,3},{3,2},{4,5},{5,4},{6,7},{7,6},{8,9},{9,8},{10,11... | collective-permute-start | bytes 3145736 | tf_op jit(solution)/shard_map/ppermute | solution.py:636
  114.4 18.5 %collective-permute-start.23 = (bf16[256,640]{1,0:T(8,128)(2,1)S(1)}, bf16[256,640]{1,0:T(8,128)(2,1)S(1)}, u32[]{:S(2)}, u32[]{:S(2)}) collective-permute-start(bf16[256,640]{1,0:T(8,128)(2,1)S(1)} %bitcast.418), channel_id=1, source_target_pairs={{0,16},{8,24},{16,0},{24,8},{1,17},{9,25},{17,1},{25,9},{2,18},{10... | collective-permute-start | bytes 983048 | tf_op jit(solution)/shard_map/ppermute | solution.py:757
  211.8 23.7 %collective-permute-start.32 = (bf16[4,4,512,128]{3,2,1,0:T(8,128)(2,1)S(1)}, bf16[4,4,512,128]{3,2,1,0:T(8,128)(2,1)S(1)}, u32[]{:S(2)}, u32[]{:S(2)}) collective-permute-start(bf16[4,4,512,128]{3,2,1,0:T(8,128)(2,1)S(1)} %bitcast.375), channel_id=1, source_target_pairs={{0,1},{1,0},{2,3},{3,2},{4,5},{5,4},{6,7},{7,6},{8,9},{9,8},{10,11... | collective-permute-start | bytes 6291464 | tf_op jit(solution)/shard_map/ppermute | solution.py:636
  243.3 27.5 %collective-permute-start.34 = (bf16[2,4,256,128]{3,2,1,0:T(8,128)(2,1)}, bf16[2,4,256,128]{3,2,1,0:T(8,128)(2,1)S(1)}, u32[]{:S(2)}, u32[]{:S(2)}) collective-permute-start(bf16[2,4,256,128]{3,2,1,0:T(8,128)(2,1)} %copy-done.27), channel_id=1, source_target_pairs={{0,2},{1,3},{2,0},{3,1},{4,6},{5,7},{6,4},{7,5},{8,10},{9,11},{10,... | collective-permute-start | bytes 1572872 | tf_op jit(solution)/shard_map/ppermute | solution.py:636
  244.4 26.3 %collective-permute-start.35 = (bf16[2,4,256,128]{3,2,1,0:T(8,128)(2,1)}, bf16[2,4,256,128]{3,2,1,0:T(8,128)(2,1)S(1)}, u32[]{:S(2)}, u32[]{:S(2)}) collective-permute-start(bf16[2,4,256,128]{3,2,1,0:T(8,128)(2,1)} %copy-done.25), channel_id=1, source_target_pairs={{0,4},{1,5},{2,6},{3,7},{4,0},{5,1},{6,2},{7,3},{8,12},{9,13},{10,... | collective-permute-start | bytes 1572872 | tf_op jit(solution)/shard_map/ppermute | solution.py:636
  245.6 25.2 %collective-permute-start.36 = (bf16[2,4,256,128]{3,2,1,0:T(8,128)(2,1)}, bf16[2,4,256,128]{3,2,1,0:T(8,128)(2,1)S(1)}, u32[]{:S(2)}, u32[]{:S(2)}) collective-permute-start(bf16[2,4,256,128]{3,2,1,0:T(8,128)(2,1)} %copy-done.26), channel_id=1, source_target_pairs={{0,2},{1,3},{2,0},{3,1},{4,6},{5,7},{6,4},{7,5},{8,10},{9,11},{10,... | collective-permute-start | bytes 1572872 | tf_op jit(solution)/shard_map/ppermute | solution.py:636
  245.8 24.9 %collective-permute-start.37 = (bf16[2,4,256,128]{3,2,1,0:T(8,128)(2,1)}, bf16[2,4,256,128]{3,2,1,0:T(8,128)(2,1)S(1)}, u32[]{:S(2)}, u32[]{:S(2)}) collective-permute-start(bf16[2,4,256,128]{3,2,1,0:T(8,128)(2,1)} %copy-done.24), channel_id=1, source_target_pairs={{0,4},{1,5},{2,6},{3,7},{4,0},{5,1},{6,2},{7,3},{8,12},{9,13},{10,... | collective-permute-start | bytes 1572872 | tf_op jit(solution)/shard_map/ppermute | solution.py:636
  305.4 39.1 %collective-permute-start.42 = (bf16[1024,128]{1,0:T(8,128)(2,1)}, bf16[1024,128]{1,0:T(8,128)(2,1)}, u32[]{:S(2)}, u32[]{:S(2)}) collective-permute-start(bf16[1024,128]{1,0:T(8,128)(2,1)} %get-tuple-element.280), channel_id=1, source_target_pairs={{0,8},{8,16},{16,24},{24,0},{1,9},{9,17},{17,25},{25,1},{2,10},{10... | collective-permute-start | bytes 786440 | tf_op jit(solution)/shard_map/ppermute | solution.py:748
  306.1 38.4 %collective-permute-start.44 = (bf16[1024,128]{1,0:T(8,128)(2,1)S(1)}, bf16[1024,128]{1,0:T(8,128)(2,1)}, u32[]{:S(2)}, u32[]{:S(2)}) collective-permute-start(bf16[1024,128]{1,0:T(8,128)(2,1)S(1)} %get-tuple-element.281), channel_id=1, source_target_pairs={{0,24},{8,0},{16,8},{24,16},{1,25},{9,1},{17,9},{25,17},{2,26},{10... | collective-permute-start | bytes 786440 | tf_op jit(solution)/shard_map/ppermute | solution.py:748
  308.7 35.9 %collective-permute-start.43 = (bf16[1024,128]{1,0:T(8,128)(2,1)S(1)}, bf16[1024,128]{1,0:T(8,128)(2,1)}, u32[]{:S(2)}, u32[]{:S(2)}) collective-permute-start(bf16[1024,128]{1,0:T(8,128)(2,1)S(1)} %get-tuple-element.282), channel_id=1, source_target_pairs={{0,16},{8,24},{16,0},{24,8},{1,17},{9,25},{17,1},{25,9},{2,18},{10... | collective-permute-start | bytes 786440 | tf_op jit(solution)/shard_map/ppermute | solution.py:748
  309.5 24.9 %all-to-all-start.4 = ((f32[32,1,1024]{2,1,0:T(1,128)}), f32[32,1,1024]{2,1,0:T(1,128)S(1)}, u32[]{:S(2)}, u32[]{:S(2)}) async-start(f32[32,1,1024]{2,1,0:T(1,128)} %bitcast.96), calls=%async_computation.4 | async-start | bytes 262144 | tf_op jit(solution)/shard_map/all_to_all | solution.py:628
  344.5 68.6 %reduce-scatter.2.cloned.1.call-start = ((), (), s32[]{:S(2)}) async-start(), calls=%async_computation.10 | async-start | bytes 2293760 | tf_op jit(solution)/shard_map/reduce_scatter | solution.py:1068
  415.3 23.0 %collective-permute-start.55 = (bf16[1024,256]{1,0:T(8,128)(2,1)S(1)}, bf16[1024,256]{1,0:T(8,128)(2,1)}, u32[]{:S(2)}, u32[]{:S(2)}) collective-permute-start(bf16[1024,256]{1,0:T(8,128)(2,1)S(1)} %get-tuple-element.223), channel_id=1, source_target_pairs={{8,0},{16,8},{24,16},{9,1},{17,9},{25,17},{10,2},{18,10},{26,18},{... | collective-permute-start | bytes 1572872 | tf_op jit(solution)/shard_map/ppermute | solution.py:641
  420.2 18.2 %collective-permute-start.58 = (bf16[2,64,1024]{2,1,0:T(8,128)(2,1)}, bf16[2,64,1024]{2,1,0:T(8,128)(2,1)}, u32[]{:S(2)}, u32[]{:S(2)}) collective-permute-start(bf16[2,64,1024]{2,1,0:T(8,128)(2,1)} %get-tuple-element.274), channel_id=1, source_target_pairs={{0,4},{1,5},{2,6},{3,7},{4,0},{5,1},{6,2},{7,3},{8,12},{9,13},{10,... | collective-permute-start | bytes 786440 | tf_op jit(solution)/shard_map/ppermute | solution.py:636
  421.4 17.0 %collective-permute-start.57 = (bf16[2,64,1024]{2,1,0:T(8,128)(2,1)}, bf16[2,64,1024]{2,1,0:T(8,128)(2,1)}, u32[]{:S(2)}, u32[]{:S(2)}) collective-permute-start(bf16[2,64,1024]{2,1,0:T(8,128)(2,1)} %get-tuple-element.275), channel_id=1, source_target_pairs={{0,2},{1,3},{2,0},{3,1},{4,6},{5,7},{6,4},{7,5},{8,10},{9,11},{10,... | collective-permute-start | bytes 786440 | tf_op jit(solution)/shard_map/ppermute | solution.py:636
  479.0 24.0 %collective-permute-start.66 = (bf16[256,512]{1,0:T(8,128)(2,1)S(1)}, bf16[256,512]{1,0:T(8,128)(2,1)S(1)}, u32[]{:S(2)}, u32[]{:S(2)}) collective-permute-start(bf16[256,512]{1,0:T(8,128)(2,1)S(1)} %get-tuple-element.270), channel_id=1, source_target_pairs={{0,16},{8,24},{16,0},{24,8},{1,17},{9,25},{17,1},{25,9},{2,18},{10... | collective-permute-start | bytes 786440 | tf_op jit(solution)/shard_map/ppermute | solution.py:748
  480.1 22.9 %collective-permute-start.65 = (bf16[256,512]{1,0:T(8,128)(2,1)S(1)}, bf16[256,512]{1,0:T(8,128)(2,1)S(1)}, u32[]{:S(2)}, u32[]{:S(2)}) collective-permute-start(bf16[256,512]{1,0:T(8,128)(2,1)S(1)} %get-tuple-element.271), channel_id=1, source_target_pairs={{0,8},{8,16},{16,24},{24,0},{1,9},{9,17},{17,25},{25,1},{2,10},{10... | collective-permute-start | bytes 786440 | tf_op jit(solution)/shard_map/ppermute | solution.py:748
  484.0 18.9 %collective-permute-start.64 = (bf16[2,64,1024]{2,1,0:T(8,128)(2,1)S(1)}, bf16[2,64,1024]{2,1,0:T(8,128)(2,1)S(1)}, u32[]{:S(2)}, u32[]{:S(2)}) collective-permute-start(bf16[2,64,1024]{2,1,0:T(8,128)(2,1)S(1)} %get-tuple-element.272), channel_id=1, source_target_pairs={{0,4},{1,5},{2,6},{3,7},{4,0},{5,1},{6,2},{7,3},{8,12},{9,13},{10,... | collective-permute-start | bytes 786440 | tf_op jit(solution)/shard_map/ppermute | solution.py:636
  484.4 18.6 %collective-permute-start.63 = (bf16[2,64,1024]{2,1,0:T(8,128)(2,1)S(1)}, bf16[2,64,1024]{2,1,0:T(8,128)(2,1)S(1)}, u32[]{:S(2)}, u32[]{:S(2)}) collective-permute-start(bf16[2,64,1024]{2,1,0:T(8,128)(2,1)S(1)} %get-tuple-element.273), channel_id=1, source_target_pairs={{0,2},{1,3},{2,0},{3,1},{4,6},{5,7},{6,4},{7,5},{8,10},{9,11},{10,... | collective-permute-start | bytes 786440 | tf_op jit(solution)/shard_map/ppermute | solution.py:636
  514.4 17.0 %collective-permute-start.70 = (bf16[3,32,1024]{2,1,0:T(8,128)(2,1)S(1)}, bf16[3,32,1024]{2,1,0:T(8,128)(2,1)S(1)}, u32[]{:S(2)}, u32[]{:S(2)}) collective-permute-start(bf16[3,32,1024]{2,1,0:T(8,128)(2,1)S(1)} %pad_maximum_fusion.18), channel_id=1, source_target_pairs={{0,0},{1,4},{2,8},{3,12},{4,16},{5,20},{6,24},{7,28},{8,1},{9,5},{... | collective-permute-start | bytes 589832 | tf_op jit(solution)/shard_map/ppermute | solution.py:1120
  (136 other events, 1400.1 us)
Sparse Core Ops, SparseCore 0:
  158.8 76.2 all-gather.1
  375.7 37.4 reduce-scatter.1

commit v3 on v2

--- a/solution.py
+++ b/solution.py
@@ -130,7 +130,7 @@
 
 def attn_fwd(base, rows, low_first, here, low, queries, keys_values):
     span = queries.shape[0]
-    block_q, block_k = 256, 512
+    block_q, block_k = 512, 512
     by_row, one_lane, two_lane, by_lane = attn_specs(block_q, rows, span)
     return pl.pallas_call(
         lambda *refs: attn_fwd_kernel(base, span, rows, block_k, *refs),
@@ -149,7 +149,7 @@
             jax.ShapeDtypeStruct((2, span), f32),
             jax.ShapeDtypeStruct((span, LANES), bf16),
         ],
-        compiler_params=params(32),
+        compiler_params=params(24),
         cost_estimate=lasting(keys_values.shape[0] / 250),
         name="attn_fwd",
     )(low_first[::block_q], here, queries, keys_values, low[None, :])
@@ -228,7 +228,7 @@
 
 def attn_bwd(base, rows, low_first, here, low, queries, keys_values, lse, att, grads):
     span = queries.shape[0]
-    block_q, block_k = 256, 512
+    block_q, block_k = 512, 512
     reach = keys_values.shape[0]
     by_row, one_lane, two_lane, by_lane = attn_specs(block_q, rows, span)
     return pl.pallas_call(
@@ -250,7 +250,7 @@
         ),
         out_shape=[jax.ShapeDtypeStruct((span, LANES), bf16)]
         + [jax.ShapeDtypeStruct((span, 2 * LANES), bf16)] * (reach // span),
-        compiler_params=params(48),
+        compiler_params=params(32),
         cost_estimate=lasting(keys_values.shape[0] / 200),
         name="attn_bwd",
     )(low_first[::block_q], here, queries, keys_values, low[None, :], lse, att, grads)
@@ -301,7 +301,7 @@
         entries_kernel,
         out_shape=jax.ShapeDtypeStruct((places // LANES, 3 * LANES), bf16),
         scratch_shapes=[pltpu.VMEM(high.shape, f32)],
-        compiler_params=params(32),
+        compiler_params=params(16),
         cost_estimate=lasting(5),
         name="make_entries",
     )(high, low, first.astype(f32), second.astype(f32))
@@ -324,7 +324,7 @@
             jax.ShapeDtypeStruct(high.shape, f32),
             jax.ShapeDtypeStruct((places // LANES, LANES), bf16),
         ],
-        compiler_params=params(32),
+        compiler_params=params(16),
         cost_estimate=lasting(3),
         name="make_weights",
     )(picked, high, low)
@@ -361,7 +361,7 @@
         grads_kernel,
         out_shape=jax.ShapeDtypeStruct((high.shape[1], high.shape[0]), f32),
         scratch_shapes=[pltpu.VMEM(high.shape, f32)],
-        compiler_params=params(32),
+        compiler_params=params(16),
         cost_estimate=lasting(5),
         name="pick_grads",
     )(high, low, weights, table)
@@ -450,7 +450,7 @@
             piece_shape,
         ],
         input_output_aliases=aliases,
-        compiler_params=params(48),
+        compiler_params=params(36),
         cost_estimate=lasting(heads * blocks // turns * rows / 90),
         name="spread_weights",
     )(*operands)
@@ -488,19 +488,21 @@
         )
 
 
-def row_dots(rows, subs, head, outer, token, first, second, grads, values, dense):
+def row_dots(rows, subs, part, parts, outer, token, first, second, grads, values, dense):
     heads, blocks, capacity = token.shape[0], token.shape[1], token.shape[3]
     width = values.shape[1]
     count = 2
     fold = rows // outer
-    row = pl.BlockSpec((1, count, 1, capacity), lambda i: (head, i, 0, 0))
+    mine = heads // parts
+    top = part * mine
+    row = pl.BlockSpec((1, count, 1, capacity), lambda h, i: (top + h, i, 0, 0))
     operands = [token, first, second, grads, values]
     in_specs = [
         row,
         row,
         row,
-        pl.BlockSpec((1, outer, TP, count, fold, LANES), lambda i: (head, 0, 0, i, 0, 0)),
-        pl.BlockSpec(values.shape, lambda i: (0, 0)),
+        pl.BlockSpec((1, outer, TP, count, fold, LANES), lambda h, i: (top + h, 0, 0, i, 0, 0)),
+        pl.BlockSpec(values.shape, lambda h, i: (0, 0)),
     ]
     aliases = {}
     if dense is not None:
@@ -509,19 +511,19 @@
         aliases = {5: 1}
     return pl.pallas_call(
         lambda *refs: dots_kernel(rows, subs, outer, *refs),
-        grid=(blocks // count,),
+        grid=(mine, blocks // count),
         in_specs=in_specs,
         out_specs=[
-            pl.BlockSpec((1, count, 1, capacity), lambda i: (0, i, 0, 0)),
-            pl.BlockSpec((1, count * rows, width), lambda i: (head, i, 0)),
+            pl.BlockSpec((1, count, 1, capacity), lambda h, i: (h, i, 0, 0)),
+            pl.BlockSpec((1, count * rows, width), lambda h, i: (top + h, i, 0)),
         ],
         out_shape=[
-            jax.ShapeDtypeStruct((1, blocks, 1, capacity), f32),
+            jax.ShapeDtypeStruct((mine, blocks, 1, capacity), f32),
             jax.ShapeDtypeStruct((heads, blocks * rows, width), bf16),
         ],
         input_output_aliases=aliases,
-        compiler_params=params(48),
-        cost_estimate=lasting(blocks * rows / 90),
+        compiler_params=params(36),
+        cost_estimate=lasting(mine * blocks * rows / 90),
         name="row_dots",
     )(*operands)
 
@@ -553,7 +555,7 @@
         out_specs=pl.BlockSpec((block, width), lambda i: (turn * steps + i, 0)),
         out_shape=jax.ShapeDtypeStruct((own_rows, width), f32),
         input_output_aliases=aliases,
-        compiler_params=params(56),
+        compiler_params=params(48 if dense.size <= 2**23 else 58),
         cost_estimate=lasting(15 * 2 / turns),
         name="value_grads",
     )(*operands)
@@ -581,7 +583,7 @@
         ],
         out_specs=pl.BlockSpec((KPICK, block), lambda i: (0, i)),
         out_shape=jax.ShapeDtypeStruct((KPICK, rows), f32),
-        compiler_params=params(32),
+        compiler_params=params(16),
         cost_estimate=lasting(rows / 600),
         name="pick_scores",
     )(query, table, index)
@@ -618,12 +620,86 @@
             jax.ShapeDtypeStruct((NSUB, rows), bf16),
             jax.ShapeDtypeStruct((rows, QHALF), bf16),
         ],
-        compiler_params=params(32),
+        compiler_params=params(16),
         cost_estimate=lasting(rows / 180),
         name="unpick_scores",
     )(grads, index, table)
 
 
+def products_kernel(dims, rows, *refs):
+    left_ref, right_ref, keep_ref, send_ref = refs[-4:]
+    if len(refs) > 4:
+        place = lax.broadcasted_iota(jnp.int32, (2 * rows, refs[0].shape[1]), 0)
+        home = place + pl.program_id(0) * 2 * rows == refs[0][...]
+        left = mm(jnp.where(home, 1.0, 0.0).astype(bf16), left_ref[...]).astype(bf16)
+    else:
+        left = left_ref[...]
+    product = mm(left, right_ref[...], dims).astype(bf16)
+    keep_ref[0] = product[:rows]
+    send_ref[0] = product[rows:]
+
+
+def two_products(left, right, dims, rows, dealt_from=None):
+    width = right.shape[1] if dims == NN else right.shape[0]
+    operands = [left, right]
+    in_specs = [
+        pl.BlockSpec((2 * rows, left.shape[1]), lambda i: (i, 0)),
+        pl.BlockSpec(right.shape, lambda i: (0, 0)),
+    ]
+    if dealt_from is not None:
+        in_specs[0] = pl.BlockSpec(left.shape, lambda i: (0, 0))
+        operands.insert(0, dealt_from[None, :])
+        in_specs.insert(0, pl.BlockSpec((1, dealt_from.shape[0]), lambda i: (0, 0)))
+    return pl.pallas_call(
+        lambda *refs: products_kernel(dims, rows, *refs),
+        grid=(TP // 2,),
+        in_specs=in_specs,
+        out_specs=[pl.BlockSpec((1, rows, width), lambda i: (i, 0, 0))] * 2,
+        out_shape=[jax.ShapeDtypeStruct((TP // 2, rows, width), bf16)] * 2,
+        compiler_params=params(16),
+        cost_estimate=lasting(4),
+        name="two_products",
+    )(*operands)
+
+
+def shards_kernel(splits, sums_ref, gain_ref, weight_refs, out_refs, gain_grad_ref):
+    sources = sums_ref.shape[0]
+    turned = jnp.zeros(gain_grad_ref.shape, f32)
+    for part in range(TP):
+        total = sums_ref[part].astype(f32)
+        for more in range(part + TP, sources, TP):
+            total = total + sums_ref[more].astype(f32)
+        start = 0
+        for (width, stride, offset), weight_ref, out_ref in zip(splits, weight_refs, out_refs):
+            here = slice(offset + part * stride, offset + part * stride + width)
+            piece = total[:, start : start + width]
+            product = piece * weight_ref[:, here].astype(f32)
+            turned = turned + jnp.sum(product, axis=1, keepdims=True)
+            out_ref[:, here] = piece * gain_ref[...]
+            start = start + width
+    gain_grad_ref[...] = turned
+
+
+def shard_grads(sums, gain, splits, *weights):
+    rows = gain.shape[0]
+    count = len(weights)
+    owners = [min(at, count - 1) for at in range(len(splits))]
+
+    def kernel(sums_ref, gain_ref, *refs):
+        weight_refs = [refs[at] for at in owners]
+        out_refs = [refs[count + at] for at in owners]
+        shards_kernel(splits, sums_ref, gain_ref, weight_refs, out_refs, refs[-1])
+
+    return pl.pallas_call(
+        kernel,
+        out_shape=[jax.ShapeDtypeStruct(weight.shape, f32) for weight in weights]
+        + [jax.ShapeDtypeStruct((rows, 1), f32)],
+        compiler_params=params(16),
+        cost_estimate=lasting(3),
+        name="shard_grads",
+    )(sums, gain, *weights)
+
+
 def swap(array, axes):
     return lax.all_to_all(array, axes, split_axis=0, concat_axis=0, tiled=True)
 
@@ -641,49 +717,36 @@
     return lax.ppermute(array, GROUP, pairs)
 
 
-def gather_tp(own):
-    half = own.shape[0] // 2
-    near = across(own, 2)
-    next_one = across(own, 4)
-    far = jnp.concatenate([across(near[:half], 4), across(next_one[half:], 2)])
-    quad = jnp.stack([own, near, next_one, far])
+def gather_hop(own):
+    far = across(own, 6)
+    return across(own, 2), across(own, 4), far
+
+
+def gather_cores(own, near):
+    quad = jnp.stack([own, *near])
     both = jnp.stack([quad, across(quad, 1)], axis=1)
     return both.reshape((TP * own.shape[0],) + own.shape[1:])
 
 
-def halves(array):
-    blocks = array.reshape((TP // 2, 2, -1) + array.shape[1:])
-    return tuple(blocks[:, core].reshape((-1,) + array.shape[1:]) for core in range(2))
-
-
-def sum_back_start(left, right, dims, rows):
-    keep_left, send_left = halves(left)
-    met = across(mm(send_left, right, dims).astype(bf16), 1)
-    return mm(keep_left, right, dims).reshape(4, rows, -1), met.reshape(4, rows, -1)
-
-
-def first_hop(keep, met):
-    half = keep.shape[1] // 2
-    sums = keep + met.astype(f32)
-    stay = (sums[0::2, :half], sums[:2, half:])
-    got = (across(sums[1::2, :half].astype(bf16), 2), across(sums[2:, half:].astype(bf16), 4))
-    return stay, got
-
-
-def second_hop(stay, got):
-    sums = (stay[0] + got[0].astype(f32), stay[1] + got[1].astype(f32))
-    got = (across(sums[0][1].astype(bf16), 4), across(sums[1][1].astype(bf16), 2))
-    return (sums[0][0], sums[1][0]), got
-
-
-def last_hop(stay, got):
-    return jnp.concatenate(
-        [stay[0] + got[0].astype(f32), stay[1] + got[1].astype(f32)], axis=0
-    )
+def gather_tp(own):
+    return gather_cores(own, gather_hop(own))
+
+
+def chip_send(sums):
+    return sums[0], [across(sums[turn].astype(bf16), 2 * turn) for turn in (3, 1, 2)]
+
+
+def chip_hop(keep, met):
+    return chip_send(keep.astype(f32) + met.astype(f32))
+
+
+def last_hop(own, got):
+    return own + sum(part.astype(f32) for part in got)
 
 
 def sum_back(left, right, dims, rows):
-    return last_hop(*second_hop(*first_hop(*sum_back_start(left, right, dims, rows))))
+    keep, send = two_products(left, right, dims, rows)
+    return last_hop(*chip_hop(keep, across(send, 1)))
 
 
 def chip_sums(keep_ref, met_ref, chip, half):
@@ -731,7 +794,7 @@
         in_specs=[four, four, two, two, one, one][: len(operands) + 1],
         out_specs=[specs[out] for out in outs],
         out_shape=[jax.ShapeDtypeStruct(shapes[out], bf16) for out in outs],
-        compiler_params=params(32),
+        compiler_params=params(16),
         cost_estimate=lasting(keep.size / 5e5),
         name=name,
     )(keep, *operands)
@@ -817,7 +880,16 @@
     back = min(groups - 1, -(-(tokens // 2 - 1) // span))
     base = back * span
 
-    group_inputs = gather_tp(inputs)
+    near = gather_hop(inputs)
+    row_cut = jnp.stack([attn_out, memory_out, sub_keys.reshape(rows_w, width)])
+    own_cot, row_cut, *near = tie(cotangent, row_cut, *near)
+    near_cot = gather_hop(own_cot)
+    to_turned = [
+        (groups * part + group, group * TP + part) for group in range(groups) for part in range(TP)
+    ]
+    from_turned = [(there, at) for at, there in to_turned]
+    row_cut = lax.ppermute(row_cut, ALL, to_turned)
+    group_inputs = gather_cores(inputs, near)
     gain_one = attn_gain.astype(f32)[:, None]
     gain_two = memory_gain.astype(f32)[:, None]
     scaled_qkv = (attn_qkv.astype(f32) * gain_one).astype(bf16)
@@ -828,10 +900,6 @@
         qkv_cut.reshape(1, TP, rows_w, 3 * LANES), (groups, TP, rows_w, 3 * LANES)
     ).reshape(devices, rows_w, 3 * LANES)
     weight_qkv = swap(qkv_cut, ALL).reshape(width, 3 * LANES)
-    to_turned = [
-        (groups * part + group, group * TP + part) for group in range(groups) for part in range(TP)
-    ]
-    from_turned = [(there, at) for at, there in to_turned]
 
     def columns(piece):
         return jnp.moveaxis(piece.reshape(rows_w, TP, -1), 1, 0)
@@ -840,7 +908,6 @@
     by_half = by_half.reshape(blocks, KPICK, fold).astype(bf16)
     rest_cut = jnp.concatenate([columns(scaled_query), columns(scaled_gate)], axis=2)
     rest_width = rest_cut.shape[2]
-    row_cut = jnp.stack([attn_out, memory_out, sub_keys.reshape(rows_w, width)])
 
     laid = token_order.reshape(heads, blocks, outer, fold)
     mine = lax.dynamic_index_in_dim(laid, head_index, 0, keepdims=False)
@@ -848,31 +915,27 @@
     local = jnp.bitwise_xor(mine.reshape(span) - group_index * span, here * rows)
     span_range = jnp.arange(span, dtype=jnp.int32)
     deal = (local[:, None] == span_range[None, :]).astype(bf16)
-    undeal = (span_range[:, None] == local[None, :]).astype(bf16)
 
     group_wide = group_inputs.astype(f32)
     normed_one = (group_wide * norm_scale(group_wide)).astype(bf16)
     projected = mm(normed_one, weight_qkv).astype(bf16)
     queries = projected[:, :LANES] * jnp.asarray(1.0 / math.sqrt(HD), bf16)
     kv_pieces = [projected[:, LANES:]]
-    own_cot, own_picks, rest_cut, by_half, row_cut, unused = tie(
-        cotangent, memory_picks, rest_cut, by_half, row_cut, kv_pieces[0]
+    own_picks, rest_cut, by_half, kv_pieces[0] = tie(
+        memory_picks, rest_cut, by_half, kv_pieces[0]
     )
     if back > 0:
         kv_pieces.insert(0, onward(kv_pieces[0], groups, 1))
-    group_cot = gather_tp(own_cot)
-    row_cut = lax.ppermute(row_cut, ALL, to_turned)
-    attn_shifts = {away: shift(row_cut[0], groups, away) for away in range(1, groups)}
-    weight_attn = by_group(row_cut[0], attn_shifts, groups, group_index).reshape(LANES, width)
     if by_half.shape[:2] == rest_cut.shape[:2]:
         both = swap(jnp.concatenate([rest_cut, by_half], axis=2), "tp")
         rest_rows, by_half = both[:, :, :rest_width], both[:, :, rest_width:]
     else:
         rest_rows, by_half = swap(rest_cut, "tp"), swap(by_half, BLK)
     rest_rows = rest_rows.reshape(TP * rows_w, rest_width)
-    kv_pieces[0], rest_rows = tie(kv_pieces[0], rest_rows)
+    kv_pieces[0], row_cut, *near_cot = tie(kv_pieces[0], row_cut, *near_cot)
     for away in range(1, back):
         kv_pieces.insert(0, onward(kv_pieces[0], groups, 1))
+    group_cot = gather_cores(own_cot, near_cot)
 
     first_pick = own_picks[:, :, :, 0].reshape(rows, picks)
     second_pick = own_picks[:, :, :, 1].reshape(rows, picks)
@@ -896,13 +959,12 @@
     entries = make_entries(target_high, target_low, first_pick % subs, second_pick, places)
 
     turned_one, unused = tie(jnp.transpose(normed_one), kv_pieces[0])
-    keys_values, rest_rows, by_half, entries, turned_one, group_cot, row_cut = tie(
+    keys_values, rest_rows, by_half, entries, turned_one, row_cut = tie(
         jnp.concatenate(kv_pieces, axis=0),
         rest_rows,
         by_half,
         entries,
         turned_one,
-        group_cot,
         row_cut,
     )
     half_index = jnp.moveaxis(by_half, 1, 0).reshape(KPICK, span).astype(jnp.int32)
@@ -920,8 +982,13 @@
     attended, lse, attended_low = attn_fwd(
         base, rows, low_first, here_word, low, queries, keys_values
     )
-    attended_low, rest_rows, *shifted = tie(attended_low, rest_rows, *rest_shifts.values())
-    rest_shifts = dict(zip(rest_shifts, shifted))
+    attn_shifts = {away: shift(row_cut[0], groups, away) for away in range(1, groups)}
+    attended_low, group_cot, rest_rows, *shifted = tie(
+        attended_low, group_cot, rest_rows, *attn_shifts.values(), *rest_shifts.values()
+    )
+    attn_shifts = dict(zip(attn_shifts, shifted))
+    rest_shifts = dict(zip(rest_shifts, shifted[len(attn_shifts) :]))
+    weight_attn = by_group(row_cut[0], attn_shifts, groups, group_index).reshape(LANES, width)
     even_shifts = {away: shift(rest_rows, groups, away) for away in range(2, groups, 2)}
     inputs_wide = inputs.astype(f32)
     hidden_one = inputs_wide + sum_back(attended_low, weight_attn, NN, rows)
@@ -934,7 +1001,6 @@
     weight_mixed = row_all[0]
     key_table = row_all[1].reshape(NSUB, QHALF)
     scale_two = norm_scale(hidden_one)
-    group_cot, unused = tie(group_cot, attended_low)
     dealt_cot = mm(deal, group_cot).astype(bf16)
     grad_mixed = mm(dealt_cot, weight_mixed, NT)
     normed_two = mm(deal, gather_tp((hidden_one * scale_two).astype(bf16))).astype(bf16)
@@ -982,17 +1048,17 @@
             table,
         )
         leaving.append((keep.reshape(flat), across(send.reshape(flat), 1)))
-    leaves = []
-    for keep, met in leaving:
-        leaves += hop_call(leave_kernel, "sums_first", keep, ("two", "two"), met)
-
-    parts = [None] * heads
-
-    def dots(head, dense, *moved):
-        parts[head], dense = row_dots(
+    dots = []
+    dense = None
+
+    def more_dots(dense, *moved):
+        if len(dots) == heads:
+            return dense, moved
+        part, dense = row_dots(
             rows,
             subs,
-            head,
+            len(dots),
+            heads,
             outer,
             entry_token,
             entry_first,
@@ -1001,43 +1067,39 @@
             memory_values,
             dense,
         )
-        parts[head], dense, *moved = tie(parts[head], dense, *moved)
+        part, dense, *moved = tie(part, dense, *moved)
+        dots.append(part)
         return dense, moved
 
+    def sums_call(kernel, name, outs, half, *operands):
+        keep, met = leaving[half]
+        return hop_call(kernel, name, keep, outs, met, *operands)
+
+    leaves = sums_call(leave_kernel, "sums_first", ("two", "two"), 0)
     every_grad, *leaves = tie(every_grad, *leaves)
-    first = [across(leaf, (2, 4)[turn % 2]) for turn, leaf in enumerate(leaves)]
-    dense, unused = dots(0, None)
-    dense, first = dots(1, dense, *first)
-    leaves = []
-    for turn, (keep, met) in enumerate(leaving):
-        leaves += hop_call(
-            pass_kernel, "sums_second", keep, ("one", "one"), met, *first[2 * turn : 2 * turn + 2]
-        )
+    first = [[across(leaves[0], 2), across(leaves[1], 4)]]
+    dense, leaving[1] = more_dots(dense, *leaving[1])
+    leaves = sums_call(leave_kernel, "sums_first", ("two", "two"), 1)
     dense, *leaves = tie(dense, *leaves)
-    second = [across(leaf, (4, 2)[turn % 2]) for turn, leaf in enumerate(leaves)]
-    dense, second = dots(2, dense, *second)
-    total = jnp.concatenate(
-        [
-            hop_call(
-                total_kernel,
-                "sums_last",
-                keep,
-                ("whole",),
-                met,
-                *first[2 * turn : 2 * turn + 2],
-                *second[2 * turn : 2 * turn + 2],
-            )[0]
-            for turn, (keep, met) in enumerate(leaving)
-        ],
-        axis=1,
-    )
-    dense, total = tie(dense, total)
-    dense, unused = dots(3, dense)
-    for head in range(4, heads):
-        dense, unused = dots(head, dense)
+    first.append([across(leaves[0], 2), across(leaves[1], 4)])
+    dense, first[0] = more_dots(dense, *first[0])
+    leaves = sums_call(pass_kernel, "sums_second", ("one", "one"), 0, *first[0])
+    dense, *leaves = tie(dense, *leaves)
+    second = [[across(leaves[0], 4), across(leaves[1], 2)]]
+    dense, moved = more_dots(dense, *first[1], *second[0])
+    first[1], second[0] = moved[:2], moved[2:]
+    leaves = sums_call(pass_kernel, "sums_second", ("one", "one"), 1, *first[1])
+    total = sums_call(total_kernel, "sums_last", ("whole",), 0, *first[0], *second[0])
+    dense, *leaves = tie(dense, *leaves)
+    second.append([across(leaves[0], 4), across(leaves[1], 2)])
+    dense, second[1] = more_dots(dense, *second[1])
+    while len(dots) < heads:
+        dense, unused = more_dots(dense)
+    total += sums_call(total_kernel, "sums_last", ("whole",), 1, *first[1], *second[1])
+    total = jnp.concatenate(total, axis=1)
     memory = sum_groups(total, groups, group_index)
 
-    entry_dots = jnp.concatenate(parts, axis=0).reshape(devices, capacity)
+    entry_dots = jnp.concatenate(dots, axis=0).reshape(devices, capacity)
     returned = swap(entry_dots, ALL).reshape(places // LANES, LANES)
     table = table.reshape(tokens, subs * NSUB)
     dense = dense.reshape(tokens, width)
@@ -1053,85 +1115,88 @@
     mixed_low = (memory * gate_pre * gate_sig).astype(bf16)
     grad_gate = (grad_mixed * memory * gate_sig * (1.0 + gate_pre * (1.0 - gate_sig))).astype(bf16)
     grad_pre = jnp.concatenate([grad_query, grad_gate], axis=1)
-    home_pre = mm(undeal, grad_pre).astype(bf16)
-
-    keep, met = sum_back_start(home_pre, weight_rest, NT, rows)
+    keep, send = two_products(grad_pre, weight_rest, NT, rows, local)
+    met = across(send, 1)
+
     met, grad_pre, mixed_low, grad_sub = tie(met, grad_pre, mixed_low, grad_sub)
-    stay, got = first_hop(keep, met)
+    own, got = chip_hop(keep, met)
     rest_grads = mm(turned_two, grad_pre).astype(bf16)
     row_grads = [mm(mixed_low, dealt_cot, TN), mm(grad_sub, query_mem).reshape(LANES, width)]
     row_grads = jnp.stack(row_grads).astype(bf16).reshape(2, groups, rows_w, width)
     row_grads = jnp.moveaxis(row_grads, 0, 1).reshape(groups * TP * rows_w, -1)
     memory_grads = jnp.concatenate([rest_grads, row_grads], axis=1)
-    got_0, got_1, memory_grads = tie(*got, memory_grads)
-    weighted_two = last_hop(*second_hop(stay, (got_0, got_1)))
+    memory_grads, mixed_low, *got = tie(memory_grads, mixed_low, *got)
     memory_grads = lax.psum_scatter(memory_grads, GROUP, scatter_dimension=0, tiled=True)
+    weighted_two = last_hop(own, got)
     grad_hidden = cotangent.astype(f32) + norm_back(hidden_one, scale_two, weighted_two)
 
-    grad_branch = gather_tp(grad_hidden.astype(bf16))
+    output_keep, output_met = two_products(mixed_low, weight_mixed, NN, rows, local)
+    own_branch = grad_hidden.astype(bf16)
+    near_branch = gather_hop(own_branch)
+    output_keep, output_met, *near_branch = tie(output_keep, output_met, *near_branch)
+    output_met = across(output_met, 1)
+    grad_branch = gather_cores(own_branch, near_branch)
     grad_attended = mm(grad_branch, weight_attn, NT).astype(bf16)
     grad_q, *grad_kv = attn_bwd(
         base, rows, low_first, here_word, low, queries, keys_values, lse, attended, grad_attended
     )
-    mixed_low, table, memory_grads, *grad_kv = tie(mixed_low, table, memory_grads, *grad_kv)
-    home_mixed = mm(undeal, mixed_low).astype(bf16)
-    output_stay, output_got = first_hop(*sum_back_start(home_mixed, weight_mixed, NN, rows))
+    output_keep, output_met, table, memory_grads, *grad_kv = tie(
+        output_keep, output_met, table, memory_grads, *grad_kv
+    )
+
+    rest_home = swap(memory_grads[:, :rest_width].reshape(TP, rows_w, -1), "tp")
+    attended_low, unused = tie(attended_low, grad_kv[0])
+    attn_rows = mm(attended_low, grad_branch, TN).astype(bf16).reshape(groups, rows_w, width)
+    attn_rows = sum_groups_start(attn_rows, groups, group_index)
+    output_got = None
     carry = grad_kv[0]
     for away in range(back):
         met = onward(carry, groups, -1)
+        if away == back - 1:
+            output_own, output_got = chip_hop(output_keep, output_met)
+            grad_values = value_grads(1, turns, table, dense, grad_values)
+            met, grad_values, *output_got = tie(met, grad_values, *output_got)
         if away == 0:
-            grad_values = value_grads(1, turns, table, dense, grad_values)
-            met, grad_values, memory_grads, *output_got = tie(
-                met, grad_values, memory_grads, *output_got
+            met, rest_home, output_keep, output_met, table = tie(
+                met, rest_home, output_keep, output_met, table
             )
         carry = (grad_kv[away + 1].astype(f32) + met.astype(f32)).astype(bf16)
     if back == 0:
+        output_own, output_got = chip_hop(output_keep, output_met)
         grad_values = value_grads(1, turns, table, dense, grad_values)
-    output_stay, output_got = second_hop(output_stay, output_got)
-    output = (hidden_one + last_hop(output_stay, output_got)).astype(bf16)
-
-    def columns_home(cut, *splits):
-        home = jnp.moveaxis(swap(cut.reshape(TP, rows_w, -1), "tp"), 0, 1).astype(f32)
-        return jnp.split(home, splits, axis=2)
-
-    query_home, gate_home = columns_home(memory_grads[:, :rest_width], QHALF)
-    query_home = query_home.reshape(rows_w, -1)
-    gate_home = gate_home.reshape(rows_w, -1)
     grad_projected = jnp.concatenate([grad_q, carry], axis=1)
-    grad_projected, output, query_home, gate_home = tie(
-        grad_projected, output, query_home, gate_home
-    )
-
-    stay, got = first_hop(*sum_back_start(grad_projected, weight_qkv, NT, rows))
-    late_grads = mm(turned_one, grad_projected).reshape(groups, TP * rows_w, 3 * LANES)
-    attn_rows = mm(attended_low, grad_branch, TN).reshape(groups, TP * rows_w, LANES)
-    late_grads = jnp.concatenate([late_grads, attn_rows], axis=2)
-    late_parts = sum_groups_start(late_grads, groups, group_index)
-    got_0, got_1, *late_parts = tie(*got, *late_parts)
-    stay, got = second_hop(stay, (got_0, got_1))
-    late_grads = sum(part.astype(f32) for part in late_parts).astype(bf16)
-    got_0, got_1, late_grads = tie(*got, late_grads)
-    weighted_one = last_hop(stay, (got_0, got_1))
+
+    late_grads = mm(turned_one, grad_projected).astype(bf16)
+    grad_projected, late_grads = tie(grad_projected, late_grads)
+    qkv_home = swap(late_grads.reshape(devices, rows_w, 3 * LANES), ALL)
+    keep, send = two_products(grad_projected, weight_qkv, NT, rows)
+    sums = keep.astype(f32) + across(send, 1).astype(f32)
+    sums, rest_home, memory_grads, *attn_rows = tie(sums, rest_home, memory_grads, *attn_rows)
+    own, got = chip_send(sums)
+    attn_rows = sum(part.astype(f32) for part in attn_rows).astype(bf16)
+    row_sums = memory_grads[:, rest_width:].reshape(2, rows_w, width)
+    row_home = jnp.concatenate([attn_rows[None], row_sums])
+    row_home = lax.ppermute(row_home, ALL, from_turned)
+    weighted_one = last_hop(own, got)
     grad_inputs = grad_hidden + norm_back(inputs_wide, norm_scale(inputs_wide), weighted_one)
-    qkv_home = columns_home(late_grads[:, : 3 * LANES])[0]
-    qkv_home = jnp.moveaxis(qkv_home.reshape(rows_w, TP, 3, LANES), 1, 2).reshape(rows_w, -1)
-    row_sums = memory_grads[:, rest_width:].reshape(2, rows_w, width)
-    row_home = jnp.concatenate([late_grads[:, 3 * LANES :].reshape(1, rows_w, width), row_sums])
-    row_home = lax.ppermute(row_home, ALL, from_turned).astype(f32)
-    grad_attn_gain = jnp.sum(qkv_home * attn_qkv.astype(f32), axis=1)
-    grad_memory_gain = jnp.sum(query_home * memory_query.astype(f32), axis=1) + jnp.sum(
-        gate_home * memory_gate.astype(f32), axis=1
-    )
+    output = (hidden_one + last_hop(output_own, output_got)).astype(bf16)
+    row_home = row_home.astype(f32)
+    splits = ((QHALF, QHALF, 0), (LANES, LANES, 0))
+    grad_query_home, grad_gate_home, grad_memory_gain = shard_grads(
+        rest_home, gain_two, splits, memory_query, memory_gate
+    )
+    splits = tuple((LANES, LANES, part * width) for part in range(3))
+    grad_qkv_home, grad_attn_gain = shard_grads(qkv_home, gain_one, splits, attn_qkv)
     return (
         output,
         grad_inputs,
-        grad_attn_gain,
-        qkv_home * gain_one,
+        grad_attn_gain.reshape(-1),
+        grad_qkv_home,
         row_home[0],
-        grad_memory_gain,
-        query_home * gain_two,
+        grad_memory_gain.reshape(-1),
+        grad_query_home,
         row_home[2].reshape(sub_keys.shape),
-        gate_home * gain_two,
+        grad_gate_home,
         row_home[1],
         grad_values,
     )

time: 550 us -> 534 us (0.971)
  the two profiles are of different devices: /device:TPU:1 before, /device:TPU:0 now
where the time goes in v3:
time: 534 us; the launch traced here: 530 us
  Pallas kernels  168 us (31%)
  starting transfers between devices  119 us (22%)
  waiting for transfers between devices  91.1 us (17%)
  other arithmetic  53.2 us (10%)
  local copies, waits for them, and re-layouts  33.1 us (6%)
  blocking collectives  28.9 us (5%)
  matrix products  20.5 us (4%)
  between operations  16.1 us (3%)
    ppermute x42, waiting for transfers between devices, across(): return lax.ppermute(array, 'tp', [(at, at ^ distance) for at in range(TP)])  52.7 us
    pallas_call x4, Pallas kernels, row_dots(): pl.pallas_call(lambda *refs: dots_kernel(rows, subs, outer, *refs), grid=...  44.3 us
    pallas_call x2, Pallas kernels, spread_weights(): pl.pallas_call(lambda *refs: spread_kernel(rows, subs, outer, *refs), gri...  41.6 us
    ppermute x42, starting transfers between devices, across(): return lax.ppermute(array, 'tp', [(at, at ^ distance) for at in range(TP)])  41.6 us
    all_to_all x6, starting transfers between devices, swap(): return lax.all_to_all(array, axes, split_axis=0, concat_axis=0, tiled=True)  33.6 us
    pallas_call x2, Pallas kernels, value_grads(): pl.pallas_call(value_grads_kernel, grid=(steps,), in_specs=in_specs, out_...  30.4 us
    all_to_all x2, blocking collectives, swap(): return lax.all_to_all(array, axes, split_axis=0, concat_axis=0, tiled=True)  28.9 us
    dot_general x11, matrix products, mm(): return lax.dot_general(left, right, dims, preferred_element_type=f32)  19.6 us
  transfers between devices with their start and end apart: 71, of which 26 were waited for; matrix products, arithmetic and copies ran while one was open for 14% of the time, Pallas kernels for 28%

profile of v3, /device:TPU:0, one launch (start us, length us, event | category | flops | bytes accessed | tf_op | source)
XLA Modules:
  0.0 530.3 jit_solution(17886080375830322398)
XLA Ops:
  15.3 6.3 %all-to-all-start = ((bf16[32,32,384]{2,1,0:T(8,128)(2,1)}), bf16[32,32,384]{2,1,0:T(8,128)(2,1)S(1)}, u32[]{:S(2)}, u32[]{:S(2)}) async-start(bf16[32,32,384]{2,1,0:T(8,128)(2,1)} %bitcast.14), calls=%async_computation | async-start | bytes 1572864 | tf_op jit(solution)/shard_map/all_to_all | solution.py:704
  39.4 7.6 %all-to-all-done = bf16[32,32,384]{2,1,0:T(8,128)(2,1)S(1)} async-done(((bf16[32,32,384]{2,1,0:T(8,128)(2,1)}), bf16[32,32,384]{2,1,0:T(8,128)(2,1)S(1)}, u32[]{:S(2)}, u32[]{:S(2)}) %all-to-all-start) | async-done | bytes 786464 | tf_op jit(solution)/shard_map/all_to_all | solution.py:704
  62.4 5.3 collective-permute-start.9
  86.9 5.0 attn_fwd.1
  92.0 5.4 %collective-permute-start.13 = (bf16[32,1024]{1,0:T(8,128)(2,1)S(1)}, bf16[32,1024]{1,0:T(8,128)(2,1)S(1)}, u32[]{:S(2)}, u32[]{:S(2)}) collective-permute-start(bf16[32,1024]{1,0:T(8,128)(2,1)S(1)} %get-tuple-element.373), channel_id=1, source_target_pairs={{0,24},{8,0},{16,8},{24,16},{1,25},{9,1},{17,9},{25,17},{2,26},{10... | collective-permute-start | bytes 196616 | tf_op jit(solution)/shard_map/ppermute | solution.py:820
  113.1 6.5 %collective-permute-done.17 = bf16[128,1024]{1,0:T(8,128)(2,1)S(1)} collective-permute-done((bf16[128,1024]{1,0:T(8,128)(2,1)S(1)}, bf16[128,1024]{1,0:T(8,128)(2,1)S(1)}, u32[]{:S(2)}, u32[]{:S(2)}) %collective-permute-start.17) | collective-permute-done | bytes 262176 | tf_op jit(solution)/shard_map/ppermute | solution.py:712
  134.2 5.6 %collective-permute-done.21 = bf16[128,1024]{1,0:T(8,128)(2,1)S(1)} collective-permute-done((bf16[128,1024]{1,0:T(8,128)(2,1)S(1)}, bf16[128,1024]{1,0:T(8,128)(2,1)S(1)}, u32[]{:S(2)}, u32[]{:S(2)}) %collective-permute-start.21) | collective-permute-done | bytes 262176 | tf_op jit(solution)/shard_map/ppermute | solution.py:712
  156.9 13.5 %all-to-all-start.2 = ((f32[8,32,128]{2,1,0:T(8,128)}), f32[8,32,128]{2,1,0:T(8,128)S(1)}, u32[]{:S(2)}, u32[]{:S(2)}) async-start(f32[8,32,128]{2,1,0:T(8,128)} %bitcast_bitcast_fusion), calls=%async_computation.2 | async-start | bytes 262144 | tf_op jit(solution)/shard_map/all_to_all | solution.py:704
  170.5 5.2 all-to-all-done.2.picked_ref
  178.3 17.6 %all_to_all.44 = bf16[32,4,1024]{2,1,0:T(4,128)(2,1)S(1)} all-to-all(bf16[32,4,1024]{2,1,0:T(4,128)(2,1)S(1)} %reshape.410), channel_id=1, replica_groups=mesh['head'=4,'blk'=8] {'head','blk'}, dimensions={0} | all-to-all | bytes 524288 | tf_op jit(solution)/shard_map/all_to_all | solution.py:704
  198.7 20.8 %spread_weights.2 = (bf16[4,1024,2048]{2,1,0:T(8,128)(2,1)}, bf16[4,4,1,4,128,128]{5,4,3,2,1,0:T(8,128)(2,1)S(1)}, bf16[4,4,1,4,128,128]{5,4,3,2,1,0:T(8,128)(2,1)S(1)}) custom-call(s32[1]{0:T(128)} %bitcast.2.refs_1_.refs_0_, s32[4,8,1,1024]{3,2,1,0:T(1,128)S(1)} %get-tuple-element.363.refs_1_.refs_0_, ...), custom_call_target="tpu_custom_call" | custom-call | bytes 79644448 | tf_op jit(solution)/shard_map/spread_weights/pallas_call | solution.py:433
  219.4 20.9 %spread_weights.3 = (bf16[4,1024,2048]{2,1,0:T(8,128)(2,1)}, bf16[4,4,1,4,128,128]{5,4,3,2,1,0:T(8,128)(2,1)S(1)}, bf16[4,4,1,4,128,128]{5,4,3,2,1,0:T(8,128)(2,1)}) custom-call(s32[1]{0:T(128)} %bitcast.2.refs_1_.refs_0_, s32[4,8,1,1024]{3,2,1,0:T(1,128)S(1)} %get-tuple-element.363.refs_1_.refs_0_, ...), custom_call_target="tpu_custom_call", output_to_operand_aliasing={{0}: (6, {})} | custom-call | bytes 79644448 | tf_op jit(solution)/shard_map/spread_weights/pallas_call | solution.py:433
  250.3 10.9 %row_dots.4 = (f32[1,8,1,1024]{3,2,1,0:T(1,128)S(1)}, bf16[4,1024,1024]{2,1,0:T(8,128)(2,1)S(1)}) custom-call(s32[4,8,1,1024]{3,2,1,0:T(1,128)S(1)} %get-tuple-element.363.refs_1_.refs_0_, s32[4,8,1,1024]{3,2,1,0:T(1,128)S(1)} %get-tuple-element.362.refs_2_.refs_1_, s32[4,8,1,1024]{3,2,1,0:T(1,128)S(1)} %get-tuple-element.361.refs_3_.refs_2_, ...), custom_call_target="tpu_custom_call" | custom-call | bytes 39822224 | tf_op jit(solution)/shard_map/row_dots/pallas_call | solution.py:512
  264.5 11.2 %row_dots.5 = (f32[1,8,1,1024]{3,2,1,0:T(1,128)S(1)}, bf16[4,1024,1024]{2,1,0:T(8,128)(2,1)S(1)}) custom-call(s32[4,8,1,1024]{3,2,1,0:T(1,128)S(1)} %get-tuple-element.363.refs_1_.refs_0_, s32[4,8,1,1024]{3,2,1,0:T(1,128)S(1)} %get-tuple-element.362.refs_2_.refs_1_, ...), custom_call_target="tpu_custom_call", output_to_operand_aliasing={{1}: (5, {})} | custom-call | bytes 39822224 | tf_op jit(solution)/shard_map/row_dots/pallas_call | solution.py:512
  279.6 10.9 %row_dots.6 = (f32[1,8,1,1024]{3,2,1,0:T(1,128)S(1)}, bf16[4,1024,1024]{2,1,0:T(8,128)(2,1)S(1)}) custom-call(s32[4,8,1,1024]{3,2,1,0:T(1,128)S(1)} %get-tuple-element.363.refs_1_.refs_0_, s32[4,8,1,1024]{3,2,1,0:T(1,128)S(1)} %get-tuple-element.362.refs_2_.refs_1_, ...), custom_call_target="tpu_custom_call", output_to_operand_aliasing={{1}: (5, {})} | custom-call | bytes 39822224 | tf_op jit(solution)/shard_map/row_dots/pallas_call | solution.py:512
  294.1 11.3 %row_dots.7 = (f32[1,8,1,1024]{3,2,1,0:T(1,128)S(1)}, bf16[4,1024,1024]{2,1,0:T(8,128)(2,1)S(1)}) custom-call(s32[4,8,1,1024]{3,2,1,0:T(1,128)S(1)} %get-tuple-element.363.refs_1_.refs_0_, s32[4,8,1,1024]{3,2,1,0:T(1,128)S(1)} %get-tuple-element.362.refs_2_.refs_1_, ...), custom_call_target="tpu_custom_call", output_to_operand_aliasing={{1}: (5, {})} | custom-call | bytes 39822224 | tf_op jit(solution)/shard_map/row_dots/pallas_call | solution.py:512
  322.8 15.1 %value_grads.2.refs_0_ = f32[2048,1024]{1,0:T(8,128)} custom-call(bf16[4096,2048]{1,0:T(8,128)(2,1)} %bitcast.317, bf16[4096,1024]{1,0:T(8,128)(2,1)} %bitcast.294), custom_call_target="tpu_custom_call" | custom-call | bytes 52500000 | tf_op jit(solution)/shard_map/value_grads/pallas_call | solution.py:551
  341.8 5.1 pick_grads.1
  356.4 5.6 %unpick_scores.1 = (bf16[256,1024]{1,0:T(8,128)(2,1)S(1)}, bf16[1024,512]{1,0:T(8,128)(2,1)S(1)}) custom-call(f32[32,1024]{1,0:T(8,128)S(1)} %copy_bitcast_fusion.1.grad_ref, s32[32,1024]{1,0:T(8,128)S(1)} %copy-done.36, bf16[256,512]{1,0:T(8,128)(2,1)S(1)} %copy-done.20), custom_call_target="tpu_custom_call" | custom-call | bytes 19911112 | tf_op jit(solution)/shard_map/unpick_scores/pallas_call | solution.py:607
  411.1 6.5 %attn_bwd.1 = (bf16[1024,128]{1,0:T(8,128)(2,1)S(1)}, bf16[1024,256]{1,0:T(8,128)(2,1)S(1)}, bf16[1024,256]{1,0:T(8,128)(2,1)S(1)}, bf16[1024,256]{1,0:T(8,128)(2,1)S(1)}) custom-call(s32[2]{0:T(128)S(1)} %slice.136.refs_0_, s32[1]{0:T(128)} %bitcast.2.refs_1_.refs_0_, bf16[1024,128]{1,0:T(8,128)(2,1)S(1)} %copy-done.18, bf16[3072,256]{1,0:T(8,128)(2,1)S(1)} %copy-done.8, ...), custom_call_target="tpu_custom_call" | custom-call | bytes 53760000 | tf_op jit(solution)/shard_map/attn_bwd/pallas_call | solution.py:234
  417.6 5.4 %reduce-scatter.2.cloned.1.call-done = bf16[256,896]{0,1:T(8,128)(2,1)} async-done(((bf16[1024,896]{0,1:T(8,128)(2,1)}), bf16[256,896]{0,1:T(8,128)(2,1)}) %reduce-scatter.2.cloned.1.call-update) | async-done | bytes 458768 | tf_op jit(solution)/shard_map/reduce_scatter | solution.py:1129
  426.2 11.3 %all_to_all.45.sums_ref = bf16[8,32,640]{2,1,0:T(8,128)(2,1)S(1)} all-to-all(bf16[8,32,640]{2,1,0:T(8,128)(2,1)} %bitcast.338), channel_id=1, replica_groups=mesh['head'=4,'blk'=8] {'blk'}, dimensions={0} | all-to-all | bytes 655360 | tf_op jit(solution)/shard_map/all_to_all | solution.py:704
  448.2 15.2 %value_grads.3 = f32[2048,1024]{1,0:T(8,128)} custom-call(bf16[4096,2048]{1,0:T(8,128)(2,1)} %bitcast.318, bf16[4096,1024]{1,0:T(8,128)(2,1)} %bitcast.295, f32[2048,1024]{1,0:T(8,128)} %value_grads.2.refs_0_), custom_call_target="tpu_custom_call", output_to_operand_aliasing={{}: (2, {})} | custom-call | bytes 52500000 | tf_op jit(solution)/shard_map/value_grads/pallas_call | solution.py:551
  504.2 8.9 %collective-permute-done.59 = bf16[128,1024]{1,0:T(8,128)(2,1)} collective-permute-done((bf16[128,1024]{1,0:T(8,128)(2,1)}, bf16[128,1024]{1,0:T(8,128)(2,1)}, u32[]{:S(2)}, u32[]{:S(2)}) %collective-permute-start.59) | collective-permute-done | bytes 262176 | tf_op jit(solution)/shard_map/ppermute | solution.py:712
  (455 shorter events, 277.2 us)
Async XLA Ops:
  15.3 31.6 %all-to-all-start = ((bf16[32,32,384]{2,1,0:T(8,128)(2,1)}), bf16[32,32,384]{2,1,0:T(8,128)(2,1)S(1)}, u32[]{:S(2)}, u32[]{:S(2)}) async-start(bf16[32,32,384]{2,1,0:T(8,128)(2,1)} %bitcast.14), calls=%async_computation | async-start | bytes 1572864 | tf_op jit(solution)/shard_map/all_to_all | solution.py:704
  28.8 29.5 %collective-permute-start.6 = (bf16[128,1024]{1,0:T(8,128)(2,1)}, bf16[128,1024]{1,0:T(8,128)(2,1)}, u32[]{:S(2)}, u32[]{:S(2)}) collective-permute-start(bf16[128,1024]{1,0:T(8,128)(2,1)} %param.27), channel_id=1, source_target_pairs={{0,2},{1,3},{2,0},{3,1},{4,6},{5,7},{6,4},{7,5},{8,10},{9,11},{10,... | collective-permute-start | bytes 786440 | tf_op jit(solution)/shard_map/ppermute | solution.py:712
  30.1 28.2 %collective-permute-start.7 = (bf16[128,1024]{1,0:T(8,128)(2,1)}, bf16[128,1024]{1,0:T(8,128)(2,1)}, u32[]{:S(2)}, u32[]{:S(2)}) collective-permute-start(bf16[128,1024]{1,0:T(8,128)(2,1)} %param.27), channel_id=1, source_target_pairs={{0,4},{1,5},{2,6},{3,7},{4,0},{5,1},{6,2},{7,3},{8,12},{9,13},{10,... | collective-permute-start | bytes 786440 | tf_op jit(solution)/shard_map/ppermute | solution.py:712
  31.5 26.7 %collective-permute-start.8 = (bf16[128,1024]{1,0:T(8,128)(2,1)}, bf16[128,1024]{1,0:T(8,128)(2,1)}, u32[]{:S(2)}, u32[]{:S(2)}) collective-permute-start(bf16[128,1024]{1,0:T(8,128)(2,1)} %param.27), channel_id=1, source_target_pairs={{0,6},{1,7},{2,4},{3,5},{4,2},{5,3},{6,0},{7,1},{8,14},{9,15},{10,... | collective-permute-start | bytes 786440 | tf_op jit(solution)/shard_map/ppermute | solution.py:712
  32.3 26.0 %collective-permute-start.5 = (bf16[3,32,1024]{2,1,0:T(8,128)(2,1)}, bf16[3,32,1024]{2,1,0:T(8,128)(2,1)}, u32[]{:S(2)}, u32[]{:S(2)}) collective-permute-start(bf16[3,32,1024]{2,1,0:T(8,128)(2,1)} %pad_maximum_fusion.13), channel_id=1, source_target_pairs={{0,0},{4,1},{8,2},{12,3},{16,4},{20,5},{24,6},{28,7},{1,8},{5,9},{... | collective-permute-start | bytes 589832 | tf_op jit(solution)/shard_map/ppermute | solution.py:891
  53.6 22.8 %all-to-all-start.1 = ((bf16[8,32,768]{2,1,0:T(8,128)(2,1)}), bf16[8,32,768]{2,1,0:T(8,128)(2,1)S(1)}, u32[]{:S(2)}, u32[]{:S(2)}) async-start(bf16[8,32,768]{2,1,0:T(8,128)(2,1)} %copy.167), calls=%async_computation.1 | async-start | bytes 786432 | tf_op jit(solution)/shard_map/all_to_all | solution.py:704
  57.4 187.0 %all-gather.2.cloned.1.call-start = ((), (), s32[]{:S(2)}) async-start(), calls=%async_computation.9 | async-start | bytes 8650752 | tf_op jit(solution)/shard_map/all_gather | solution.py:708
  69.9 22.0 %collective-permute-start.10 = (bf16[4,128,1024]{2,1,0:T(8,128)(2,1)}, bf16[4,128,1024]{2,1,0:T(8,128)(2,1)}, u32[]{:S(2)}, u32[]{:S(2)}) collective-permute-start(bf16[4,128,1024]{2,1,0:T(8,128)(2,1)} %get-tuple-element.357), channel_id=1, source_target_pairs={{0,1},{1,0},{2,3},{3,2},{4,5},{5,4},{6,7},{7,6},{8,9},{9,8},{10,11... | collective-permute-start | bytes 3145736 | tf_op jit(solution)/shard_map/ppermute | solution.py:712
  80.7 23.0 %collective-permute-start.14 = (bf16[256,640]{1,0:T(8,128)(2,1)S(1)}, bf16[256,640]{1,0:T(8,128)(2,1)S(1)}, u32[]{:S(2)}, u32[]{:S(2)}) collective-permute-start(bf16[256,640]{1,0:T(8,128)(2,1)S(1)} %bitcast.334), channel_id=1, source_target_pairs={{0,8},{8,16},{16,24},{24,0},{1,9},{9,17},{17,25},{25,1},{2,10},{10... | collective-permute-start | bytes 983048 | tf_op jit(solution)/shard_map/ppermute | solution.py:820
  219.4 21.3 %collective-permute-start.28 = (bf16[4,4,512,128]{3,2,1,0:T(8,128)(2,1)S(1)}, bf16[4,4,512,128]{3,2,1,0:T(8,128)(2,1)S(1)}, u32[]{:S(2)}, u32[]{:S(2)}) collective-permute-start(bf16[4,4,512,128]{3,2,1,0:T(8,128)(2,1)S(1)} %bitcast.316), channel_id=1, source_target_pairs={{0,1},{1,0},{2,3},{3,2},{4,5},{5,4},{6,7},{7,6},{8,9},{9,8},{10,11... | collective-permute-start | bytes 6291464 | tf_op jit(solution)/shard_map/ppermute | solution.py:712
  244.4 31.3 %collective-permute-start.30 = (bf16[2,4,256,128]{3,2,1,0:T(8,128)(2,1)}, bf16[2,4,256,128]{3,2,1,0:T(8,128)(2,1)S(1)}, u32[]{:S(2)}, u32[]{:S(2)}) collective-permute-start(bf16[2,4,256,128]{3,2,1,0:T(8,128)(2,1)} %copy-done.42), channel_id=1, source_target_pairs={{0,2},{1,3},{2,0},{3,1},{4,6},{5,7},{6,4},{7,5},{8,10},{9,11},{10,... | collective-permute-start | bytes 1572872 | tf_op jit(solution)/shard_map/ppermute | solution.py:712
  246.6 29.1 %collective-permute-start.31 = (bf16[2,4,256,128]{3,2,1,0:T(8,128)(2,1)}, bf16[2,4,256,128]{3,2,1,0:T(8,128)(2,1)S(1)}, u32[]{:S(2)}, u32[]{:S(2)}) collective-permute-start(bf16[2,4,256,128]{3,2,1,0:T(8,128)(2,1)} %copy-done.41), channel_id=1, source_target_pairs={{0,4},{1,5},{2,6},{3,7},{4,0},{5,1},{6,2},{7,3},{8,12},{9,13},{10,... | collective-permute-start | bytes 1572872 | tf_op jit(solution)/shard_map/ppermute | solution.py:712
  263.8 26.7 %collective-permute-start.32 = (bf16[2,4,256,128]{3,2,1,0:T(8,128)(2,1)S(1)}, bf16[2,4,256,128]{3,2,1,0:T(8,128)(2,1)S(1)}, u32[]{:S(2)}, u32[]{:S(2)}) collective-permute-start(bf16[2,4,256,128]{3,2,1,0:T(8,128)(2,1)S(1)} %get-tuple-element.238), channel_id=1, source_target_pairs={{0,2},{1,3},{2,0},{3,1},{4,6},{5,7},{6,4},{7,5},{8,10},{9,11},{10,... | collective-permute-start | bytes 1572872 | tf_op jit(solution)/shard_map/ppermute | solution.py:712
  263.9 26.6 %collective-permute-start.33 = (bf16[2,4,256,128]{3,2,1,0:T(8,128)(2,1)S(1)}, bf16[2,4,256,128]{3,2,1,0:T(8,128)(2,1)S(1)}, u32[]{:S(2)}, u32[]{:S(2)}) collective-permute-start(bf16[2,4,256,128]{3,2,1,0:T(8,128)(2,1)S(1)} %get-tuple-element.239), channel_id=1, source_target_pairs={{0,4},{1,5},{2,6},{3,7},{4,0},{5,1},{6,2},{7,3},{8,12},{9,13},{10,... | collective-permute-start | bytes 1572872 | tf_op jit(solution)/shard_map/ppermute | solution.py:712
  313.2 37.8 %collective-permute-start.38 = (bf16[1024,128]{1,0:T(8,128)(2,1)}, bf16[1024,128]{1,0:T(8,128)(2,1)S(1)}, u32[]{:S(2)}, u32[]{:S(2)}) collective-permute-start(bf16[1024,128]{1,0:T(8,128)(2,1)} %get-tuple-element.348), channel_id=1, source_target_pairs={{0,8},{8,16},{16,24},{24,0},{1,9},{9,17},{17,25},{25,1},{2,10},{10... | collective-permute-start | bytes 786440 | tf_op jit(solution)/shard_map/ppermute | solution.py:811
  313.9 37.0 %collective-permute-start.39 = (bf16[1024,128]{1,0:T(8,128)(2,1)}, bf16[1024,128]{1,0:T(8,128)(2,1)S(1)}, u32[]{:S(2)}, u32[]{:S(2)}) collective-permute-start(bf16[1024,128]{1,0:T(8,128)(2,1)} %get-tuple-element.349), channel_id=1, source_target_pairs={{0,16},{8,24},{16,0},{24,8},{1,17},{9,25},{17,1},{25,9},{2,18},{10... | collective-permute-start | bytes 786440 | tf_op jit(solution)/shard_map/ppermute | solution.py:811
  315.1 35.9 %collective-permute-start.40 = (bf16[1024,128]{1,0:T(8,128)(2,1)}, bf16[1024,128]{1,0:T(8,128)(2,1)}, u32[]{:S(2)}, u32[]{:S(2)}) collective-permute-start(bf16[1024,128]{1,0:T(8,128)(2,1)} %get-tuple-element.350), channel_id=1, source_target_pairs={{0,24},{8,0},{16,8},{24,16},{1,25},{9,1},{17,9},{25,17},{2,26},{10... | collective-permute-start | bytes 786440 | tf_op jit(solution)/shard_map/ppermute | solution.py:811
  318.1 23.6 %all-to-all-start.4 = ((f32[32,1,1024]{2,1,0:T(1,128)}), f32[32,1,1024]{2,1,0:T(1,128)S(1)}, u32[]{:S(2)}, u32[]{:S(2)}) async-start(f32[32,1,1024]{2,1,0:T(1,128)} %bitcast.92), calls=%async_computation.4 | async-start | bytes 262144 | tf_op jit(solution)/shard_map/all_to_all | solution.py:704
  350.9 72.1 %reduce-scatter.2.cloned.1.call-start = ((), (), s32[]{:S(2)}) async-start(), calls=%async_computation.10 | async-start | bytes 2293760 | tf_op jit(solution)/shard_map/reduce_scatter | solution.py:1129
  440.1 23.3 %collective-permute-start.51 = (bf16[1024,256]{1,0:T(8,128)(2,1)S(1)}, bf16[1024,256]{1,0:T(8,128)(2,1)S(1)}, u32[]{:S(2)}, u32[]{:S(2)}) collective-permute-start(bf16[1024,256]{1,0:T(8,128)(2,1)S(1)} %add_convert_fusion.1), channel_id=1, source_target_pairs={{8,0},{16,8},{24,16},{9,1},{17,9},{25,17},{10,2},{18,10},{26,18},{... | collective-permute-start | bytes 1572872 | tf_op jit(solution)/shard_map/ppermute | solution.py:717
  479.2 42.4 %all-to-all-start.7 = ((bf16[32,32,384]{2,1,0:T(8,128)(2,1)}), bf16[32,32,384]{2,1,0:T(8,128)(2,1)S(1)}, u32[]{:S(2)}, u32[]{:S(2)}) async-start(bf16[32,32,384]{2,1,0:T(8,128)(2,1)} %bitcast.351), calls=%async_computation.8 | async-start | bytes 1572864 | tf_op jit(solution)/shard_map/all_to_all | solution.py:704
  491.7 21.4 %collective-permute-start.59 = (bf16[128,1024]{1,0:T(8,128)(2,1)}, bf16[128,1024]{1,0:T(8,128)(2,1)}, u32[]{:S(2)}, u32[]{:S(2)}) collective-permute-start(bf16[128,1024]{1,0:T(8,128)(2,1)} %get-tuple-element.337), channel_id=1, source_target_pairs={{0,6},{1,7},{2,4},{3,5},{4,2},{5,3},{6,0},{7,1},{8,14},{9,15},{10,... | collective-permute-start | bytes 786440 | tf_op jit(solution)/shard_map/ppermute | solution.py:712
  496.6 21.4 %collective-permute-start.60 = (bf16[128,1024]{1,0:T(8,128)(2,1)}, bf16[128,1024]{1,0:T(8,128)(2,1)}, u32[]{:S(2)}, u32[]{:S(2)}) collective-permute-start(bf16[128,1024]{1,0:T(8,128)(2,1)} %get-tuple-element.339), channel_id=1, source_target_pairs={{0,2},{1,3},{2,0},{3,1},{4,6},{5,7},{6,4},{7,5},{8,10},{9,11},{10,... | collective-permute-start | bytes 786440 | tf_op jit(solution)/shard_map/ppermute | solution.py:712
  496.6 21.4 %collective-permute-start.61 = (bf16[128,1024]{1,0:T(8,128)(2,1)}, bf16[128,1024]{1,0:T(8,128)(2,1)}, u32[]{:S(2)}, u32[]{:S(2)}) collective-permute-start(bf16[128,1024]{1,0:T(8,128)(2,1)} %get-tuple-element.338), channel_id=1, source_target_pairs={{0,4},{1,5},{2,6},{3,7},{4,0},{5,1},{6,2},{7,3},{8,12},{9,13},{10,... | collective-permute-start | bytes 786440 | tf_op jit(solution)/shard_map/ppermute | solution.py:712
  (129 other events, 1562.8 us)
Sparse Core Ops, SparseCore 0:
  153.5 79.8 all-gather.1
  387.1 35.8 reduce-scatter.1

commit v4 on v3

--- a/solution.py
+++ b/solution.py
@@ -59,34 +59,34 @@
     return jnp.bitwise_xor(place, lax.rem(here * rows, shape[axis]))
 
 
-def key_blocks(step, base, block_q, block_k, low_first_ref):
-    return (
-        low_first_ref[step] // block_k,
-        (base + (step + 1) * block_q - 1) // block_k + 1,
-    )
-
-
-def key_start(turn, span, here, block_k, rows):
+def key_blocks(step, base, span, bounds, block_q, block_k, low_first_ref):
+    first = jnp.maximum(low_first_ref[step], bounds[0] * span) // block_k
+    stop = (base + (step + 1) * block_q - 1) // block_k + 1
+    return first, jnp.minimum(stop, bounds[1] * span // block_k)
+
+
+def key_start(turn, span, here, block_k, rows, skipped):
     per_group = span // block_k
-    group = turn // per_group
+    group = turn // per_group - skipped
     within = turned_block(lax.rem(turn, per_group), here, block_k, rows)
     return pl.multiple_of(group * span + within * block_k, block_k)
 
 
 def attn_fwd_kernel(
-    base, span, rows, block_k, low_first_ref, here_ref, q_ref, kv_ref, low_ref, att_ref, lse_ref, out_ref
+    base, span, rows, block_k, bounds, low_first_ref, here_ref, q_ref, kv_ref, low_ref, *refs
 ):
+    att_ref, lse_ref, out_ref = refs[-3:]
     block_q = q_ref.shape[0]
     step = pl.program_id(0)
     here = here_ref[0]
-    first, stop = key_blocks(step, base, block_q, block_k, low_first_ref)
+    first, stop = key_blocks(step, base, span, bounds, block_q, block_k, low_first_ref)
     queries = head_rows(q_ref[...])
     low = low_ref[...]
     high = base + step * block_q + turned_iota((1, block_q), 1, here, rows)
     inner = turned_iota((block_k, block_q), 0, here, rows)
 
     def visit(turn, carried):
-        start = key_start(turn, span, here, block_k, rows)
+        start = key_start(turn, span, here, block_k, rows, bounds[0])
         keys = kv_ref[pl.ds(start, block_k), :LANES]
         values = kv_ref[pl.ds(start, block_k), LANES:]
         place = turn * block_k + inner
@@ -103,12 +103,20 @@
             out.append((new_max, run_sum, run_acc))
         return tuple(out)
 
-    fresh = (
-        jnp.full((1, block_q), neg_big, f32),
-        jnp.zeros((1, block_q), f32),
-        jnp.zeros((LANES, block_q), f32),
-    )
-    done = lax.fori_loop(first, stop, visit, (fresh, fresh))
+    if len(refs) > 3:
+        near_att = refs[0][...]
+        fresh = tuple(
+            (refs[1][head : head + 1, :], jnp.ones((1, block_q), f32), near_att)
+            for head in range(2)
+        )
+    else:
+        fresh = (
+            jnp.full((1, block_q), neg_big, f32),
+            jnp.zeros((1, block_q), f32),
+            jnp.zeros((LANES, block_q), f32),
+        )
+        fresh = (fresh, fresh)
+    done = lax.fori_loop(first, stop, visit, fresh)
     att_ref[:HD, :] = done[0][2][:HD] / done[0][1]
     att_ref[HD:, :] = done[1][2][HD:] / done[1][1]
     out_ref[...] = jnp.transpose(att_ref[...]).astype(bf16)
@@ -128,20 +136,23 @@
     )
 
 
-def attn_fwd(base, rows, low_first, here, low, queries, keys_values):
+def attn_fwd(base, rows, bounds, low_first, here, low, queries, keys_values, near=()):
     span = queries.shape[0]
     block_q, block_k = 512, 512
     by_row, one_lane, two_lane, by_lane = attn_specs(block_q, rows, span)
+    in_specs = [
+        by_row,
+        pl.BlockSpec(keys_values.shape, lambda i, s, here: (0, 0)),
+        one_lane,
+        by_lane,
+        two_lane,
+    ]
     return pl.pallas_call(
-        lambda *refs: attn_fwd_kernel(base, span, rows, block_k, *refs),
+        lambda *refs: attn_fwd_kernel(base, span, rows, block_k, bounds, *refs),
         grid_spec=pltpu.PrefetchScalarGridSpec(
             num_scalar_prefetch=2,
             grid=(span // block_q,),
-            in_specs=[
-                by_row,
-                pl.BlockSpec(keys_values.shape, lambda i, s, here: (0, 0)),
-                one_lane,
-            ],
+            in_specs=in_specs[: 3 + len(near)],
             out_specs=[by_lane, two_lane, by_row],
         ),
         out_shape=[
@@ -152,7 +163,7 @@
         compiler_params=params(24),
         cost_estimate=lasting(keys_values.shape[0] / 250),
         name="attn_fwd",
-    )(low_first[::block_q], here, queries, keys_values, low[None, :])
+    )(low_first[::block_q], here, queries, keys_values, low[None, :], *near)
 
 
 def attn_bwd_kernel(
@@ -160,6 +171,7 @@
     span,
     rows,
     block_k,
+    bounds,
     low_first_ref,
     here_ref,
     q_ref,
@@ -168,14 +180,16 @@
     lse_ref,
     att_ref,
     grad_ref,
-    dq_ref,
     *refs,
 ):
     dk_ref, dv_ref = refs[-2:]
+    count = bounds[1] - bounds[0]
+    out_refs = refs[-2 - count : -2]
+    dq_ref = refs[-3 - count]
     block_q = q_ref.shape[0]
     step = pl.program_id(0)
     here = here_ref[0]
-    first, stop = key_blocks(step, base, block_q, block_k, low_first_ref)
+    first, stop = key_blocks(step, base, span, bounds, block_q, block_k, low_first_ref)
 
     @pl.when(step == 0)
     def clear():
@@ -194,7 +208,7 @@
     inner = turned_iota((block_k, block_q), 0, here, rows)
 
     def visit(turn, carried):
-        start = key_start(turn, span, here, block_k, rows)
+        start = key_start(turn, span, here, block_k, rows, bounds[0])
         keys = kv_ref[pl.ds(start, block_k), :LANES]
         values = kv_ref[pl.ds(start, block_k), LANES:]
         place = turn * block_k + inner
@@ -217,33 +231,40 @@
     fresh = jnp.zeros((LANES, block_q), f32)
     done = lax.fori_loop(first, stop, visit, (fresh, fresh))
     turned = jnp.concatenate([done[0][:HD], done[1][HD:]], axis=0) * (1.0 / math.sqrt(HD))
-    dq_ref[...] = jnp.transpose(turned).astype(bf16)
+    total = jnp.transpose(turned)
+    if len(refs) > 3 + count:
+        total = total + refs[0][...].astype(f32)
+    dq_ref[...] = total.astype(bf16)
 
     @pl.when(step == span // block_q - 1)
     def leave():
-        for turn, out_ref in enumerate(refs[:-2]):
+        for turn, out_ref in enumerate(out_refs):
             out_ref[:, :LANES] = dk_ref[turn * span : (turn + 1) * span, :].astype(bf16)
             out_ref[:, LANES:] = dv_ref[turn * span : (turn + 1) * span, :].astype(bf16)
 
 
-def attn_bwd(base, rows, low_first, here, low, queries, keys_values, lse, att, grads):
+def attn_bwd(
+    base, rows, bounds, low_first, here, low, queries, keys_values, lse, att, grads, far=()
+):
     span = queries.shape[0]
     block_q, block_k = 512, 512
     reach = keys_values.shape[0]
     by_row, one_lane, two_lane, by_lane = attn_specs(block_q, rows, span)
+    in_specs = [
+        by_row,
+        pl.BlockSpec(keys_values.shape, lambda i, s, here: (0, 0)),
+        one_lane,
+        two_lane,
+        by_lane,
+        by_row,
+        by_row,
+    ]
     return pl.pallas_call(
-        lambda *refs: attn_bwd_kernel(base, span, rows, block_k, *refs),
+        lambda *refs: attn_bwd_kernel(base, span, rows, block_k, bounds, *refs),
         grid_spec=pltpu.PrefetchScalarGridSpec(
             num_scalar_prefetch=2,
             grid=(span // block_q,),
-            in_specs=[
-                by_row,
-                pl.BlockSpec(keys_values.shape, lambda i, s, here: (0, 0)),
-                one_lane,
-                two_lane,
-                by_lane,
-                by_row,
-            ],
+            in_specs=in_specs[: 6 + len(far)],
             out_specs=[by_row]
             + [pl.BlockSpec((span, 2 * LANES), lambda i, s, here: (0, 0))] * (reach // span),
             scratch_shapes=[pltpu.VMEM((reach, LANES), f32), pltpu.VMEM((reach, LANES), f32)],
@@ -253,7 +274,7 @@
         compiler_params=params(32),
         cost_estimate=lasting(keys_values.shape[0] / 200),
         name="attn_bwd",
-    )(low_first[::block_q], here, queries, keys_values, low[None, :], lse, att, grads)
+    )(low_first[::block_q], here, queries, keys_values, low[None, :], lse, att, grads, *far)
 
 
 def hits(count, row):
@@ -536,12 +557,12 @@
 def value_grads(turn, turns, table, dense, sums):
     tokens, own_rows = table.shape
     width = dense.shape[1]
-    block = min(512, own_rows // turns)
+    block = min(256, own_rows // turns)
     steps = own_rows // turns // block
     operands = [table, dense]
     in_specs = [
         pl.BlockSpec((tokens, block), lambda i: (0, turn * steps + i)),
-        pl.BlockSpec(dense.shape, lambda i: (0, 0)),
+        pl.BlockSpec(dense.shape, lambda i: (0, 0), pipeline_mode=pl.Buffered(1)),
     ]
     aliases = {}
     if sums is not None:
@@ -555,7 +576,7 @@
         out_specs=pl.BlockSpec((block, width), lambda i: (turn * steps + i, 0)),
         out_shape=jax.ShapeDtypeStruct((own_rows, width), f32),
         input_output_aliases=aliases,
-        compiler_params=params(48 if dense.size <= 2**23 else 58),
+        compiler_params=params(30 if dense.size <= 2**23 else 58),
         cost_estimate=lasting(15 * 2 / turns),
         name="value_grads",
     )(*operands)
@@ -827,6 +848,12 @@
         source = lax.rem(group_index + groups - away, groups)
         result = lax.dynamic_update_index_in_dim(result, piece, source, 0)
     return result
+
+
+def rows_home(attn_parts, memory_sums, pairs):
+    attn_sums = sum(part.astype(f32) for part in attn_parts).astype(bf16)
+    memory_sums = memory_sums.reshape((2,) + attn_sums.shape)
+    return lax.ppermute(jnp.concatenate([attn_sums[None], memory_sums]), ALL, pairs)
 
 
 def tie(*arrays):
@@ -980,8 +1007,12 @@
     low_first = lowest(span_range)
     low = lowest(jnp.bitwise_xor(span_range, here * rows))
     attended, lse, attended_low = attn_fwd(
-        base, rows, low_first, here_word, low, queries, keys_values
-    )
+        base, rows, (0, back + 1), low_first, here_word, low, queries, keys_values
+    )
+    split = back > 1
+    near_bounds = (1 if split else 0, back + 1)
+    far_kv = keys_values[:span]
+    near_kv = keys_values[near_bounds[0] * span :]
     attn_shifts = {away: shift(row_cut[0], groups, away) for away in range(1, groups)}
     attended_low, group_cot, rest_rows, *shifted = tie(
         attended_low, group_cot, rest_rows, *attn_shifts.values(), *rest_shifts.values()
@@ -1137,32 +1168,43 @@
     output_met = across(output_met, 1)
     grad_branch = gather_cores(own_branch, near_branch)
     grad_attended = mm(grad_branch, weight_attn, NT).astype(bf16)
-    grad_q, *grad_kv = attn_bwd(
-        base, rows, low_first, here_word, low, queries, keys_values, lse, attended, grad_attended
-    )
-    output_keep, output_met, table, memory_grads, *grad_kv = tie(
-        output_keep, output_met, table, memory_grads, *grad_kv
-    )
-
-    rest_home = swap(memory_grads[:, :rest_width].reshape(TP, rows_w, -1), "tp")
-    attended_low, unused = tie(attended_low, grad_kv[0])
+    through = (low_first, here_word, low, queries)
+    results = (lse, attended, grad_attended)
+    far = far_grads = ()
+    if split:
+        far_grad_q, *far_grads = attn_bwd(base, rows, (0, 1), *through, far_kv, *results)
+        far = (far_grad_q,)
+        output_keep, output_met, far_grads[0] = tie(output_keep, output_met, far_grads[0])
+        output_own, output_got = chip_hop(output_keep, output_met)
+        attended_low, far_grads[0] = tie(attended_low, far_grads[0])
     attn_rows = mm(attended_low, grad_branch, TN).astype(bf16).reshape(groups, rows_w, width)
     attn_rows = sum_groups_start(attn_rows, groups, group_index)
-    output_got = None
+    grad_q, *grad_kv = attn_bwd(base, rows, near_bounds, *through, near_kv, *results, far)
+    grad_kv = [*far_grads, *grad_kv]
+    if not split:
+        output_own, output_got = chip_hop(output_keep, output_met)
+    output_own, table, memory_grads, *near_grads = tie(
+        output_own, table, memory_grads, *grad_kv[len(far_grads) :]
+    )
+    grad_kv = [*far_grads, *near_grads]
+
+    row_home = None
     carry = grad_kv[0]
     for away in range(back):
         met = onward(carry, groups, -1)
         if away == back - 1:
-            output_own, output_got = chip_hop(output_keep, output_met)
+            rest_home = swap(memory_grads[:, :rest_width].reshape(TP, rows_w, -1), "tp")
             grad_values = value_grads(1, turns, table, dense, grad_values)
-            met, grad_values, *output_got = tie(met, grad_values, *output_got)
+            row_home = rows_home(attn_rows, memory_grads[:, rest_width:], from_turned)
+            met, rest_home, row_home, grad_values, *output_got = tie(
+                met, rest_home, row_home, grad_values, *output_got
+            )
         if away == 0:
-            met, rest_home, output_keep, output_met, table = tie(
-                met, rest_home, output_keep, output_met, table
-            )
+            met, memory_grads, table, *attn_rows = tie(met, memory_grads, table, *attn_rows)
         carry = (grad_kv[away + 1].astype(f32) + met.astype(f32)).astype(bf16)
     if back == 0:
-        output_own, output_got = chip_hop(output_keep, output_met)
+        rest_home = swap(memory_grads[:, :rest_width].reshape(TP, rows_w, -1), "tp")
+        row_home = rows_home(attn_rows, memory_grads[:, rest_width:], from_turned)
         grad_values = value_grads(1, turns, table, dense, grad_values)
     grad_projected = jnp.concatenate([grad_q, carry], axis=1)
 
@@ -1171,12 +1213,7 @@
     qkv_home = swap(late_grads.reshape(devices, rows_w, 3 * LANES), ALL)
     keep, send = two_products(grad_projected, weight_qkv, NT, rows)
     sums = keep.astype(f32) + across(send, 1).astype(f32)
-    sums, rest_home, memory_grads, *attn_rows = tie(sums, rest_home, memory_grads, *attn_rows)
     own, got = chip_send(sums)
-    attn_rows = sum(part.astype(f32) for part in attn_rows).astype(bf16)
-    row_sums = memory_grads[:, rest_width:].reshape(2, rows_w, width)
-    row_home = jnp.concatenate([attn_rows[None], row_sums])
-    row_home = lax.ppermute(row_home, ALL, from_turned)
     weighted_one = last_hop(own, got)
     grad_inputs = grad_hidden + norm_back(inputs_wide, norm_scale(inputs_wide), weighted_one)
     output = (hidden_one + last_hop(output_own, output_got)).astype(bf16)

time: 534 us -> 513 us (0.961); the launches traced: 530 us -> 503 us
  blocking collectives: 28.9 us -> 12.6 us
  other arithmetic: 53.2 us -> 45.1 us
  local copies, waits for them, and re-layouts: 33.1 us -> 41.1 us
    all_to_all x2 -> x1, blocking collectives: 28.9 us -> 12.6 us  [swap(): return lax.all_to_all(array, axes, split_axis=0, concat_axis=0, tiled=True)]
    ppermute x42, starting transfers between devices: 41.6 us -> 47.9 us  [across(): return lax.ppermute(array, 'tp', [(at, at ^ distance) for at in range(TP)])]
    pallas_call x2, Pallas kernels: 30.4 us -> 24.1 us  [value_grads(): pl.pallas_call(value_grads_kernel, grid=(steps,), in_specs=in_specs, out_...]
    all_to_all x6 -> x7, starting transfers between devices: 33.6 us -> 27.5 us  [swap(): return lax.all_to_all(array, axes, split_axis=0, concat_axis=0, tiled=True)]
    unnamed x164 -> x154, local copies, waits for them, and re-layouts: 16.7 us -> 22.4 us
    all_to_all x6 -> x7, waiting for transfers between devices: 19.5 us -> 21.2 us  [swap(): return lax.all_to_all(array, axes, split_axis=0, concat_axis=0, tiled=True)]
    pallas_call x2 -> x3, Pallas kernels: 11.5 us -> 13 us  [the longest x2 7.93 us: attn_bwd(): pl.pallas_call(lambda *refs: attn_bwd_kernel(base, span, rows, block_k, b...]
  transfers between devices with their start and end apart: 71 -> 72, of which waited for: 26 -> 27; matrix products, arithmetic and copies ran while one was open for 14% -> 14% of each run, Pallas kernels for 28% -> 29%
where the time goes in v4:
time: 513 us; the launch traced here: 503 us
  Pallas kernels  164 us (32%)
  starting transfers between devices  115 us (22%)
  waiting for transfers between devices  89.7 us (17%)
  other arithmetic  45.1 us (9%)
  local copies, waits for them, and re-layouts  41.1 us (8%)
  matrix products  18.9 us (4%)
  between operations  16 us (3%)
  blocking collectives  12.6 us (2%)
    ppermute x42, waiting for transfers between devices, across(): return lax.ppermute(array, 'tp', [(at, at ^ distance) for at in range(TP)])  51.4 us
    ppermute x42, starting transfers between devices, across(): return lax.ppermute(array, 'tp', [(at, at ^ distance) for at in range(TP)])  47.9 us
    pallas_call x4, Pallas kernels, row_dots(): pl.pallas_call(lambda *refs: dots_kernel(rows, subs, outer, *refs), grid=...  43.7 us
    pallas_call x2, Pallas kernels, spread_weights(): pl.pallas_call(lambda *refs: spread_kernel(rows, subs, outer, *refs), gri...  41.6 us
    all_to_all x7, starting transfers between devices, swap(): return lax.all_to_all(array, axes, split_axis=0, concat_axis=0, tiled=True)  27.5 us
    pallas_call x2, Pallas kernels, value_grads(): pl.pallas_call(value_grads_kernel, grid=(steps,), in_specs=in_specs, out_...  24.1 us
    unnamed x154, local copies, waits for them, and re-layouts  22.4 us
    all_to_all x7, waiting for transfers between devices, swap(): return lax.all_to_all(array, axes, split_axis=0, concat_axis=0, tiled=True)  21.2 us
  transfers between devices with their start and end apart: 72, of which 27 were waited for; matrix products, arithmetic and copies ran while one was open for 14% of the time, Pallas kernels for 29%

profile of v4, /device:TPU:0, one launch (start us, length us, event | category | flops | bytes accessed | tf_op | source)
XLA Modules:
  0.0 502.6 jit_solution(18444355037586146673)
XLA Ops:
  15.3 6.3 %all-to-all-start = ((bf16[32,32,384]{2,1,0:T(8,128)(2,1)}), bf16[32,32,384]{2,1,0:T(8,128)(2,1)S(1)}, u32[]{:S(2)}, u32[]{:S(2)}) async-start(bf16[32,32,384]{2,1,0:T(8,128)(2,1)} %bitcast.14), calls=%async_computation | async-start | bytes 1572864 | tf_op jit(solution)/shard_map/all_to_all | solution.py:725
  39.4 7.5 %all-to-all-done = bf16[32,32,384]{2,1,0:T(8,128)(2,1)S(1)} async-done(((bf16[32,32,384]{2,1,0:T(8,128)(2,1)}), bf16[32,32,384]{2,1,0:T(8,128)(2,1)S(1)}, u32[]{:S(2)}, u32[]{:S(2)}) %all-to-all-start) | async-done | bytes 786464 | tf_op jit(solution)/shard_map/all_to_all | solution.py:725
  62.4 5.3 %collective-permute-start.9 = (bf16[1024,256]{1,0:T(8,128)(2,1)}, bf16[1024,256]{1,0:T(8,128)(2,1)}, u32[]{:S(2)}, u32[]{:S(2)}) collective-permute-start(bf16[1024,256]{1,0:T(8,128)(2,1)} %collective-permute-done.4), channel_id=1, source_target_pairs={{0,8},{8,16},{16,24},{1,9},{9,17},{17,25},{2,10},{10,18},{18,26},{... | collective-permute-start | bytes 1572872 | tf_op jit(solution)/shard_map/ppermute | solution.py:738
  87.1 5.0 %attn_fwd.1 = (f32[128,1024]{1,0:T(8,128)S(1)}, f32[2,1024]{1,0:T(2,128)S(1)}, bf16[1024,128]{1,0:T(8,128)(2,1)S(1)}) custom-call(s32[2]{0:T(128)S(1)} %slice.143.refs_0_, s32[1]{0:T(128)} %bitcast.2.refs_1_.refs_0_, bf16[1024,128]{1,0:T(8,128)(2,1)S(1)} %slice_multiply_fusion.refs_2_, bf16[3072,256]{1,0:T(8,128)(2,1)S(1)} %pad_maximum_fusion.4.refs_3_, ...), custom_call_target="tpu_custom_call" | custom-call | bytes 43008000 | tf_op jit(solution)/shard_map/attn_fwd/pallas_call | solution.py:150
  92.2 5.4 %collective-permute-start.13 = (bf16[32,1024]{1,0:T(8,128)(2,1)S(1)}, bf16[32,1024]{1,0:T(8,128)(2,1)S(1)}, u32[]{:S(2)}, u32[]{:S(2)}) collective-permute-start(bf16[32,1024]{1,0:T(8,128)(2,1)S(1)} %get-tuple-element.375), channel_id=1, source_target_pairs={{0,24},{8,0},{16,8},{24,16},{1,25},{9,1},{17,9},{25,17},{2,26},{10... | collective-permute-start | bytes 196616 | tf_op jit(solution)/shard_map/ppermute | solution.py:841
  113.1 6.5 %collective-permute-done.17 = bf16[128,1024]{1,0:T(8,128)(2,1)S(1)} collective-permute-done((bf16[128,1024]{1,0:T(8,128)(2,1)S(1)}, bf16[128,1024]{1,0:T(8,128)(2,1)S(1)}, u32[]{:S(2)}, u32[]{:S(2)}) %collective-permute-start.17) | collective-permute-done | bytes 262176 | tf_op jit(solution)/shard_map/ppermute | solution.py:733
  134.3 5.6 %collective-permute-done.21 = bf16[128,1024]{1,0:T(8,128)(2,1)S(1)} collective-permute-done((bf16[128,1024]{1,0:T(8,128)(2,1)S(1)}, bf16[128,1024]{1,0:T(8,128)(2,1)S(1)}, u32[]{:S(2)}, u32[]{:S(2)}) %collective-permute-start.21) | collective-permute-done | bytes 262176 | tf_op jit(solution)/shard_map/ppermute | solution.py:733
  160.6 6.8 %all-to-all-done.2.picked_ref = f32[8,32,128]{2,1,0:T(8,128)S(1)} async-done(((f32[8,32,128]{2,1,0:T(8,128)}), f32[8,32,128]{2,1,0:T(8,128)S(1)}, u32[]{:S(2)}, u32[]{:S(2)}) %all-to-all-start.2) | async-done | bytes 131104 | tf_op jit(solution)/shard_map/all_to_all | solution.py:725
  169.9 12.6 %all_to_all.44 = bf16[32,4,1024]{2,1,0:T(4,128)(2,1)S(1)} all-to-all(bf16[32,4,1024]{2,1,0:T(4,128)(2,1)S(1)} %reshape.410), channel_id=1, replica_groups=mesh['head'=4,'blk'=8] {'head','blk'}, dimensions={0} | all-to-all | bytes 524288 | tf_op jit(solution)/shard_map/all_to_all | solution.py:725
  185.3 20.8 %spread_weights.2 = (bf16[4,1024,2048]{2,1,0:T(8,128)(2,1)}, bf16[4,4,1,4,128,128]{5,4,3,2,1,0:T(8,128)(2,1)S(1)}, bf16[4,4,1,4,128,128]{5,4,3,2,1,0:T(8,128)(2,1)S(1)}) custom-call(s32[1]{0:T(128)} %bitcast.2.refs_1_.refs_0_, s32[4,8,1,1024]{3,2,1,0:T(1,128)S(1)} %get-tuple-element.365.refs_1_.refs_0_, ...), custom_call_target="tpu_custom_call" | custom-call | bytes 79644448 | tf_op jit(solution)/shard_map/spread_weights/pallas_call | solution.py:454
  206.0 20.9 %spread_weights.3 = (bf16[4,1024,2048]{2,1,0:T(8,128)(2,1)}, bf16[4,4,1,4,128,128]{5,4,3,2,1,0:T(8,128)(2,1)S(1)}, bf16[4,4,1,4,128,128]{5,4,3,2,1,0:T(8,128)(2,1)}) custom-call(s32[1]{0:T(128)} %bitcast.2.refs_1_.refs_0_, s32[4,8,1,1024]{3,2,1,0:T(1,128)S(1)} %get-tuple-element.365.refs_1_.refs_0_, ...), custom_call_target="tpu_custom_call", output_to_operand_aliasing={{0}: (6, {})} | custom-call | bytes 79644448 | tf_op jit(solution)/shard_map/spread_weights/pallas_call | solution.py:454
  236.4 10.9 %row_dots.4 = (f32[1,8,1,1024]{3,2,1,0:T(1,128)S(1)}, bf16[4,1024,1024]{2,1,0:T(8,128)(2,1)S(1)}) custom-call(s32[4,8,1,1024]{3,2,1,0:T(1,128)S(1)} %get-tuple-element.365.refs_1_.refs_0_, s32[4,8,1,1024]{3,2,1,0:T(1,128)S(1)} %get-tuple-element.364.refs_2_.refs_1_, s32[4,8,1,1024]{3,2,1,0:T(1,128)S(1)} %get-tuple-element.363.refs_3_.refs_2_, ...), custom_call_target="tpu_custom_call" | custom-call | bytes 39822224 | tf_op jit(solution)/shard_map/row_dots/pallas_call | solution.py:533
  251.3 10.9 %row_dots.5 = (f32[1,8,1,1024]{3,2,1,0:T(1,128)S(1)}, bf16[4,1024,1024]{2,1,0:T(8,128)(2,1)S(1)}) custom-call(s32[4,8,1,1024]{3,2,1,0:T(1,128)S(1)} %get-tuple-element.365.refs_1_.refs_0_, s32[4,8,1,1024]{3,2,1,0:T(1,128)S(1)} %get-tuple-element.364.refs_2_.refs_1_, ...), custom_call_target="tpu_custom_call", output_to_operand_aliasing={{1}: (5, {})} | custom-call | bytes 39822224 | tf_op jit(solution)/shard_map/row_dots/pallas_call | solution.py:533
  265.7 10.9 %row_dots.6 = (f32[1,8,1,1024]{3,2,1,0:T(1,128)S(1)}, bf16[4,1024,1024]{2,1,0:T(8,128)(2,1)S(1)}) custom-call(s32[4,8,1,1024]{3,2,1,0:T(1,128)S(1)} %get-tuple-element.365.refs_1_.refs_0_, s32[4,8,1,1024]{3,2,1,0:T(1,128)S(1)} %get-tuple-element.364.refs_2_.refs_1_, ...), custom_call_target="tpu_custom_call", output_to_operand_aliasing={{1}: (5, {})} | custom-call | bytes 39822224 | tf_op jit(solution)/shard_map/row_dots/pallas_call | solution.py:533
  280.6 11.1 %row_dots.7 = (f32[1,8,1,1024]{3,2,1,0:T(1,128)S(1)}, bf16[4,1024,1024]{2,1,0:T(8,128)(2,1)S(1)}) custom-call(s32[4,8,1,1024]{3,2,1,0:T(1,128)S(1)} %get-tuple-element.365.refs_1_.refs_0_, s32[4,8,1,1024]{3,2,1,0:T(1,128)S(1)} %get-tuple-element.364.refs_2_.refs_1_, ...), custom_call_target="tpu_custom_call", output_to_operand_aliasing={{1}: (5, {})} | custom-call | bytes 39822224 | tf_op jit(solution)/shard_map/row_dots/pallas_call | solution.py:533
  312.2 12.1 %value_grads.2.refs_0_ = f32[2048,1024]{1,0:T(8,128)} custom-call(bf16[4096,2048]{1,0:T(8,128)(2,1)} %bitcast.314, bf16[4096,1024]{1,0:T(8,128)(2,1)S(1)} %bitcast.290), custom_call_target="tpu_custom_call" | custom-call | bytes 52500000 | tf_op jit(solution)/shard_map/value_grads/pallas_call | solution.py:572
  328.2 5.1 %pick_grads.1 = f32[128,128]{1,0:T(8,128)S(1)} custom-call(s32[128,128]{1,0:T(8,128)S(1)} %copy-done.32, s32[128,128]{1,0:T(8,128)S(1)} %copy-done.30, f32[128,128]{1,0:T(8,128)S(1)} %copy-done.42, f32[256,128]{1,0:T(8,128)S(1)} %bitcast.306), custom_call_target="tpu_custom_call" | custom-call | bytes 17500000 | tf_op jit(solution)/shard_map/pick_grads/pallas_call | solution.py:381
  342.9 5.9 %unpick_scores.1 = (bf16[256,1024]{1,0:T(8,128)(2,1)S(1)}, bf16[1024,512]{1,0:T(8,128)(2,1)S(1)}) custom-call(f32[32,1024]{1,0:T(8,128)S(1)} %copy_bitcast_fusion.1.grad_ref, s32[32,1024]{1,0:T(8,128)S(1)} %copy-done.38, bf16[256,512]{1,0:T(8,128)(2,1)S(1)} %copy-done.22), custom_call_target="tpu_custom_call" | custom-call | bytes 19911112 | tf_op jit(solution)/shard_map/unpick_scores/pallas_call | solution.py:628
  386.5 4.9 collective-permute-done.46
  407.5 6.6 %attn_bwd.3 = (bf16[1024,128]{1,0:T(8,128)(2,1)S(1)}, bf16[1024,256]{1,0:T(8,128)(2,1)S(1)}, bf16[1024,256]{1,0:T(8,128)(2,1)S(1)}) custom-call(s32[2]{0:T(128)S(1)} %slice.143.refs_0_, s32[1]{0:T(128)} %bitcast.2.refs_1_.refs_0_, bf16[1024,128]{1,0:T(8,128)(2,1)S(1)} %copy-done.18, bf16[2048,256]{1,0:T(8,128)(2,1)S(1)} %slice.170.refs_3_, ...), custom_call_target="tpu_custom_call" | custom-call | bytes 35840000 | tf_op jit(solution)/shard_map/attn_bwd/pallas_call | solution.py:262
  436.7 12.0 %value_grads.3 = f32[2048,1024]{1,0:T(8,128)} custom-call(bf16[4096,2048]{1,0:T(8,128)(2,1)} %bitcast.315, bf16[4096,1024]{1,0:T(8,128)(2,1)S(1)} %bitcast.291, f32[2048,1024]{1,0:T(8,128)} %value_grads.2.refs_0_), custom_call_target="tpu_custom_call", output_to_operand_aliasing={{}: (2, {})} | custom-call | bytes 52500000 | tf_op jit(solution)/shard_map/value_grads/pallas_call | solution.py:572
  455.4 6.2 %collective-permute-start.59 = (bf16[4,128,1024]{2,1,0:T(8,128)(2,1)}, bf16[4,128,1024]{2,1,0:T(8,128)(2,1)}, u32[]{:S(2)}, u32[]{:S(2)}) collective-permute-start(bf16[4,128,1024]{2,1,0:T(8,128)(2,1)} %get-tuple-element.313), channel_id=1, source_target_pairs={{0,1},{1,0},{2,3},{3,2},{4,5},{5,4},{6,7},{7,6},{8,9},{9,8},{10,11... | collective-permute-start | bytes 3145736 | tf_op jit(solution)/shard_map/ppermute | solution.py:733
  479.1 6.8 %collective-permute-done.60 = bf16[128,1024]{1,0:T(8,128)(2,1)S(1)} collective-permute-done((bf16[128,1024]{1,0:T(8,128)(2,1)S(1)}, bf16[128,1024]{1,0:T(8,128)(2,1)S(1)}, u32[]{:S(2)}, u32[]{:S(2)}) %collective-permute-start.60) | collective-permute-done | bytes 262176 | tf_op jit(solution)/shard_map/ppermute | solution.py:733
  486.0 6.1 %collective-permute-done.61 = bf16[128,1024]{1,0:T(8,128)(2,1)S(1)} collective-permute-done((bf16[128,1024]{1,0:T(8,128)(2,1)S(1)}, bf16[128,1024]{1,0:T(8,128)(2,1)S(1)}, u32[]{:S(2)}, u32[]{:S(2)}) %collective-permute-start.61) | collective-permute-done | bytes 262176 | tf_op jit(solution)/shard_map/ppermute | solution.py:733
  (449 shorter events, 274.6 us)
Async XLA Ops:
  15.3 31.6 %all-to-all-start = ((bf16[32,32,384]{2,1,0:T(8,128)(2,1)}), bf16[32,32,384]{2,1,0:T(8,128)(2,1)S(1)}, u32[]{:S(2)}, u32[]{:S(2)}) async-start(bf16[32,32,384]{2,1,0:T(8,128)(2,1)} %bitcast.14), calls=%async_computation | async-start | bytes 1572864 | tf_op jit(solution)/shard_map/all_to_all | solution.py:725
  28.8 29.5 %collective-permute-start.6 = (bf16[128,1024]{1,0:T(8,128)(2,1)}, bf16[128,1024]{1,0:T(8,128)(2,1)}, u32[]{:S(2)}, u32[]{:S(2)}) collective-permute-start(bf16[128,1024]{1,0:T(8,128)(2,1)} %param.27), channel_id=1, source_target_pairs={{0,2},{1,3},{2,0},{3,1},{4,6},{5,7},{6,4},{7,5},{8,10},{9,11},{10,... | collective-permute-start | bytes 786440 | tf_op jit(solution)/shard_map/ppermute | solution.py:733
  30.0 28.2 %collective-permute-start.7 = (bf16[128,1024]{1,0:T(8,128)(2,1)}, bf16[128,1024]{1,0:T(8,128)(2,1)}, u32[]{:S(2)}, u32[]{:S(2)}) collective-permute-start(bf16[128,1024]{1,0:T(8,128)(2,1)} %param.27), channel_id=1, source_target_pairs={{0,4},{1,5},{2,6},{3,7},{4,0},{5,1},{6,2},{7,3},{8,12},{9,13},{10,... | collective-permute-start | bytes 786440 | tf_op jit(solution)/shard_map/ppermute | solution.py:733
  31.5 26.8 %collective-permute-start.8 = (bf16[128,1024]{1,0:T(8,128)(2,1)}, bf16[128,1024]{1,0:T(8,128)(2,1)}, u32[]{:S(2)}, u32[]{:S(2)}) collective-permute-start(bf16[128,1024]{1,0:T(8,128)(2,1)} %param.27), channel_id=1, source_target_pairs={{0,6},{1,7},{2,4},{3,5},{4,2},{5,3},{6,0},{7,1},{8,14},{9,15},{10,... | collective-permute-start | bytes 786440 | tf_op jit(solution)/shard_map/ppermute | solution.py:733
  32.3 26.0 %collective-permute-start.5 = (bf16[3,32,1024]{2,1,0:T(8,128)(2,1)}, bf16[3,32,1024]{2,1,0:T(8,128)(2,1)}, u32[]{:S(2)}, u32[]{:S(2)}) collective-permute-start(bf16[3,32,1024]{2,1,0:T(8,128)(2,1)} %pad_maximum_fusion.13), channel_id=1, source_target_pairs={{0,0},{4,1},{8,2},{12,3},{16,4},{20,5},{24,6},{28,7},{1,8},{5,9},{... | collective-permute-start | bytes 589832 | tf_op jit(solution)/shard_map/ppermute | solution.py:918
  53.6 22.7 %all-to-all-start.1 = ((bf16[8,32,768]{2,1,0:T(8,128)(2,1)}), bf16[8,32,768]{2,1,0:T(8,128)(2,1)S(1)}, u32[]{:S(2)}, u32[]{:S(2)}) async-start(bf16[8,32,768]{2,1,0:T(8,128)(2,1)} %copy.167), calls=%async_computation.1 | async-start | bytes 786432 | tf_op jit(solution)/shard_map/all_to_all | solution.py:725
  57.4 173.6 %all-gather.2.cloned.1.call-start = ((), (), s32[]{:S(2)}) async-start(), calls=%async_computation.9 | async-start | bytes 8650752 | tf_op jit(solution)/shard_map/all_gather | solution.py:729
  69.9 22.3 %collective-permute-start.10 = (bf16[4,128,1024]{2,1,0:T(8,128)(2,1)}, bf16[4,128,1024]{2,1,0:T(8,128)(2,1)}, u32[]{:S(2)}, u32[]{:S(2)}) collective-permute-start(bf16[4,128,1024]{2,1,0:T(8,128)(2,1)} %get-tuple-element.359), channel_id=1, source_target_pairs={{0,1},{1,0},{2,3},{3,2},{4,5},{5,4},{6,7},{7,6},{8,9},{9,8},{10,11... | collective-permute-start | bytes 3145736 | tf_op jit(solution)/shard_map/ppermute | solution.py:733
  80.7 23.1 %collective-permute-start.14 = (bf16[256,640]{1,0:T(8,128)(2,1)S(1)}, bf16[256,640]{1,0:T(8,128)(2,1)S(1)}, u32[]{:S(2)}, u32[]{:S(2)}) collective-permute-start(bf16[256,640]{1,0:T(8,128)(2,1)S(1)} %bitcast.331), channel_id=1, source_target_pairs={{0,8},{8,16},{16,24},{24,0},{1,9},{9,17},{17,25},{25,1},{2,10},{10... | collective-permute-start | bytes 983048 | tf_op jit(solution)/shard_map/ppermute | solution.py:841
  231.0 31.2 %collective-permute-start.30 = (bf16[2,4,256,128]{3,2,1,0:T(8,128)(2,1)}, bf16[2,4,256,128]{3,2,1,0:T(8,128)(2,1)S(1)}, u32[]{:S(2)}, u32[]{:S(2)}) collective-permute-start(bf16[2,4,256,128]{3,2,1,0:T(8,128)(2,1)} %copy-done.44), channel_id=1, source_target_pairs={{0,2},{1,3},{2,0},{3,1},{4,6},{5,7},{6,4},{7,5},{8,10},{9,11},{10,... | collective-permute-start | bytes 1572872 | tf_op jit(solution)/shard_map/ppermute | solution.py:733
  233.0 29.2 %collective-permute-start.31 = (bf16[2,4,256,128]{3,2,1,0:T(8,128)(2,1)}, bf16[2,4,256,128]{3,2,1,0:T(8,128)(2,1)S(1)}, u32[]{:S(2)}, u32[]{:S(2)}) collective-permute-start(bf16[2,4,256,128]{3,2,1,0:T(8,128)(2,1)} %copy-done.43), channel_id=1, source_target_pairs={{0,4},{1,5},{2,6},{3,7},{4,0},{5,1},{6,2},{7,3},{8,12},{9,13},{10,... | collective-permute-start | bytes 1572872 | tf_op jit(solution)/shard_map/ppermute | solution.py:733
  249.9 26.7 %collective-permute-start.32 = (bf16[2,4,256,128]{3,2,1,0:T(8,128)(2,1)S(1)}, bf16[2,4,256,128]{3,2,1,0:T(8,128)(2,1)S(1)}, u32[]{:S(2)}, u32[]{:S(2)}) collective-permute-start(bf16[2,4,256,128]{3,2,1,0:T(8,128)(2,1)S(1)} %get-tuple-element.238), channel_id=1, source_target_pairs={{0,2},{1,3},{2,0},{3,1},{4,6},{5,7},{6,4},{7,5},{8,10},{9,11},{10,... | collective-permute-start | bytes 1572872 | tf_op jit(solution)/shard_map/ppermute | solution.py:733
  251.3 25.3 %collective-permute-start.33 = (bf16[2,4,256,128]{3,2,1,0:T(8,128)(2,1)S(1)}, bf16[2,4,256,128]{3,2,1,0:T(8,128)(2,1)S(1)}, u32[]{:S(2)}, u32[]{:S(2)}) collective-permute-start(bf16[2,4,256,128]{3,2,1,0:T(8,128)(2,1)S(1)} %get-tuple-element.239), channel_id=1, source_target_pairs={{0,4},{1,5},{2,6},{3,7},{4,0},{5,1},{6,2},{7,3},{8,12},{9,13},{10,... | collective-permute-start | bytes 1572872 | tf_op jit(solution)/shard_map/ppermute | solution.py:733
  299.5 37.9 %collective-permute-start.38 = (bf16[1024,128]{1,0:T(8,128)(2,1)}, bf16[1024,128]{1,0:T(8,128)(2,1)S(1)}, u32[]{:S(2)}, u32[]{:S(2)}) collective-permute-start(bf16[1024,128]{1,0:T(8,128)(2,1)} %get-tuple-element.350), channel_id=1, source_target_pairs={{0,8},{8,16},{16,24},{24,0},{1,9},{9,17},{17,25},{25,1},{2,10},{10... | collective-permute-start | bytes 786440 | tf_op jit(solution)/shard_map/ppermute | solution.py:832
  301.1 36.4 %collective-permute-start.39 = (bf16[1024,128]{1,0:T(8,128)(2,1)}, bf16[1024,128]{1,0:T(8,128)(2,1)S(1)}, u32[]{:S(2)}, u32[]{:S(2)}) collective-permute-start(bf16[1024,128]{1,0:T(8,128)(2,1)} %get-tuple-element.351), channel_id=1, source_target_pairs={{0,16},{8,24},{16,0},{24,8},{1,17},{9,25},{17,1},{25,9},{2,18},{10... | collective-permute-start | bytes 786440 | tf_op jit(solution)/shard_map/ppermute | solution.py:832
  302.3 35.1 %collective-permute-start.40 = (bf16[1024,128]{1,0:T(8,128)(2,1)}, bf16[1024,128]{1,0:T(8,128)(2,1)}, u32[]{:S(2)}, u32[]{:S(2)}) collective-permute-start(bf16[1024,128]{1,0:T(8,128)(2,1)} %get-tuple-element.352), channel_id=1, source_target_pairs={{0,24},{8,0},{16,8},{24,16},{1,25},{9,1},{17,9},{25,17},{2,26},{10... | collective-permute-start | bytes 786440 | tf_op jit(solution)/shard_map/ppermute | solution.py:832
  304.7 23.5 %all-to-all-start.4 = ((f32[32,1,1024]{2,1,0:T(1,128)}), f32[32,1,1024]{2,1,0:T(1,128)S(1)}, u32[]{:S(2)}, u32[]{:S(2)}) async-start(f32[32,1,1024]{2,1,0:T(1,128)} %bitcast.92), calls=%async_computation.4 | async-start | bytes 262144 | tf_op jit(solution)/shard_map/all_to_all | solution.py:725
  337.4 77.1 %reduce-scatter.2.cloned.1.call-start = ((), (), s32[]{:S(2)}) async-start(), calls=%async_computation.10 | async-start | bytes 2293760 | tf_op jit(solution)/shard_map/reduce_scatter | solution.py:1160
  406.0 42.7 %collective-permute-start.56 = (bf16[128,1024]{1,0:T(8,128)(2,1)}, bf16[128,1024]{1,0:T(8,128)(2,1)}, u32[]{:S(2)}, u32[]{:S(2)}) collective-permute-start(bf16[128,1024]{1,0:T(8,128)(2,1)} %get-tuple-element.344), channel_id=1, source_target_pairs={{0,6},{1,7},{2,4},{3,5},{4,2},{5,3},{6,0},{7,1},{8,14},{9,15},{10,... | collective-permute-start | bytes 786440 | tf_op jit(solution)/shard_map/ppermute | solution.py:733
  414.4 34.3 %collective-permute-start.57 = (bf16[128,1024]{1,0:T(8,128)(2,1)}, bf16[128,1024]{1,0:T(8,128)(2,1)}, u32[]{:S(2)}, u32[]{:S(2)}) collective-permute-start(bf16[128,1024]{1,0:T(8,128)(2,1)} %get-tuple-element.343), channel_id=1, source_target_pairs={{0,2},{1,3},{2,0},{3,1},{4,6},{5,7},{6,4},{7,5},{8,10},{9,11},{10,... | collective-permute-start | bytes 786440 | tf_op jit(solution)/shard_map/ppermute | solution.py:733
  415.9 32.9 %collective-permute-start.58 = (bf16[128,1024]{1,0:T(8,128)(2,1)}, bf16[128,1024]{1,0:T(8,128)(2,1)}, u32[]{:S(2)}, u32[]{:S(2)}) collective-permute-start(bf16[128,1024]{1,0:T(8,128)(2,1)} %get-tuple-element.342), channel_id=1, source_target_pairs={{0,4},{1,5},{2,6},{3,7},{4,0},{5,1},{6,2},{7,3},{8,12},{9,13},{10,... | collective-permute-start | bytes 786440 | tf_op jit(solution)/shard_map/ppermute | solution.py:733
  425.2 23.5 %collective-permute-start.54 = (bf16[1024,256]{1,0:T(8,128)(2,1)}, bf16[1024,256]{1,0:T(8,128)(2,1)S(1)}, u32[]{:S(2)}, u32[]{:S(2)}) collective-permute-start(bf16[1024,256]{1,0:T(8,128)(2,1)} %add_convert_fusion.1), channel_id=1, source_target_pairs={{8,0},{16,8},{24,16},{9,1},{17,9},{25,17},{10,2},{18,10},{26,18},{... | collective-permute-start | bytes 1572872 | tf_op jit(solution)/shard_map/ppermute | solution.py:738
  427.4 21.3 %all-to-all-start.6 = ((bf16[8,32,640]{2,1,0:T(8,128)(2,1)}), bf16[8,32,640]{2,1,0:T(8,128)(2,1)S(1)}, u32[]{:S(2)}, u32[]{:S(2)}) async-start(bf16[8,32,640]{2,1,0:T(8,128)(2,1)} %bitcast.124), calls=%async_computation.7 | async-start | bytes 655360 | tf_op jit(solution)/shard_map/all_to_all | solution.py:725
  464.3 29.6 %all-to-all-start.7 = ((bf16[32,32,384]{2,1,0:T(8,128)(2,1)}), bf16[32,32,384]{2,1,0:T(8,128)(2,1)S(1)}, u32[]{:S(2)}, u32[]{:S(2)}) async-start(bf16[32,32,384]{2,1,0:T(8,128)(2,1)} %bitcast.347), calls=%async_computation.8 | async-start | bytes 1572864 | tf_op jit(solution)/shard_map/all_to_all | solution.py:725
  (125 other events, 1510.8 us)
Sparse Core Ops, SparseCore 0:
  153.5 77.0 all-gather.1
  373.8 40.6 reduce-scatter.1
